TPU v7x, 256 devices: a whole 4x4x8 slice. The times are simulated.
256 devices in a mesh: dp: 8 (over y, core), seq: 32 (over z, x).
Axes of the slice: x: 4, y: 4, z: 8, core: 2. Of those that a mesh axis runs over, the one named last changes fastest.
Arguments:
- queries: bfloat16 [8, 4096, 4096], P('dp', 'seq'), may hold values from -120 to 120, as said below
- keys: bfloat16 [8, 4096, 512], P('dp', 'seq'), may hold values from -4 to 4
- values: bfloat16 [8, 4096, 512], P('dp', 'seq'), may hold values from -6 to 6
- cotangent: bfloat16 [8, 4096, 4096], P('dp', 'seq'), may hold values from -6 to 6
- lengths: int32 [8, 16], P('dp'), may hold values from 1 to 1024, 4096 in all within a row
- loss_mask: int32 [8, 4096], P('dp', 'seq'), may hold values from 0 to 1, as said below
Outputs:
- attn_out: bfloat16 [8, 4096, 4096], P('dp', 'seq')
- grad_q: bfloat16 [8, 4096, 4096], P('dp', 'seq')
- grad_k: bfloat16 [8, 4096, 512], P('dp', 'seq')
- grad_v: bfloat16 [8, 4096, 512], P('dp', 'seq')
- row_loss: float32 [8], P('dp')
Inputs may be any that keep to these rules, and one draw needn't show every extreme that they name: `queries`: in the shown draw entries lie within -4 to 4. Each row's 16 lengths sum to 4096; the longest is exactly 1024. `loss_mask`: entries are 0 or 1; position 0 of every row is 1.
All inputs are finite; a program needn't handle non-finite values.
Results may differ from a plain program's by a relative error of at most 0.015.
The roundings to bfloat16 on the way count: a program that leaves them out, or rounds other values in their place, can miss the bound.
Values may be sent and summed in bfloat16 or wider, within the bound.
No kernel may reach another device: no remote copies, remote signals or barrier semaphores. Data moves between devices by JAX's collectives and lax.ppermute only.
A program may use at most 64 MiB of HBM per device.

v0:
```python
import jax
import jax.numpy as jnp
from jax import lax
from jax.sharding import PartitionSpec as P

HD = 128


masked_value = -1e30


def doc_tables(lengths_row, seq_len):
    doc_ends = jnp.cumsum(lengths_row)
    doc_starts = doc_ends - lengths_row
    positions = jnp.arange(seq_len, dtype=jnp.int32)
    started = positions[:, None] >= doc_starts[None, :]
    within = started & (positions[:, None] < doc_ends[None, :])
    doc_ids = jnp.sum(started.astype(jnp.int32), axis=1)
    doc_first = jnp.sum(jnp.where(within, doc_starts[None, :], 0), axis=1)
    return (doc_ids, doc_first)


def tile_scores(
    query_block,
    key_block,
    query_docs,
    key_docs,
    query_start,
    key_start,
    query_rows,
    key_rows,
    score_scale,
):
    scores = (
        lax.dot_general(
            query_block, key_block, (((1,), (1,)), ((), ())), preferred_element_type=jnp.float32
        )
        * score_scale
    )
    query_pos = query_start + jnp.arange(query_rows, dtype=jnp.int32)
    key_pos = key_start + jnp.arange(key_rows, dtype=jnp.int32)
    allowed = (query_docs[:, None] == key_docs[None, :]) & (key_pos[None, :] <= query_pos[:, None])
    return (jnp.where(allowed, scores, masked_value), allowed)


def attend_forward(query_head, key_head, value_head, doc_ids, block_rows):
    seq_len, head_size = query_head.shape
    score_scale = head_size ** (-0.5)
    block_count = seq_len // block_rows
    window = min(seq_len, seq_len // 4 + block_rows)

    def query_step(qblock, loop_state):
        output, log_total = loop_state
        query_start = qblock * block_rows
        query_block = lax.dynamic_slice_in_dim(query_head, query_start, block_rows, 0)
        query_docs = lax.dynamic_slice_in_dim(doc_ids, query_start, block_rows, 0)
        key_start = jnp.clip(query_start + block_rows - window, 0, seq_len - window)
        key_block = lax.dynamic_slice_in_dim(key_head, key_start, window, 0)
        value_block = lax.dynamic_slice_in_dim(value_head, key_start, window, 0)
        key_docs = lax.dynamic_slice_in_dim(doc_ids, key_start, window, 0)
        scores, allowed = tile_scores(
            query_block,
            key_block,
            query_docs,
            key_docs,
            query_start,
            key_start,
            block_rows,
            window,
            score_scale,
        )
        row_top = jnp.max(scores, axis=1)
        block_total = row_top + jnp.log(
            jnp.sum(jnp.where(allowed, jnp.exp(scores - row_top[:, None]), 0.0), axis=1)
        )
        probs = jnp.where(allowed, jnp.exp(scores - block_total[:, None]), 0.0).astype(jnp.bfloat16)
        value_sum = jnp.dot(probs, value_block, preferred_element_type=jnp.float32)
        output = lax.dynamic_update_slice_in_dim(
            output, value_sum.astype(jnp.bfloat16), query_start, 0
        )
        log_total = lax.dynamic_update_slice_in_dim(log_total, block_total, query_start, 0)
        return (output, log_total)

    start = (jnp.zeros((seq_len, head_size), jnp.bfloat16), jnp.zeros((seq_len,), jnp.float32))
    return lax.fori_loop(0, block_count, query_step, start)


def attend_backward(
    query_head,
    key_head,
    value_head,
    upstream_head,
    output_head,
    log_total,
    doc_ids,
    doc_first,
    block_rows,
):
    seq_len, head_size = query_head.shape
    score_scale = head_size ** (-0.5)
    block_count = seq_len // block_rows
    delta = jnp.sum(upstream_head.astype(jnp.float32) * output_head.astype(jnp.float32), axis=1)

    def query_step(qblock, loop_state):
        query_grad, key_grad, value_grad = loop_state
        query_start = qblock * block_rows
        query_block = lax.dynamic_slice_in_dim(query_head, query_start, block_rows, 0)
        upstream_block = lax.dynamic_slice_in_dim(upstream_head, query_start, block_rows, 0)
        query_docs = lax.dynamic_slice_in_dim(doc_ids, query_start, block_rows, 0)
        block_total = lax.dynamic_slice_in_dim(log_total, query_start, block_rows, 0)
        block_delta = lax.dynamic_slice_in_dim(delta, query_start, block_rows, 0)
        kblock_first = (
            lax.dynamic_index_in_dim(doc_first, query_start, 0, keepdims=False) // block_rows
        )

        def grad_step(kblock, inner):
            block_query_grad, key_all, value_all = inner
            key_start = kblock * block_rows
            key_block = lax.dynamic_slice_in_dim(key_head, key_start, block_rows, 0)
            value_block = lax.dynamic_slice_in_dim(value_head, key_start, block_rows, 0)
            key_docs = lax.dynamic_slice_in_dim(doc_ids, key_start, block_rows, 0)
            scores, allowed = tile_scores(
                query_block,
                key_block,
                query_docs,
                key_docs,
                query_start,
                key_start,
                block_rows,
                block_rows,
                score_scale,
            )
            weights = jnp.where(allowed, jnp.exp(scores - block_total[:, None]), 0.0)
            probs = weights.astype(jnp.bfloat16)
            prob_grad = lax.dot_general(
                upstream_block,
                value_block,
                (((1,), (1,)), ((), ())),
                preferred_element_type=jnp.float32,
            )
            score_grad = (weights * (prob_grad - block_delta[:, None])).astype(jnp.bfloat16)
            block_query_grad = block_query_grad + jnp.dot(
                score_grad, key_block, preferred_element_type=jnp.float32
            )
            key_term = lax.dot_general(
                score_grad,
                query_block,
                (((0,), (0,)), ((), ())),
                preferred_element_type=jnp.float32,
            )
            value_term = lax.dot_general(
                probs, upstream_block, (((0,), (0,)), ((), ())), preferred_element_type=jnp.float32
            )
            key_old = lax.dynamic_slice_in_dim(key_all, key_start, block_rows, 0)
            value_old = lax.dynamic_slice_in_dim(value_all, key_start, block_rows, 0)
            key_all = lax.dynamic_update_slice_in_dim(key_all, key_old + key_term, key_start, 0)
            value_all = lax.dynamic_update_slice_in_dim(
                value_all, value_old + value_term, key_start, 0
            )
            return (block_query_grad, key_all, value_all)

        inner = (jnp.zeros((block_rows, head_size), jnp.float32), key_grad, value_grad)
        block_query_grad, key_grad, value_grad = lax.fori_loop(
            kblock_first, qblock + 1, grad_step, inner
        )
        query_grad = lax.dynamic_update_slice_in_dim(query_grad, block_query_grad, query_start, 0)
        return (query_grad, key_grad, value_grad)

    empty = jnp.zeros((seq_len, head_size), jnp.float32)
    return lax.fori_loop(0, block_count, query_step, (empty, empty, empty))


def per_device(queries, keys, values, cotangent, lengths, loss_mask):
    seq_count = lax.axis_size("seq")
    tok_rows = queries.shape[1]
    head_size = HD
    query_heads = queries.shape[2] // head_size
    kv_heads = keys.shape[2] // head_size
    group = query_heads // kv_heads
    seq_len = tok_rows * seq_count
    block_rows = min(512, seq_len)
    doc_ids, doc_first = doc_tables(lengths[0], seq_len)
    query_local = queries[0].reshape(tok_rows, query_heads, head_size)
    cot_local = cotangent[0].reshape(tok_rows, query_heads, head_size)
    mask_row = loss_mask[0]
    local_count = jnp.sum(mask_row).astype(jnp.float32)
    token_total = lax.psum(local_count, ("dp", "seq"))
    query_split = lax.all_to_all(query_local, "seq", split_axis=1, concat_axis=0, tiled=True)
    query_head = query_split[:, 0, :]
    key_local = keys[0].reshape(tok_rows, kv_heads, head_size)
    value_local = values[0].reshape(tok_rows, kv_heads, head_size)
    key_copies = jnp.repeat(key_local, group, axis=1)
    value_copies = jnp.repeat(value_local, group, axis=1)
    key_split, value_split = (
        lax.all_to_all(key_copies, "seq", split_axis=1, concat_axis=0, tiled=True),
        lax.all_to_all(value_copies, "seq", split_axis=1, concat_axis=0, tiled=True),
    )
    key_head = key_split[:, 0, :]
    value_head = value_split[:, 0, :]
    output_head, log_total = attend_forward(query_head, key_head, value_head, doc_ids, block_rows)
    output_local = lax.all_to_all(
        output_head[:, None, :], "seq", split_axis=0, concat_axis=1, tiled=True
    )
    token_terms = jnp.sum(
        output_local.astype(jnp.float32) * cot_local.astype(jnp.float32), axis=(1, 2)
    )
    loss_part = jnp.sum(mask_row.astype(jnp.float32) * token_terms)
    dp_count = lax.axis_size("dp")
    row_sum = lax.psum(loss_part, "seq")
    grad_scale = jnp.float32(dp_count * seq_len) / token_total
    row_loss = (grad_scale * row_sum / seq_len).reshape(1)
    upstream_local = jnp.where(mask_row[:, None, None] > 0, cot_local, 0)
    upstream_split = lax.all_to_all(upstream_local, "seq", split_axis=1, concat_axis=0, tiled=True)
    upstream_head = upstream_split[:, 0, :]
    query_grad, key_grad, value_grad = attend_backward(
        query_head,
        key_head,
        value_head,
        upstream_head,
        output_head,
        log_total,
        doc_ids,
        doc_first,
        block_rows,
    )
    key_factor = grad_scale * head_size ** (-0.5)
    query_grad_head = (key_factor * query_grad).astype(jnp.bfloat16)
    key_piece = (key_factor * key_grad).astype(jnp.bfloat16)
    value_piece = (grad_scale * value_grad).astype(jnp.bfloat16)
    query_back, key_back, value_back = (
        lax.all_to_all(query_grad_head[:, None, :], "seq", split_axis=0, concat_axis=1, tiled=True),
        lax.all_to_all(key_piece[:, None, :], "seq", split_axis=0, concat_axis=1, tiled=True),
        lax.all_to_all(value_piece[:, None, :], "seq", split_axis=0, concat_axis=1, tiled=True),
    )
    grad_key = jnp.sum(
        key_back.astype(jnp.float32).reshape(tok_rows, kv_heads, group, head_size), axis=2
    )
    grad_value = jnp.sum(
        value_back.astype(jnp.float32).reshape(tok_rows, kv_heads, group, head_size), axis=2
    )
    grad_key = grad_key.astype(jnp.bfloat16).reshape(1, tok_rows, kv_heads * head_size)
    grad_value = grad_value.astype(jnp.bfloat16).reshape(1, tok_rows, kv_heads * head_size)
    attn_out = output_local.reshape(1, tok_rows, query_heads * head_size)
    grad_q = query_back.reshape(1, tok_rows, query_heads * head_size)
    return (attn_out, grad_q, grad_key, grad_value, row_loss)


def solution(mesh):
    return jax.shard_map(
        per_device,
        mesh=mesh,
        in_specs=(
            P("dp", "seq", None),
            P("dp", "seq", None),
            P("dp", "seq", None),
            P("dp", "seq", None),
            P("dp", None),
            P("dp", "seq"),
        ),
        out_specs=(
            P("dp", "seq", None),
            P("dp", "seq", None),
            P("dp", "seq", None),
            P("dp", "seq", None),
            P("dp"),
        ),
        check_vma=False,
    )
```

profile of v0, /device:TPU:128, one launch (start us, length us, event | category | flops | bytes accessed | tf_op | source)
XLA Modules:
  0.0 554.7 jit_solution(14328199125128773742)
XLA Ops:
  2.9 9.8 %all-to-all-start.2 = ((bf16[128,32,128]{2,0,1:T(8,128)(2,1)}), bf16[128,32,128]{2,0,1:T(8,128)(2,1)S(1)}, u32[]{:S(2)}, u32[]{:S(2)}) async-start(bf16[128,32,128]{2,0,1:T(8,128)(2,1)} %bitcast.12), calls=%async_computation.2 | async-start | bytes 2097152 | tf_op jit(solution)/shard_map/all_to_all | solution.py:196
  12.8 25.1 %all-to-all-done.2 = bf16[128,32,128]{2,0,1:T(8,128)(2,1)S(1)} async-done(((bf16[128,32,128]{2,0,1:T(8,128)(2,1)}), bf16[128,32,128]{2,0,1:T(8,128)(2,1)S(1)}, u32[]{:S(2)}, u32[]{:S(2)}) %all-to-all-start.2) | async-done | bytes 1048608 | tf_op jit(solution)/shard_map/all_to_all | solution.py:196
  39.1 8.5 %all-to-all-start.1 = ((bf16[128,32,128]{2,0,1:T(8,128)(2,1)}), bf16[128,32,128]{2,0,1:T(8,128)(2,1)S(1)}, u32[]{:S(2)}, u32[]{:S(2)}) async-start(bf16[128,32,128]{2,0,1:T(8,128)(2,1)} %bitcast.8), calls=%async_computation.1 | async-start | bytes 2097152 | tf_op jit(solution)/shard_map/all_to_all | solution.py:195
  49.2 22.4 %all-to-all-done.1 = bf16[128,32,128]{2,0,1:T(8,128)(2,1)S(1)} async-done(((bf16[128,32,128]{2,0,1:T(8,128)(2,1)}), bf16[128,32,128]{2,0,1:T(8,128)(2,1)S(1)}, u32[]{:S(2)}, u32[]{:S(2)}) %all-to-all-start.1) | async-done | bytes 1048608 | tf_op jit(solution)/shard_map/all_to_all | solution.py:195
  71.6 8.5 %all-to-all-start = ((bf16[128,32,128]{2,0,1:T(8,128)(2,1)}), bf16[128,32,128]{2,0,1:T(8,128)(2,1)}, u32[]{:S(2)}, u32[]{:S(2)}) async-start(bf16[128,32,128]{2,0,1:T(8,128)(2,1)} %copy.68), calls=%async_computation | async-start | bytes 2097152 | tf_op jit(solution)/shard_map/all_to_all | solution.py:188
  81.5 75.4 %psum.14 = f32[]{:T(128)} all-reduce(f32[]{:T(128)S(6)} %convert_element_type.131), channel_id=1, replica_groups=mesh['dp'=8,'seq'=32] {'dp','seq'}, use_global_device_ids=true, to_apply=%region_7.8 | all-reduce | flops 1 | bytes 8 | tf_op jit(solution)/shard_map/psum | solution.py:187
  157.1 1.6 copy.73
  159.8 2.3 copy.74
  163.0 9.7 %all-to-all-start.4 = ((bf16[128,32,128]{2,0,1:T(8,128)(2,1)}), bf16[128,32,128]{2,0,1:T(8,128)(2,1)}, u32[]{:S(2)}, u32[]{:S(2)}) async-start(bf16[128,32,128]{2,0,1:T(8,128)(2,1)} %copy.74), calls=%async_computation.4 | async-start | bytes 2097152 | tf_op jit(solution)/shard_map/all_to_all | solution.py:213
  172.9 33.9 %while.77 = (s32[]{:T(128)}, bf16[4096,128]{1,0:T(8,128)(2,1)S(1)}, f32[4096]{0:T(1024)S(1)}, s32[4096]{0:T(1024)S(1)}, bf16[4096,128]{1,0:T(8,128)(2,1)}, /*ind...) while((s32[]{:T(128)}, bf16[4096,128]{1,0:T(8,128)(2,1)S(1)}, ...), condition=%wide.region_5.6_spmd, body=%wide.region_2.5_spmd.sunk | while | flops 416876032 | bytes 10584307 | solution.py:85
  173.1 1.9 fusion.61
  177.3 1.9 fusion.61
  181.6 1.9 fusion.61
  185.8 1.9 fusion.61
  190.0 1.9 fusion.61
  194.3 1.9 fusion.61
  198.5 1.9 fusion.61
  202.8 1.9 fusion.61
  207.4 2.1 reduce.5
  209.5 2.1 reshape.134
  211.6 9.9 %all-to-all-start.3 = ((bf16[32,2,8192]{2,1,0:T(2,128)(2,1)}), bf16[32,2,8192]{2,1,0:T(2,128)(2,1)}, u32[]{:S(2)}, u32[]{:S(2)}) async-start(bf16[32,2,8192]{2,1,0:T(2,128)(2,1)} %reshape.134), calls=%async_computation.3 | async-start | bytes 2097152 | tf_op jit(solution)/shard_map/all_to_all | solution.py:201
  221.5 1.8 multiply_reduce_fusion
  224.9 1.5 broadcast_in_dim.118
  226.4 140.9 %while.79 = (s32[]{:T(128)}, f32[4096,128]{1,0:T(8,128)}, f32[4096,128]{1,0:T(8,128)}, f32[4096,128]{1,0:T(8,128)S(1)}, s32[4096]{0:T(1024)S(1)}, /*index=5*/bf1...) while((s32[]{:T(128)}, f32[4096,128]{1,0:T(8,128)}, ...), condition=%wide.region_13.14_spmd, body=%wide.region_10.13_spmd.sunk | while | flops 338625568 | bytes 8553280 | solution.py:170
  230.8 6.3 %while.80 = (s32[]{:T(128)}, f32[512,128]{1,0:T(8,128)S(1)}, f32[4096,128]{1,0:T(8,128)}, f32[4096,128]{1,0:T(8,128)S(1)}, s32[]{:T(128)}, /*index=5*/s32[512]{0...) while((s32[]{:T(128)}, f32[512,128]{1,0:T(8,128)S(1)}, ...), condition=%wide.region_12.12_spmd, body=%wide.region_11.11_spmd.sunk | while | flops 338625536 | bytes 7229683 | solution.py:163
  235.1 2.0 fusion.76
  242.2 12.5 %while.80 = (s32[]{:T(128)}, f32[512,128]{1,0:T(8,128)S(1)}, f32[4096,128]{1,0:T(8,128)}, f32[4096,128]{1,0:T(8,128)S(1)}, s32[]{:T(128)}, /*index=5*/s32[512]{0...) while((s32[]{:T(128)}, f32[512,128]{1,0:T(8,128)S(1)}, ...), condition=%wide.region_12.12_spmd, body=%wide.region_11.11_spmd.sunk | while | flops 338625536 | bytes 7229683 | solution.py:163
  246.5 2.0 fusion.76
  252.7 2.0 fusion.76
  259.8 18.7 %while.80 = (s32[]{:T(128)}, f32[512,128]{1,0:T(8,128)S(1)}, f32[4096,128]{1,0:T(8,128)}, f32[4096,128]{1,0:T(8,128)S(1)}, s32[]{:T(128)}, /*index=5*/s32[512]{0...) while((s32[]{:T(128)}, f32[512,128]{1,0:T(8,128)S(1)}, ...), condition=%wide.region_12.12_spmd, body=%wide.region_11.11_spmd.sunk | while | flops 338625536 | bytes 7229683 | solution.py:163
  264.1 2.0 fusion.76
  270.3 2.0 fusion.76
  276.6 1.9 fusion.76
  283.7 12.4 %while.80 = (s32[]{:T(128)}, f32[512,128]{1,0:T(8,128)S(1)}, f32[4096,128]{1,0:T(8,128)}, f32[4096,128]{1,0:T(8,128)S(1)}, s32[]{:T(128)}, /*index=5*/s32[512]{0...) while((s32[]{:T(128)}, f32[512,128]{1,0:T(8,128)S(1)}, ...), condition=%wide.region_12.12_spmd, body=%wide.region_11.11_spmd.sunk | while | flops 338625536 | bytes 7229683 | solution.py:163
  287.9 1.9 fusion.76
  294.1 2.0 fusion.76
  301.3 12.5 %while.80 = (s32[]{:T(128)}, f32[512,128]{1,0:T(8,128)S(1)}, f32[4096,128]{1,0:T(8,128)}, f32[4096,128]{1,0:T(8,128)S(1)}, s32[]{:T(128)}, /*index=5*/s32[512]{0...) while((s32[]{:T(128)}, f32[512,128]{1,0:T(8,128)S(1)}, ...), condition=%wide.region_12.12_spmd, body=%wide.region_11.11_spmd.sunk | while | flops 338625536 | bytes 7229683 | solution.py:163
  305.5 2.0 fusion.76
  311.8 2.0 fusion.76
  318.9 12.5 %while.80 = (s32[]{:T(128)}, f32[512,128]{1,0:T(8,128)S(1)}, f32[4096,128]{1,0:T(8,128)}, f32[4096,128]{1,0:T(8,128)S(1)}, s32[]{:T(128)}, /*index=5*/s32[512]{0...) while((s32[]{:T(128)}, f32[512,128]{1,0:T(8,128)S(1)}, ...), condition=%wide.region_12.12_spmd, body=%wide.region_11.11_spmd.sunk | while | flops 338625536 | bytes 7229683 | solution.py:163
  323.2 2.0 fusion.76
  329.4 2.0 fusion.76
  336.5 12.4 %while.80 = (s32[]{:T(128)}, f32[512,128]{1,0:T(8,128)S(1)}, f32[4096,128]{1,0:T(8,128)}, f32[4096,128]{1,0:T(8,128)S(1)}, s32[]{:T(128)}, /*index=5*/s32[512]{0...) while((s32[]{:T(128)}, f32[512,128]{1,0:T(8,128)S(1)}, ...), condition=%wide.region_12.12_spmd, body=%wide.region_11.11_spmd.sunk | while | flops 338625536 | bytes 7229683 | solution.py:163
  340.8 2.0 fusion.76
  347.0 1.9 fusion.76
  354.1 12.4 %while.80 = (s32[]{:T(128)}, f32[512,128]{1,0:T(8,128)S(1)}, f32[4096,128]{1,0:T(8,128)}, f32[4096,128]{1,0:T(8,128)S(1)}, s32[]{:T(128)}, /*index=5*/s32[512]{0...) while((s32[]{:T(128)}, f32[512,128]{1,0:T(8,128)S(1)}, ...), condition=%wide.region_12.12_spmd, body=%wide.region_11.11_spmd.sunk | while | flops 338625536 | bytes 7229683 | solution.py:163
  358.4 2.0 fusion.76
  364.6 2.0 fusion.76
  367.4 2.1 reduce.8
  369.5 2.3 reshape.140
  371.8 9.8 %all-to-all-start.7 = ((bf16[32,2,8192]{2,1,0:T(2,128)(2,1)}), bf16[32,2,8192]{2,1,0:T(2,128)(2,1)}, u32[]{:S(2)}, u32[]{:S(2)}) async-start(bf16[32,2,8192]{2,1,0:T(2,128)(2,1)} %reshape.140), calls=%async_computation.7 | async-start | bytes 2097152 | tf_op jit(solution)/shard_map/all_to_all | solution.py:233
  381.6 2.9 fusion.28
  384.5 2.7 reduce.7
  388.3 17.4 %all-to-all-done.7 = bf16[32,2,8192]{2,1,0:T(2,128)(2,1)} async-done(((bf16[32,2,8192]{2,1,0:T(2,128)(2,1)}), bf16[32,2,8192]{2,1,0:T(2,128)(2,1)}, u32[]{:S(2)}, u32[]{:S(2)}) %all-to-all-start.7) | async-done | bytes 1048608 | tf_op jit(solution)/shard_map/all_to_all | solution.py:233
  405.7 8.5 %all-to-all-start.6 = ((bf16[32,2,8192]{2,1,0:T(2,128)(2,1)}), bf16[32,2,8192]{2,1,0:T(2,128)(2,1)S(1)}, u32[]{:S(2)}, u32[]{:S(2)}) async-start(bf16[32,2,8192]{2,1,0:T(2,128)(2,1)} %reshape.138), calls=%async_computation.6 | async-start | bytes 2097152 | tf_op jit(solution)/shard_map/all_to_all | solution.py:232
  414.2 2.1 reduce.6
  416.2 2.2 reshape.136
  418.5 19.3 %all-to-all-done.6 = bf16[32,2,8192]{2,1,0:T(2,128)(2,1)S(1)} async-done(((bf16[32,2,8192]{2,1,0:T(2,128)(2,1)}), bf16[32,2,8192]{2,1,0:T(2,128)(2,1)S(1)}, u32[]{:S(2)}, u32[]{:S(2)}) %all-to-all-start.6) | async-done | bytes 1048608 | tf_op jit(solution)/shard_map/all_to_all | solution.py:232
  437.8 8.5 %all-to-all-start.5 = ((bf16[32,2,8192]{2,1,0:T(2,128)(2,1)}), bf16[32,2,8192]{2,1,0:T(2,128)(2,1)}, u32[]{:S(2)}, u32[]{:S(2)}) async-start(bf16[32,2,8192]{2,1,0:T(2,128)(2,1)} %reshape.136), calls=%async_computation.5 | async-start | bytes 2097152 | tf_op jit(solution)/shard_map/all_to_all | solution.py:231
  447.0 5.8 %reshape.135 = bf16[4096,1,128]{2,1,0:T(2,128)(2,1)} reshape(bf16[32,2,8192]{2,1,0:T(2,128)(2,1)} %all-to-all-done.3) | data formatting | bytes 2097152
  452.8 1.7 copy.86
  455.6 78.9 %psum.15 = f32[]{:T(128)} all-reduce(f32[]{:T(128)} %fusion.33), channel_id=1, replica_groups=mesh['dp'=8,'seq'=32] {'seq'}, use_global_device_ids=true, to_apply=%region_18.19 | all-reduce | flops 1 | bytes 8 | tf_op jit(solution)/shard_map/psum | solution.py:209
  537.1 4.3 reshape.141
  547.1 4.3 reshape.137
  (274 shorter events, 128.3 us)
Async XLA Ops:
  0.6 12.1 %copy-start.8 = (bf16[1,128,512]{2,1,0:T(8,128)(2,1)S(1)}, bf16[1,128,512]{2,1,0:T(8,128)(2,1)}, u32[]{:S(2)}) copy-start(bf16[1,128,512]{2,1,0:T(8,128)(2,1)} %param.13) | copy-start | bytes 393220
  2.9 35.0 %all-to-all-start.2 = ((bf16[128,32,128]{2,0,1:T(8,128)(2,1)}), bf16[128,32,128]{2,0,1:T(8,128)(2,1)S(1)}, u32[]{:S(2)}, u32[]{:S(2)}) async-start(bf16[128,32,128]{2,0,1:T(8,128)(2,1)} %bitcast.12), calls=%async_computation.2 | async-start | bytes 2097152 | tf_op jit(solution)/shard_map/all_to_all | solution.py:196
  12.7 34.8 %copy-start.7 = (bf16[1,128,4096]{2,1,0:T(8,128)(2,1)S(1)}, bf16[1,128,4096]{2,1,0:T(8,128)(2,1)}, u32[]{:S(2)}) copy-start(bf16[1,128,4096]{2,1,0:T(8,128)(2,1)} %param.12) | copy-start | bytes 3145732
  39.1 32.6 %all-to-all-start.1 = ((bf16[128,32,128]{2,0,1:T(8,128)(2,1)}), bf16[128,32,128]{2,0,1:T(8,128)(2,1)S(1)}, u32[]{:S(2)}, u32[]{:S(2)}) async-start(bf16[128,32,128]{2,0,1:T(8,128)(2,1)} %bitcast.8), calls=%async_computation.1 | async-start | bytes 2097152 | tf_op jit(solution)/shard_map/all_to_all | solution.py:195
  47.8 32.4 %copy-start.10 = (s32[1,128]{1,0:T(1,128)S(1)}, s32[1,128]{1,0:T(1,128)}, u32[]{:S(2)}) copy-start(s32[1,128]{1,0:T(1,128)} %param.17) | copy-start | bytes 1540
  47.8 109.0 %copy-start.9 = (s32[1,16]{1,0:T(1,128)S(1)}, s32[1,16]{1,0:T(1,128)}, u32[]{:S(2)}) copy-start(s32[1,16]{1,0:T(1,128)} %param.16) | copy-start | bytes 196
  71.6 91.4 %all-to-all-start = ((bf16[128,32,128]{2,0,1:T(8,128)(2,1)}), bf16[128,32,128]{2,0,1:T(8,128)(2,1)}, u32[]{:S(2)}, u32[]{:S(2)}) async-start(bf16[128,32,128]{2,0,1:T(8,128)(2,1)} %copy.68), calls=%async_computation | async-start | bytes 2097152 | tf_op jit(solution)/shard_map/all_to_all | solution.py:188
  158.7 3.4 copy-start.3
  163.0 48.6 %all-to-all-start.4 = ((bf16[128,32,128]{2,0,1:T(8,128)(2,1)}), bf16[128,32,128]{2,0,1:T(8,128)(2,1)}, u32[]{:S(2)}, u32[]{:S(2)}) async-start(bf16[128,32,128]{2,0,1:T(8,128)(2,1)} %copy.74), calls=%async_computation.4 | async-start | bytes 2097152 | tf_op jit(solution)/shard_map/all_to_all | solution.py:213
  206.8 4.8 copy-start.1
  206.8 4.8 copy-start.2
  211.6 160.1 %all-to-all-start.3 = ((bf16[32,2,8192]{2,1,0:T(2,128)(2,1)}), bf16[32,2,8192]{2,1,0:T(2,128)(2,1)}, u32[]{:S(2)}, u32[]{:S(2)}) async-start(bf16[32,2,8192]{2,1,0:T(2,128)(2,1)} %reshape.134), calls=%async_computation.3 | async-start | bytes 2097152 | tf_op jit(solution)/shard_map/all_to_all | solution.py:201
  369.5 12.1 %copy-start = (f32[4096,128]{1,0:T(8,128)S(1)}, f32[4096,128]{1,0:T(8,128)}, u32[]{:S(2)}) copy-start(f32[4096,128]{1,0:T(8,128)} %get-tuple-element.611) | copy-start | bytes 6291460
  371.8 33.9 %all-to-all-start.7 = ((bf16[32,2,8192]{2,1,0:T(2,128)(2,1)}), bf16[32,2,8192]{2,1,0:T(2,128)(2,1)}, u32[]{:S(2)}, u32[]{:S(2)}) async-start(bf16[32,2,8192]{2,1,0:T(2,128)(2,1)} %reshape.140), calls=%async_computation.7 | async-start | bytes 2097152 | tf_op jit(solution)/shard_map/all_to_all | solution.py:233
  405.7 32.1 %all-to-all-start.6 = ((bf16[32,2,8192]{2,1,0:T(2,128)(2,1)}), bf16[32,2,8192]{2,1,0:T(2,128)(2,1)S(1)}, u32[]{:S(2)}, u32[]{:S(2)}) async-start(bf16[32,2,8192]{2,1,0:T(2,128)(2,1)} %reshape.138), calls=%async_computation.6 | async-start | bytes 2097152 | tf_op jit(solution)/shard_map/all_to_all | solution.py:232
  416.2 30.1 %copy-start.4 = (bf16[1,128,4096]{1,2,0:T(8,128)(2,1)S(1)}, bf16[1,128,4096]{1,2,0:T(8,128)(2,1)}, u32[]{:S(2)}) copy-start(bf16[1,128,4096]{1,2,0:T(8,128)(2,1)} %copy-done.3) | copy-start | bytes 3145732
  437.8 9.2 %copy-start.5 = (bf16[32,2,8192]{2,1,0:T(2,128)(2,1)}, bf16[32,2,8192]{2,1,0:T(2,128)(2,1)S(1)}, u32[]{:S(2)}) copy-start(bf16[32,2,8192]{2,1,0:T(2,128)(2,1)S(1)} %all-to-all-done.6) | copy-start | bytes 3145732
  437.8 109.3 %all-to-all-start.5 = ((bf16[32,2,8192]{2,1,0:T(2,128)(2,1)}), bf16[32,2,8192]{2,1,0:T(2,128)(2,1)}, u32[]{:S(2)}, u32[]{:S(2)}) async-start(bf16[32,2,8192]{2,1,0:T(2,128)(2,1)} %reshape.136), calls=%async_computation.5 | async-start | bytes 2097152 | tf_op jit(solution)/shard_map/all_to_all | solution.py:231
  541.4 3.4 copy-start.6
where the time goes:
time: 558 us; the launch traced here: 555 us
  blocking collectives  154 us (28%)
  matrix products  121 us (22%)
  waiting for transfers between devices  84.3 us (15%)
  starting transfers between devices  73.2 us (13%)
  local copies, waits for them, and re-layouts  68.4 us (12%)
  other arithmetic  27.3 us (5%)
  loops' own time  21.9 us (4%)
    psum x1, blocking collectives, per_device(): row_sum = lax.psum(loss_part, 'seq')  78.9 us
    psum x1, blocking collectives, per_device(): token_total = lax.psum(local_count, ('dp', 'seq'))  75.4 us
    dot_general x24, matrix products, tile_scores(): lax.dot_general(query_block, key_block, (((1,), (1,)), ((), ())), preferr...  37.2 us
    unnamed x40, local copies, waits for them, and re-layouts  32.4 us
    dot_general x16, matrix products, grad_step(): lax.dot_general(score_grad, query_block, (((0,), (0,)), ((), ())), prefer...  31.4 us
    all_to_all x1, waiting for transfers between devices, per_device(): lax.all_to_all(value_copies, 'seq', split_axis=1, concat_axis=0, tiled=True)  25.1 us
    all_to_all x1, waiting for transfers between devices, per_device(): lax.all_to_all(key_copies, 'seq', split_axis=1, concat_axis=0, tiled=True)  22.4 us
    another operation x1, loops' own time, attend_backward(): return lax.fori_loop(0, block_count, query_step, (empty, empty, empty))  21 us
  transfers between devices with their start and end apart: 8, of which 4 were waited for; matrix products, arithmetic and copies ran while one was open for 37% of the time, Pallas kernels for 0%

commit v1 on v0

v1 whole, which is shorter than its diff:
```python
import functools
import math

import jax
import jax.numpy as jnp
from jax import lax
from jax.experimental import pallas as pl
from jax.experimental.pallas import tpu as pltpu
from jax.sharding import PartitionSpec as P

HD = 128
GROUP = 8
RING = 4
SLOTS = 9
MASKED = -1e30
EXP2_SCALE = HD ** -0.5 * math.log2(math.e)
STRIP = 64

NT = (((1,), (1,)), ((), ()))
NN = (((1,), (0,)), ((), ()))
TN = (((0,), (0,)), ((), ()))


def mxu(a, b, dims):
    return lax.dot_general(a, b, dims, preferred_element_type=jnp.float32)


def attend_kernel(
    block_of, lengths, factor, q_ref, c_ref, mask_ref, kv_ref,
    out_ref, dq_ref, dkv_ref, loss_ref,
    bias, valid, kg, vg, score, prob, sgrad, dk, dv,
):
    tok = q_ref.shape[0]
    kv_width = kv_ref.shape[2] // 2
    slots = kv_ref.shape[0]
    strips = slots * tok // STRIP
    pos = block_of[0] * tok + lax.broadcasted_iota(jnp.int32, (1, tok), 1)
    first = jnp.zeros((1, tok), jnp.int32)
    start = jnp.int32(0)
    for j in range(lengths.shape[1]):
        first = jnp.where(pos >= start, start, first)
        start = start + lengths[0, j]
    for j in range(slots):
        key_pos = block_of[j] * tok + lax.broadcasted_iota(jnp.int32, (tok, tok), 0)
        allowed = (key_pos >= first) & (key_pos <= pos)
        bias[j * tok:(j + 1) * tok, :] = jnp.where(allowed, 0.0, MASKED)
    mask_rows = jnp.broadcast_to(mask_ref[...].astype(jnp.float32), (tok, tok))
    valid[...] = mask_rows.T.astype(jnp.bfloat16)
    loss_ref[...] = jnp.zeros_like(loss_ref)

    def group_step(g, _):
        k_at = pl.multiple_of(g * HD, HD)
        v_at = pl.multiple_of(g * HD + kv_width, HD)
        for j in range(slots):
            kg[j * tok:(j + 1) * tok, :] = kv_ref[j, :, pl.ds(k_at, HD)]
            vg[j * tok:(j + 1) * tok, :] = kv_ref[j, :, pl.ds(v_at, HD)]
        dk[...] = jnp.zeros_like(dk)
        dv[...] = jnp.zeros_like(dv)

        def head_pair_step(pair, _):
            h0 = pl.multiple_of((g * GROUP + 2 * pair) * HD, HD)
            h1 = pl.multiple_of((g * GROUP + 2 * pair + 1) * HD, HD)
            q = jnp.concatenate([q_ref[:, pl.ds(h0, HD)], q_ref[:, pl.ds(h1, HD)]], axis=0)
            up = jnp.concatenate(
                [c_ref[:, pl.ds(h0, HD)] * valid[...], c_ref[:, pl.ds(h1, HD)] * valid[...]],
                axis=0,
            )
            wide = 2 * tok
            score[...] = mxu(kg[...], q, NT)
            top = jnp.full((8, wide), MASKED, jnp.float32)
            for j in range(strips):
                at = slice(j * STRIP, (j + 1) * STRIP)
                b = bias[at, :]
                s = score[at, :] + jnp.concatenate([b, b], axis=1)
                score[at, :] = s
                top = jnp.maximum(top, jnp.max(s.reshape(STRIP // 8, 8, wide), axis=0))
            top = jnp.max(top, axis=0, keepdims=True)
            total = jnp.zeros((8, wide), jnp.float32)
            for j in range(strips):
                at = slice(j * STRIP, (j + 1) * STRIP)
                e = jnp.exp2((score[at, :] - top) * EXP2_SCALE)
                score[at, :] = e
                total = total + jnp.sum(e.reshape(STRIP // 8, 8, wide), axis=0)
            inverse = 1.0 / jnp.sum(total, axis=0, keepdims=True)
            for j in range(strips):
                at = slice(j * STRIP, (j + 1) * STRIP)
                w = score[at, :] * inverse
                score[at, :] = w
                prob[at, :] = w.astype(jnp.bfloat16)
            out_t = mxu(vg[...], prob[...], TN).astype(jnp.bfloat16)
            out = out_t.T
            out_ref[:, pl.ds(h0, HD)] = out[:tok]
            out_ref[:, pl.ds(h1, HD)] = out[tok:]
            up_t = up.T
            terms = up_t.astype(jnp.float32) * out_t.astype(jnp.float32)
            delta = jnp.sum(terms, axis=0, keepdims=True)
            loss_ref[...] += delta[:, :tok] + delta[:, tok:]
            pgrad = mxu(vg[...], up_t, NN)
            for j in range(strips):
                at = slice(j * STRIP, (j + 1) * STRIP)
                sgrad[at, :] = (score[at, :] * (pgrad[at, :] - delta)).astype(jnp.bfloat16)
            dq = (mxu(kg[...], sgrad[...], TN) * factor[0, 0]).astype(jnp.bfloat16).T
            dq_ref[:, pl.ds(h0, HD)] = dq[:tok]
            dq_ref[:, pl.ds(h1, HD)] = dq[tok:]
            dk[...] += mxu(sgrad[...], q, NN)
            dv[...] += mxu(prob[...], up, NN)
            return 0

        lax.fori_loop(0, GROUP // 2, head_pair_step, 0)
        for j in range(slots):
            at = slice(j * tok, (j + 1) * tok)
            dkv_ref[j, :, pl.ds(k_at, HD)] = dk[at, :].astype(jnp.bfloat16)
            dkv_ref[j, :, pl.ds(v_at, HD)] = dv[at, :].astype(jnp.bfloat16)
        return 0

    lax.fori_loop(0, kv_width // HD, group_step, 0)


def attend(block_of, lengths, factor, queries, cotangent, mask, kv):
    tok = queries.shape[0]
    rows = kv.shape[0] * tok
    vmem = pl.BlockSpec(memory_space=pltpu.VMEM)
    smem = pl.BlockSpec(memory_space=pltpu.SMEM)
    f32, bf16 = jnp.float32, jnp.bfloat16
    return pl.pallas_call(
        attend_kernel,
        out_shape=(
            jax.ShapeDtypeStruct(queries.shape, bf16),
            jax.ShapeDtypeStruct(queries.shape, bf16),
            jax.ShapeDtypeStruct(kv.shape, bf16),
            jax.ShapeDtypeStruct((1, tok), f32),
        ),
        in_specs=[smem, smem, smem, vmem, vmem, vmem, vmem],
        out_specs=(vmem, vmem, vmem, vmem),
        scratch_shapes=[
            pltpu.VMEM((rows, tok), f32),
            pltpu.VMEM((tok, tok), bf16),
            pltpu.VMEM((rows, HD), bf16),
            pltpu.VMEM((rows, HD), bf16),
            pltpu.VMEM((rows, 2 * tok), f32),
            pltpu.VMEM((rows, 2 * tok), bf16),
            pltpu.VMEM((rows, 2 * tok), bf16),
            pltpu.VMEM((rows, HD), f32),
            pltpu.VMEM((rows, HD), f32),
        ],
        compiler_params=pltpu.CompilerParams(vmem_limit_bytes=48 * 2**20),
    )(block_of, lengths, factor, queries, cotangent, mask, kv)


def per_device(queries, keys, values, cotangent, lengths, loss_mask):
    seq_count = lax.axis_size("seq")
    dp_count = lax.axis_size("dp")
    tok = queries.shape[1]
    kv_width = keys.shape[2]
    me = lax.axis_index("seq")
    x = lax.rem(me, RING)

    def down(step):
        return [(i, i + step) for i in range(seq_count - step)]

    def up(step):
        return [(i + step, i) for i in range(seq_count - step)]

    def around(step):
        return [(i, i - i % RING + (i + step) % RING) for i in range(seq_count)]

    mask_all = lax.all_gather(loss_mask.astype(jnp.float32), ("dp", "seq"))
    own = jnp.concatenate([keys[0], values[0]], axis=1)
    near = lax.ppermute(own, "seq", down(RING))
    far = lax.ppermute(own, "seq", down(2 * RING))
    got = []
    for step in range(1, RING):
        send = jnp.stack([jnp.where(x + step >= RING, far, own), near])
        got.append(lax.ppermute(send, "seq", around(step)))
    steps = jnp.arange(1, RING, dtype=jnp.int32)
    inside = x >= steps
    block_of = jnp.concatenate([
        jnp.stack([me, me - RING, me - 2 * RING]),
        jnp.where(inside, me - steps, me - RING - steps),
        jnp.where(inside, me - RING - steps, me - steps),
    ]).astype(jnp.int32)
    kv = jnp.stack([own, near, far] + [g[0] for g in got] + [g[1] for g in got])
    token_total = jnp.sum(mask_all)
    grad_scale = jnp.float32(dp_count * seq_count * tok) / token_total
    factor = (grad_scale * HD ** -0.5).reshape(1, 1)
    out, dq, dkv, loss = attend(
        block_of, lengths, factor, queries[0], cotangent[0], loss_mask, kv
    )
    loss_all = lax.all_gather(loss, ("dp", "seq"))
    loss_row = lax.dynamic_index_in_dim(
        loss_all.reshape(dp_count, seq_count * tok), lax.axis_index("dp"), 0, keepdims=False
    )
    row_loss = (grad_scale * jnp.sum(loss_row) / (seq_count * tok)).reshape(1)

    own_sum = dkv[0].astype(jnp.float32)
    near_sum = dkv[1].astype(jnp.float32)
    far_sum = dkv[2].astype(jnp.float32)
    back = [
        lax.ppermute(jnp.stack([dkv[2 + d], dkv[5 + d]]), "seq", around(-d))
        for d in range(1, RING)
    ]
    for d in range(1, RING):
        part = back[d - 1][0].astype(jnp.float32)
        near_sum = near_sum + back[d - 1][1].astype(jnp.float32)
        own_sum = own_sum + jnp.where(x + d < RING, part, 0.0)
        far_sum = far_sum + jnp.where(x + d < RING, 0.0, part)
    near_back = lax.ppermute(near_sum.astype(jnp.bfloat16), "seq", up(RING))
    far_back = lax.ppermute(far_sum.astype(jnp.bfloat16), "seq", up(2 * RING))
    total = own_sum + near_back.astype(jnp.float32) + far_back.astype(jnp.float32)
    grad_k = (total[:, :kv_width] * factor[0, 0]).astype(jnp.bfloat16)
    grad_v = (total[:, kv_width:] * grad_scale).astype(jnp.bfloat16)
    return (out[None], dq[None], grad_k[None], grad_v[None], row_loss)


def solution(mesh):
    return jax.shard_map(
        per_device,
        mesh=mesh,
        in_specs=(
            P("dp", "seq", None),
            P("dp", "seq", None),
            P("dp", "seq", None),
            P("dp", "seq", None),
            P("dp", None),
            P("dp", "seq"),
        ),
        out_specs=(
            P("dp", "seq", None),
            P("dp", "seq", None),
            P("dp", "seq", None),
            P("dp", "seq", None),
            P("dp"),
        ),
        check_vma=False,
    )
```

time: 558 us -> 263 us (0.47)
  matrix products: 121 us -> 0 us
  local copies, waits for them, and re-layouts: 68.4 us -> 8.89 us
  waiting for transfers between devices: 84.3 us -> 37.3 us
  starting transfers between devices: 73.2 us -> 33.2 us
  Pallas kernels: 0 us -> 32.4 us
  blocking collectives: 154 us -> 127 us
  loops' own time: 21.9 us -> 0 us
  other arithmetic: 27.3 us -> 16.6 us
    psum x2 -> x0, blocking collectives: 154 us -> none  [the longest x1 78.9 us: per_device(): row_sum = lax.psum(loss_part, 'seq')]
    all_gather x0 -> x2, blocking collectives: none -> 127 us  [the longest x1 64.3 us: per_device(): loss_all = lax.all_gather(loss, ('dp', 'seq'))]
    dot_general x96 -> x0, matrix products: 121 us -> none  [the longest x24 37.2 us: tile_scores(): lax.dot_general(query_block, key_block, (((1,), (1,)), ((), ())), preferr...]
    all_to_all x8 -> x0, waiting for transfers between devices: 84.3 us -> none  [the longest x1 25.1 us: per_device(): lax.all_to_all(value_copies, 'seq', split_axis=1, concat_axis=0, tiled=True)]
    all_to_all x8 -> x0, starting transfers between devices: 73.2 us -> none  [the longest x1 9.87 us: per_device(): lax.all_to_all(output_head[:, None, :], 'seq', split_axis=0, concat_axis=...]
    ppermute x0 -> x10, waiting for transfers between devices: none -> 37.3 us  [the longest x3 16.1 us: per_device(): lax.ppermute(jnp.stack([dkv[2 + d], dkv[5 + d]]), 'seq', around(-d))]
    ppermute x0 -> x10, starting transfers between devices: none -> 33.2 us  [the longest x3 11 us: per_device(): lax.ppermute(jnp.stack([dkv[2 + d], dkv[5 + d]]), 'seq', around(-d))]
    pallas_call x0 -> x1, Pallas kernels: none -> 32.4 us  [attend(): pl.pallas_call(attend_kernel, out_shape=(jax.ShapeDtypeStruct(queries.sha...]
  transfers between devices with their start and end apart: 8 -> 10, of which waited for: 4 -> 5; matrix products, arithmetic and copies ran while one was open for 37% -> 5% of each run, Pallas kernels for 0% -> 0%
where the time goes in v1:
time: 263 us; the launch traced here: 259 us
  blocking collectives  127 us (48%)
  waiting for transfers between devices  37.3 us (14%)
  starting transfers between devices  33.2 us (13%)
  Pallas kernels  32.4 us (12%)
  other arithmetic  16.6 us (6%)
  local copies, waits for them, and re-layouts  8.89 us (3%)
  between operations  3.21 us (1%)
    all_gather x1, blocking collectives, per_device(): loss_all = lax.all_gather(loss, ('dp', 'seq'))  64.3 us
    all_gather x1, blocking collectives, per_device(): mask_all = lax.all_gather(loss_mask.astype(jnp.float32), ('dp', 'seq'))  63 us
    pallas_call x1, Pallas kernels, attend(): pl.pallas_call(attend_kernel, out_shape=(jax.ShapeDtypeStruct(queries.sha...  32.4 us
    ppermute x3, waiting for transfers between devices, per_device(): lax.ppermute(jnp.stack([dkv[2 + d], dkv[5 + d]]), 'seq', around(-d))  16.1 us
    ppermute x1, waiting for transfers between devices, per_device(): far = lax.ppermute(own, 'seq', down(2 * RING))  12.4 us
    ppermute x3, starting transfers between devices, per_device(): lax.ppermute(jnp.stack([dkv[2 + d], dkv[5 + d]]), 'seq', around(-d))  11 us
    ppermute x3, waiting for transfers between devices, per_device(): got.append(lax.ppermute(send, 'seq', around(step)))  8.9 us
    ppermute x1, starting transfers between devices, per_device(): near_back = lax.ppermute(near_sum.astype(jnp.bfloat16), 'seq', up(RING))  7.05 us
  transfers between devices with their start and end apart: 10, of which 5 were waited for; matrix products, arithmetic and copies ran while one was open for 5% of the time, Pallas kernels for 0%

profile of v1, /device:TPU:128, one launch (start us, length us, event | category | flops | bytes accessed | tf_op | source)
XLA Modules:
  0.0 258.9 jit_solution(5646379079232869940)
XLA Ops:
  0.6 1.0 pad_maximum_fusion.6
  1.6 2.9 %collective-permute-start = (bf16[128,1024]{1,0:T(8,128)(2,1)S(1)}, bf16[128,1024]{1,0:T(8,128)(2,1)}, u32[]{:S(2)}, u32[]{:S(2)}) collective-permute-start(bf16[128,1024]{1,0:T(8,128)(2,1)S(1)} %pad_maximum_fusion.6), channel_id=1, source_target_pairs={{0,4},{1,5},{2,6},{3,7},{4,8},{5,9},{6,10},{7,11},{8,12},{9,13},{1... | collective-permute-start | bytes 786440 | tf_op jit(solution)/shard_map/ppermute | solution.py:169
  4.6 3.4 %collective-permute-start.1 = (bf16[128,1024]{1,0:T(8,128)(2,1)S(1)}, bf16[128,1024]{1,0:T(8,128)(2,1)S(1)}, u32[]{:S(2)}, u32[]{:S(2)}) collective-permute-start(bf16[128,1024]{1,0:T(8,128)(2,1)S(1)} %pad_maximum_fusion.6), channel_id=1, source_target_pairs={{0,8},{1,9},{2,10},{3,11},{4,12},{5,13},{6,14},{7,15},{8,16},{9,17... | collective-permute-start | bytes 786440 | tf_op jit(solution)/shard_map/ppermute | solution.py:170
  8.0 0.7 convert_bitcast_fusion
  8.6 1.0 bitcast_dynamic-update-slice_fusion.1
  9.6 0.5 compare_select_fusion
  10.1 12.4 %collective-permute-done.1 = bf16[128,1024]{1,0:T(8,128)(2,1)S(1)} collective-permute-done((bf16[128,1024]{1,0:T(8,128)(2,1)S(1)}, bf16[128,1024]{1,0:T(8,128)(2,1)S(1)}, u32[]{:S(2)}, u32[]{:S(2)}) %collective-permute-start.1) | collective-permute-done | bytes 262176 | tf_op jit(solution)/shard_map/ppermute | solution.py:170
  22.5 0.0 copy-start.5
  22.5 1.2 select_bitcast_fusion
  23.7 0.0 collective-permute-done
  23.7 0.0 copy-done.5
  23.7 2.2 pad_maximum_fusion
  25.9 0.0 copy-start
  25.9 0.0 copy-start.2
  25.9 0.0 copy-start.3
  25.9 1.5 collective-permute-start.2
  27.4 63.0 %all-gather.2 = f32[256,1,128]{2,1,0:T(1,128)S(1)} all-gather(f32[1,1,128]{2,1,0:T(1,128)S(1)} %convert_bitcast_fusion), channel_id=2, replica_groups=mesh['dp'=8,'seq'=32] {'dp','seq'}, dimensions={0}, use_global_device_ids=true | all-gather | bytes 131584 | tf_op jit(solution)/shard_map/all_gather | solution.py:167
  90.4 0.9 reduce.1
  91.9 0.7 concatenate.6.block_of
  92.6 1.4 collective-permute-start.4
  94.0 1.8 collective-permute-start.3
  95.8 1.0 constant_dynamic-update-slice_fusion
  96.8 1.0 bitcast_dynamic-update-slice_fusion
  97.8 0.0 collective-permute-done.2
  97.8 1.0 slice_dynamic-update-slice_fusion.5
  98.8 6.6 %collective-permute-done.3 = bf16[2,128,1024]{2,1,0:T(8,128)(2,1)S(1)} collective-permute-done((bf16[2,128,1024]{2,1,0:T(8,128)(2,1)}, bf16[2,128,1024]{2,1,0:T(8,128)(2,1)S(1)}, u32[]{:S(2)}, u32[]{:S(2)}) %collective-permute-start.3) | collective-permute-done | bytes 524320 | tf_op jit(solution)/shard_map/ppermute | solution.py:174
  105.4 2.3 collective-permute-done.4
  107.7 1.0 slice_dynamic-update-slice_fusion.2
  108.7 0.0 copy-start.4
  108.7 1.4 copy-done.4
  110.2 0.0 copy-done
  110.2 0.0 copy-done.2
  110.2 0.0 copy-done.3
  110.2 0.0 copy-start.1
  110.2 1.2 copy-done.1
  111.4 32.4 %shard_map.101 = (bf16[128,4096]{1,0:T(8,128)(2,1)}, bf16[128,4096]{1,0:T(8,128)(2,1)}, bf16[9,128,1024]{2,1,0:T(8,128)(2,1)S(1)}, f32[1,128]{1,0:T(1,128)S(1)}) custom-call(s32[9]{0:T(128)S(1)} %concatenate.6.block_of, s32[1,16]{1,0:T(1,128)S(1)} %copy-done.2, f32[1,1]{1,0:T(1,128)} %bitcast.4.factor, bf16[128,4096]{1,0:T(8,128)(2,1)S(1)} %bitcast.40, ...), custom_call_target="tpu_custom_call" | custom-call | tf_op jit(solution)/shard_map/pallas_call | solution.py:125
  143.8 0.2 fusion.18
  143.9 0.9 pad_maximum_fusion.4
  144.8 2.4 collective-permute-start.6
  147.2 0.8 pad_maximum_fusion.5
  148.0 7.6 %collective-permute-start.7 = (bf16[2,128,1024]{2,1,0:T(8,128)(2,1)}, bf16[2,128,1024]{2,1,0:T(8,128)(2,1)S(1)}, u32[]{:S(2)}, u32[]{:S(2)}) collective-permute-start(bf16[2,128,1024]{2,1,0:T(8,128)(2,1)} %pad_maximum_fusion.5), channel_id=1, source_target_pairs={{0,1},{1,2},{2,3},{3,0},{4,5},{5,6},{6,7},{7,4},{8,9},{9,10},{10,1... | collective-permute-start | bytes 1572872 | tf_op jit(solution)/shard_map/ppermute | solution.py:199
  155.7 0.8 pad_maximum_fusion.3
  156.5 1.0 collective-permute-start.5
  157.5 0.0 collective-permute-done.6
  157.5 9.4 %collective-permute-done.7 = bf16[2,128,1024]{2,1,0:T(8,128)(2,1)S(1)} collective-permute-done((bf16[2,128,1024]{2,1,0:T(8,128)(2,1)}, bf16[2,128,1024]{2,1,0:T(8,128)(2,1)S(1)}, u32[]{:S(2)}, u32[]{:S(2)}) %collective-permute-start.7) | collective-permute-done | bytes 524320 | tf_op jit(solution)/shard_map/ppermute | solution.py:199
  166.9 6.6 %collective-permute-done.5 = bf16[2,128,1024]{2,1,0:T(8,128)(2,1)} collective-permute-done((bf16[2,128,1024]{2,1,0:T(8,128)(2,1)}, bf16[2,128,1024]{2,1,0:T(8,128)(2,1)}, u32[]{:S(2)}, u32[]{:S(2)}) %collective-permute-start.5) | collective-permute-done | bytes 524320 | tf_op jit(solution)/shard_map/ppermute | solution.py:199
  173.6 2.2 fusion.10
  175.8 7.1 %collective-permute-start.8 = (bf16[128,1024]{1,0:T(8,128)(2,1)}, bf16[128,1024]{1,0:T(8,128)(2,1)}, u32[]{:S(2)}, u32[]{:S(2)}) collective-permute-start(bf16[128,1024]{1,0:T(8,128)(2,1)} %get-tuple-element.13), channel_id=1, source_target_pairs={{4,0},{5,1},{6,2},{7,3},{8,4},{9,5},{10,6},{11,7},{12,8},{13,9},{1... | collective-permute-start | bytes 786440 | tf_op jit(solution)/shard_map/ppermute | solution.py:207
  182.9 4.1 %collective-permute-start.9 = (bf16[128,1024]{1,0:T(8,128)(2,1)}, bf16[128,1024]{1,0:T(8,128)(2,1)}, u32[]{:S(2)}, u32[]{:S(2)}) collective-permute-start(bf16[128,1024]{1,0:T(8,128)(2,1)} %get-tuple-element.14), channel_id=1, source_target_pairs={{8,0},{9,1},{10,2},{11,3},{12,4},{13,5},{14,6},{15,7},{16,8},{17,9... | collective-permute-start | bytes 786440 | tf_op jit(solution)/shard_map/ppermute | solution.py:208
  186.9 64.3 %all-gather.3 = f32[256,1,128]{2,1,0:T(1,128)S(1)} all-gather(f32[1,1,128]{2,1,0:T(1,128)S(1)} %bitcast.42), channel_id=3, replica_groups=mesh['dp'=8,'seq'=32] {'dp','seq'}, dimensions={0}, use_global_device_ids=true | all-gather | bytes 131584 | tf_op jit(solution)/shard_map/all_gather | solution.py:189
  251.3 0.5 broadcast.26
  251.8 1.6 reduce.7
  253.4 0.9 reshape.55
  254.3 0.6 dynamic-slice_reduce_fusion
  255.6 0.0 collective-permute-done.8
  255.6 0.0 collective-permute-done.9
  255.6 1.4 fusion.5
  257.0 0.7 fusion.15
  (4 shorter events, 0.1 us)
Async XLA Ops:
  1.6 22.1 %collective-permute-start = (bf16[128,1024]{1,0:T(8,128)(2,1)S(1)}, bf16[128,1024]{1,0:T(8,128)(2,1)}, u32[]{:S(2)}, u32[]{:S(2)}) collective-permute-start(bf16[128,1024]{1,0:T(8,128)(2,1)S(1)} %pad_maximum_fusion.6), channel_id=1, source_target_pairs={{0,4},{1,5},{2,6},{3,7},{4,8},{5,9},{6,10},{7,11},{8,12},{9,13},{1... | collective-permute-start | bytes 786440 | tf_op jit(solution)/shard_map/ppermute | solution.py:169
  4.6 17.9 %collective-permute-start.1 = (bf16[128,1024]{1,0:T(8,128)(2,1)S(1)}, bf16[128,1024]{1,0:T(8,128)(2,1)S(1)}, u32[]{:S(2)}, u32[]{:S(2)}) collective-permute-start(bf16[128,1024]{1,0:T(8,128)(2,1)S(1)} %pad_maximum_fusion.6), channel_id=1, source_target_pairs={{0,8},{1,9},{2,10},{3,11},{4,12},{5,13},{6,14},{7,15},{8,16},{9,17... | collective-permute-start | bytes 786440 | tf_op jit(solution)/shard_map/ppermute | solution.py:170
  22.5 1.2 copy-start.5
  25.9 84.3 %copy-start = (bf16[1,128,4096]{2,1,0:T(8,128)(2,1)S(1)}, bf16[1,128,4096]{2,1,0:T(8,128)(2,1)}, u32[]{:S(2)}) copy-start(bf16[1,128,4096]{2,1,0:T(8,128)(2,1)} %param.6) | copy-start | bytes 3145732
  25.9 84.3 %copy-start.2 = (s32[1,16]{1,0:T(1,128)S(1)}, s32[1,16]{1,0:T(1,128)}, u32[]{:S(2)}) copy-start(s32[1,16]{1,0:T(1,128)} %lengths.1) | copy-start | bytes 196
  25.9 84.3 %copy-start.3 = (s32[1,128]{1,0:T(1,128)S(1)}, s32[1,128]{1,0:T(1,128)}, u32[]{:S(2)}) copy-start(s32[1,128]{1,0:T(1,128)} %mask_ref.1) | copy-start | bytes 1540
  25.9 71.9 %collective-permute-start.2 = (bf16[2,128,1024]{2,1,0:T(8,128)(2,1)}, bf16[2,128,1024]{2,1,0:T(8,128)(2,1)}, u32[]{:S(2)}, u32[]{:S(2)}) collective-permute-start(bf16[2,128,1024]{2,1,0:T(8,128)(2,1)} %get-tuple-element.28), channel_id=1, source_target_pairs={{0,1},{1,2},{2,3},{3,0},{4,5},{5,6},{6,7},{7,4},{8,9},{9,10},{10,1... | collective-permute-start | bytes 1572872 | tf_op jit(solution)/shard_map/ppermute | solution.py:174
  92.6 15.1 %collective-permute-start.4 = (bf16[2,128,1024]{2,1,0:T(8,128)(2,1)}, bf16[2,128,1024]{2,1,0:T(8,128)(2,1)S(1)}, u32[]{:S(2)}, u32[]{:S(2)}) collective-permute-start(bf16[2,128,1024]{2,1,0:T(8,128)(2,1)} %get-tuple-element.26), channel_id=1, source_target_pairs={{0,3},{1,0},{2,1},{3,2},{4,7},{5,4},{6,5},{7,6},{8,11},{9,8},{10,9... | collective-permute-start | bytes 1572872 | tf_op jit(solution)/shard_map/ppermute | solution.py:174
  94.0 11.3 %collective-permute-start.3 = (bf16[2,128,1024]{2,1,0:T(8,128)(2,1)}, bf16[2,128,1024]{2,1,0:T(8,128)(2,1)S(1)}, u32[]{:S(2)}, u32[]{:S(2)}) collective-permute-start(bf16[2,128,1024]{2,1,0:T(8,128)(2,1)} %get-tuple-element.27), channel_id=1, source_target_pairs={{0,2},{1,3},{2,0},{3,1},{4,6},{5,7},{6,4},{7,5},{8,10},{9,11},{10,... | collective-permute-start | bytes 1572872 | tf_op jit(solution)/shard_map/ppermute | solution.py:174
  108.7 1.4 copy-start.4
  110.2 1.2 copy-start.1
  144.8 12.7 %collective-permute-start.6 = (bf16[2,128,1024]{2,1,0:T(8,128)(2,1)}, bf16[2,128,1024]{2,1,0:T(8,128)(2,1)S(1)}, u32[]{:S(2)}, u32[]{:S(2)}) collective-permute-start(bf16[2,128,1024]{2,1,0:T(8,128)(2,1)} %pad_maximum_fusion.4), channel_id=1, source_target_pairs={{0,2},{1,3},{2,0},{3,1},{4,6},{5,7},{6,4},{7,5},{8,10},{9,11},{10,... | collective-permute-start | bytes 1572872 | tf_op jit(solution)/shard_map/ppermute | solution.py:199
  148.0 18.9 %collective-permute-start.7 = (bf16[2,128,1024]{2,1,0:T(8,128)(2,1)}, bf16[2,128,1024]{2,1,0:T(8,128)(2,1)S(1)}, u32[]{:S(2)}, u32[]{:S(2)}) collective-permute-start(bf16[2,128,1024]{2,1,0:T(8,128)(2,1)} %pad_maximum_fusion.5), channel_id=1, source_target_pairs={{0,1},{1,2},{2,3},{3,0},{4,5},{5,6},{6,7},{7,4},{8,9},{9,10},{10,1... | collective-permute-start | bytes 1572872 | tf_op jit(solution)/shard_map/ppermute | solution.py:199
  156.5 17.0 %collective-permute-start.5 = (bf16[2,128,1024]{2,1,0:T(8,128)(2,1)}, bf16[2,128,1024]{2,1,0:T(8,128)(2,1)}, u32[]{:S(2)}, u32[]{:S(2)}) collective-permute-start(bf16[2,128,1024]{2,1,0:T(8,128)(2,1)} %pad_maximum_fusion.3), channel_id=1, source_target_pairs={{0,3},{1,0},{2,1},{3,2},{4,7},{5,4},{6,5},{7,6},{8,11},{9,8},{10,9... | collective-permute-start | bytes 1572872 | tf_op jit(solution)/shard_map/ppermute | solution.py:199
  175.8 79.8 %collective-permute-start.8 = (bf16[128,1024]{1,0:T(8,128)(2,1)}, bf16[128,1024]{1,0:T(8,128)(2,1)}, u32[]{:S(2)}, u32[]{:S(2)}) collective-permute-start(bf16[128,1024]{1,0:T(8,128)(2,1)} %get-tuple-element.13), channel_id=1, source_target_pairs={{4,0},{5,1},{6,2},{7,3},{8,4},{9,5},{10,6},{11,7},{12,8},{13,9},{1... | collective-permute-start | bytes 786440 | tf_op jit(solution)/shard_map/ppermute | solution.py:207
  182.9 72.8 %collective-permute-start.9 = (bf16[128,1024]{1,0:T(8,128)(2,1)}, bf16[128,1024]{1,0:T(8,128)(2,1)}, u32[]{:S(2)}, u32[]{:S(2)}) collective-permute-start(bf16[128,1024]{1,0:T(8,128)(2,1)} %get-tuple-element.14), channel_id=1, source_target_pairs={{8,0},{9,1},{10,2},{11,3},{12,4},{13,5},{14,6},{15,7},{16,8},{17,9... | collective-permute-start | bytes 786440 | tf_op jit(solution)/shard_map/ppermute | solution.py:208

commit v2 on v1

v2 whole, which is shorter than its diff:
```python
import functools
import math

import jax
import jax.numpy as jnp
from jax import lax
from jax.experimental import pallas as pl
from jax.experimental.pallas import tpu as pltpu
from jax.sharding import PartitionSpec as P

HD = 128
GROUP = 8
RING = 4
ORDER = (1, 3, 2)
SLOTS = 3 + 2 * len(ORDER)
PARTS = ((0, 2), (2, 2))
MASKED = -1e30
EXP2_SCALE = HD ** -0.5 * math.log2(math.e)
EXTRA = 16
STRIP = 64

NT = (((1,), (1,)), ((), ()))
NN = (((1,), (0,)), ((), ()))
TN = (((0,), (0,)), ((), ()))


def mxu(a, b, dims):
    return lax.dot_general(a, b, dims, preferred_element_type=jnp.float32)


def attend_kernel(block_of, lengths, q_ref, c_ref, mask_ref, count_ref, loss_in, *refs):
    n = len(ORDER)
    key_refs, value_refs = refs[:SLOTS], refs[SLOTS:2 * SLOTS]
    out_ref, dq_ref, loss_ref = refs[2 * SLOTS:2 * SLOTS + 3]
    refs = refs[2 * SLOTS + 3:]
    single_grads, pair_grads = refs[:3], refs[3:3 + n]
    bias, valid, kg, vg, score, prob, sgrad, dk, dv = refs[3 + n:]
    tok = q_ref.shape[0]
    halves = [slice(0, tok), slice(tok, 2 * tok)]
    grads = [r.at[...] for r in single_grads] + [r.at[h] for h in halves for r in pair_grads]
    strips = SLOTS * tok // STRIP

    @pl.when(pl.program_id(0) == 0)
    def _():
        pos = block_of[0] * tok + lax.broadcasted_iota(jnp.int32, (1, tok), 1)
        first = jnp.zeros((1, tok), jnp.int32)
        start = jnp.int32(0)
        for j in range(lengths.shape[1]):
            first = jnp.where(pos >= start, start, first)
            start = start + lengths[0, j]
        for j in range(SLOTS):
            key_pos = block_of[j] * tok + lax.broadcasted_iota(jnp.int32, (tok, tok), 0)
            allowed = (key_pos >= first) & (key_pos <= pos)
            bias[j * tok:(j + 1) * tok, :] = jnp.where(allowed, 0.0, MASKED)
        mask_rows = jnp.broadcast_to(mask_ref[...].astype(jnp.float32), (tok, tok))
        valid[...] = mask_rows.T.astype(jnp.bfloat16)
        loss_ref[...] = loss_in[...]

    for j in range(SLOTS):
        kg[j * tok:(j + 1) * tok, :] = key_refs[j][...]
        vg[j * tok:(j + 1) * tok, :] = value_refs[j][...]
    dk[...] = jnp.zeros_like(dk)
    dv[...] = jnp.zeros_like(dv)

    def head_pair_step(pair, _):
        h0 = pl.multiple_of(2 * pair * HD, HD)
        h1 = pl.multiple_of((2 * pair + 1) * HD, HD)
        q = jnp.concatenate([q_ref[:, pl.ds(h0, HD)], q_ref[:, pl.ds(h1, HD)]], axis=0)
        up = jnp.concatenate(
            [c_ref[:, pl.ds(h0, HD)] * valid[...], c_ref[:, pl.ds(h1, HD)] * valid[...]],
            axis=0,
        )
        wide = 2 * tok
        score[...] = mxu(kg[...], q, NT)
        top = jnp.full((8, wide), MASKED, jnp.float32)
        for j in range(strips):
            at = slice(j * STRIP, (j + 1) * STRIP)
            b = bias[at, :]
            s = score[at, :] + jnp.concatenate([b, b], axis=1)
            score[at, :] = s
            top = jnp.maximum(top, jnp.max(s.reshape(STRIP // 8, 8, wide), axis=0))
        top = jnp.max(top, axis=0, keepdims=True)
        total = jnp.zeros((8, wide), jnp.float32)
        for j in range(strips):
            at = slice(j * STRIP, (j + 1) * STRIP)
            e = jnp.exp2((score[at, :] - top) * EXP2_SCALE)
            score[at, :] = e
            total = total + jnp.sum(e.reshape(STRIP // 8, 8, wide), axis=0)
        inverse = 1.0 / jnp.sum(total, axis=0, keepdims=True)
        for j in range(strips):
            at = slice(j * STRIP, (j + 1) * STRIP)
            w = score[at, :] * inverse
            score[at, :] = w
            prob[at, :] = w.astype(jnp.bfloat16)
        out_t = mxu(vg[...], prob[...], TN).astype(jnp.bfloat16)
        out = out_t.T
        out_ref[:, pl.ds(h0, HD)] = out[:tok]
        out_ref[:, pl.ds(h1, HD)] = out[tok:]
        up_t = up.T
        terms = up_t.astype(jnp.float32) * out_t.astype(jnp.float32)
        delta = jnp.sum(terms, axis=0, keepdims=True)
        loss_ref[...] += delta[:, :tok] + delta[:, tok:]
        pgrad = mxu(vg[...], up_t, NN)
        for j in range(strips):
            at = slice(j * STRIP, (j + 1) * STRIP)
            sgrad[at, :] = (score[at, :] * (pgrad[at, :] - delta)).astype(jnp.bfloat16)
        dq = mxu(kg[...], sgrad[...], TN).T
        dq_ref[:, pl.ds(h0, HD)] = dq[:tok]
        dq_ref[:, pl.ds(h1, HD)] = dq[tok:]
        dk[...] += mxu(sgrad[...], q, NN)
        dv[...] += mxu(prob[...], up, NN)
        return 0

    lax.fori_loop(0, GROUP // 2, head_pair_step, 0)
    for j in range(SLOTS):
        at = slice(j * tok, (j + 1) * tok)
        grads[j][:, :HD] = dk[at, :].astype(jnp.bfloat16)
        grads[j][:, HD:] = dv[at, :].astype(jnp.bfloat16)
    if pair_grads[0].shape[0] == 2 * tok:
        return

    high = loss_ref[...].astype(jnp.bfloat16).astype(jnp.float32)
    middle = (loss_ref[...] - high).astype(jnp.bfloat16).astype(jnp.float32)
    low = loss_ref[...] - high - middle
    row_of = lax.broadcasted_iota(jnp.int32, (EXTRA, tok), 0)
    extra = jnp.zeros((EXTRA, tok), jnp.float32)
    for i, row in enumerate([high, middle, low, count_ref[...]]):
        extra = jnp.where(row_of == i, row, extra)
    for ref in pair_grads:
        ref[2 * tok:, :HD] = extra.astype(jnp.bfloat16)
        ref[2 * tok:, HD:] = extra.astype(jnp.bfloat16)


def attend(part, block_of, lengths, queries, cotangent, mask, counts, loss, blocks):
    first_head, heads = part
    tok = queries.shape[0]
    kv_heads = blocks[0].shape[1] // (2 * HD)
    wide = GROUP * HD
    rows = SLOTS * tok
    n = len(ORDER)
    f32, bf16 = jnp.float32, jnp.bfloat16
    smem = pl.BlockSpec(memory_space=pltpu.SMEM)
    row = pl.BlockSpec((1, tok), lambda g: (0, 0))
    wide_in = pl.BlockSpec((tok, wide), lambda g: (0, first_head + g))
    wide_out = pl.BlockSpec((tok, wide), lambda g: (0, g))
    key = pl.BlockSpec((tok, HD), lambda g: (0, first_head + g))
    value = pl.BlockSpec((tok, HD), lambda g: (0, kv_heads + first_head + g))
    single = pl.BlockSpec((tok, 2 * HD), lambda g: (0, g))
    pair_rows = 2 * tok + (EXTRA if part is PARTS[-1] else 0)
    pair = pl.BlockSpec((pair_rows, 2 * HD), lambda g: (0, g))
    halo = [key] * SLOTS + [value] * SLOTS
    grads = [pltpu.HBM((tok, heads * 2 * HD), bf16)] * 3
    grads += [pltpu.HBM((pair_rows, heads * 2 * HD), bf16)] * n
    work = 12 * heads * GROUP * tok * rows * HD
    result = pl.pallas_call(
        attend_kernel,
        grid=(heads,),
        out_shape=(
            pltpu.HBM((tok, heads * wide), bf16),
            pltpu.HBM((tok, heads * wide), f32),
            jax.ShapeDtypeStruct((1, tok), f32),
            *grads,
        ),
        in_specs=[smem, smem, wide_in, wide_in, row, row, row, *halo],
        out_specs=(wide_out, wide_out, row, *[single] * 3, *[pair] * n),
        scratch_shapes=[
            pltpu.VMEM((rows, tok), f32),
            pltpu.VMEM((tok, tok), bf16),
            pltpu.VMEM((rows, HD), bf16),
            pltpu.VMEM((rows, HD), bf16),
            pltpu.VMEM((rows, 2 * tok), f32),
            pltpu.VMEM((rows, 2 * tok), bf16),
            pltpu.VMEM((rows, 2 * tok), bf16),
            pltpu.VMEM((rows, HD), f32),
            pltpu.VMEM((rows, HD), f32),
        ],
        compiler_params=pltpu.CompilerParams(vmem_limit_bytes=16 * 2**20),
        cost_estimate=pl.CostEstimate(
            flops=2 * work, bytes_accessed=8 * 2**20, transcendentals=work // (12 * HD)
        ),
    )(block_of, lengths, queries, cotangent, mask, counts, loss, *blocks, *blocks)
    return result[0], result[1], result[2], result[3:6], result[6:]


def per_device(queries, keys, values, cotangent, lengths, loss_mask):
    seq_count = lax.axis_size("seq")
    dp_count = lax.axis_size("dp")
    tok = queries.shape[1]
    me = lax.axis_index("seq")
    x = lax.rem(me, RING)

    def down(step):
        return [(i, i + step) for i in range(seq_count - step)]

    def up(step):
        return [(i + step, i) for i in range(seq_count - step)]

    def around(step):
        return [(i, i - i % RING + (i + step) % RING) for i in range(seq_count)]

    steps = jnp.array(ORDER, dtype=jnp.int32)
    inside = x >= steps
    block_of = jnp.concatenate([
        jnp.stack([me, me - RING, me - 2 * RING]),
        jnp.where(inside, me - steps, me - RING - steps),
        jnp.where(inside, me - RING - steps, me - steps),
    ]).astype(jnp.int32)

    def swap(a, axis, bit):
        return a + lax.ppermute(a, axis, [(i, i ^ bit) for i in range(lax.axis_size(axis))])

    own = jnp.concatenate([keys[0], values[0]], axis=1)
    near = lax.ppermute(own, "seq", down(RING))
    counts = swap(swap(loss_mask.astype(jnp.float32), "dp", 1), "dp", 2)
    near, counts = lax.optimization_barrier((near, counts))
    far = lax.ppermute(near, "seq", down(RING))
    near_got = [lax.ppermute(near, "seq", around(step)) for step in ORDER]
    far, *near_got = lax.optimization_barrier((far, *near_got))
    mixed_got = [
        lax.ppermute(jnp.where(x + step >= RING, far, own), "seq", around(step))
        for step in ORDER
    ]
    counts, mixed_got[-1] = lax.optimization_barrier((counts, mixed_got[-1]))
    all_counts = swap(counts, "dp", 4)

    in_hbm = functools.partial(pltpu.with_memory_space_constraint, memory_space=pltpu.HBM)
    blocks = [in_hbm(a) for a in (own, near, far, *mixed_got, *near_got)]
    queries_in, cotangent_in = in_hbm(queries[0]), in_hbm(cotangent[0])
    outs, dqs, sums, backs = [], [], [], []
    loss = jnp.zeros((1, tok), jnp.float32)
    for part in PARTS:
        counts = all_counts if part is PARTS[-1] else counts
        out, dq, loss, dsingle, dpair = attend(
            part, block_of, lengths, queries_in, cotangent_in, loss_mask, counts, loss, blocks
        )
        if backs:
            *dpair, backs[-1] = lax.optimization_barrier((*dpair, backs[-1]))
        outs.append(out)
        dqs.append(dq)
        sums.append(dsingle)
        backs.append([
            lax.ppermute(d, "seq", around(-step)) for step, d in zip(ORDER, dpair)
        ])
    last = 2 * HD * (PARTS[-1][1] - 1)
    terms = jnp.concatenate([counts, loss], axis=0)
    for b in backs[-1]:
        extra = b[2 * tok:2 * tok + 4, last:last + HD].astype(jnp.float32)
        terms = terms + jnp.stack([extra[3], extra[0] + extra[1] + extra[2]])
    columns = [[RING * z + i for z in range(seq_count // RING)] for i in range(RING)]
    terms = jnp.broadcast_to(terms.reshape(1, 2 * tok), (seq_count // RING, 2 * tok))
    terms = lax.all_to_all(terms, "seq", 0, 0, axis_index_groups=columns, tiled=True)
    terms = jnp.sum(terms, axis=0).reshape(2, tok)
    terms = jnp.sum(terms, axis=1)
    grad_scale = jnp.float32(dp_count * seq_count * tok) / terms[0]
    factor = grad_scale * HD ** -0.5
    row_loss = (grad_scale * terms[1] / (seq_count * tok)).reshape(1)

    grad_k, grad_v, totals, before = [], [], [], []
    for part, single, back in zip(PARTS, sums, backs):
        own_sum, near_sum, far_sum = [s.astype(jnp.float32) for s in single]
        for step, b in zip(ORDER, back):
            mixed = b[:tok].astype(jnp.float32)
            near_sum = near_sum + b[tok:2 * tok].astype(jnp.float32)
            own_sum = own_sum + jnp.where(x + step < RING, mixed, 0.0)
            far_sum = far_sum + jnp.where(x + step < RING, 0.0, mixed)
        near_sum, far_sum = near_sum.astype(jnp.bfloat16), far_sum.astype(jnp.bfloat16)
        if before:
            near_sum, far_sum, *before = lax.optimization_barrier((near_sum, far_sum, *before))
            totals[-1] = totals[-1] + before[0].astype(jnp.float32) + before[1].astype(jnp.float32)
        before = [lax.ppermute(near_sum, "seq", up(RING)), lax.ppermute(far_sum, "seq", up(2 * RING))]
        totals.append(own_sum)
    totals[-1] = totals[-1] + before[0].astype(jnp.float32) + before[1].astype(jnp.float32)
    for part, total in zip(PARTS, totals):
        for h in range(part[1]):
            grad_k.append(total[:, 2 * h * HD:(2 * h + 1) * HD] * factor)
            grad_v.append(total[:, (2 * h + 1) * HD:(2 * h + 2) * HD] * grad_scale)
    grad_k = jnp.concatenate(grad_k, axis=1).astype(jnp.bfloat16)
    grad_v = jnp.concatenate(grad_v, axis=1).astype(jnp.bfloat16)
    out = jnp.concatenate(outs, axis=1)
    grad_q = (jnp.concatenate(dqs, axis=1) * factor).astype(jnp.bfloat16)
    return (out[None], grad_q[None], grad_k[None], grad_v[None], row_loss)


def solution(mesh):
    return jax.shard_map(
        per_device,
        mesh=mesh,
        in_specs=(
            P("dp", "seq", None),
            P("dp", "seq", None),
            P("dp", "seq", None),
            P("dp", "seq", None),
            P("dp", None),
            P("dp", "seq"),
        ),
        out_specs=(
            P("dp", "seq", None),
            P("dp", "seq", None),
            P("dp", "seq", None),
            P("dp", "seq", None),
            P("dp"),
        ),
        check_vma=False,
    )
```

time: 263 us -> 134 us (0.51)
  blocking collectives: 127 us -> 0 us
  starting transfers between devices: 33.2 us -> 45.5 us
  local copies, waits for them, and re-layouts: 8.89 us -> 2.71 us
  other arithmetic: 16.6 us -> 11.9 us
  waiting for transfers between devices: 37.3 us -> 33.7 us
    all_gather x2 -> x0, blocking collectives: 127 us -> none  [the longest x1 64.3 us: per_device(): loss_all = lax.all_gather(loss, ('dp', 'seq'))]
    all_to_all x0 -> x1, starting transfers between devices: none -> 7.75 us  [per_device(): lax.all_to_all(terms, 'seq', 0, 0, axis_index_groups=columns, tiled=True)]
    another operation x5 -> x0, other arithmetic: 5.95 us -> none  [the longest x2 3.38 us: per_device(): send = jnp.stack([jnp.where(x + step >= RING, far, own), near])]
    ppermute x9 -> x20, waiting for transfers between devices: 37.3 us -> 31.5 us  [the longest x6 11.7 us: per_device(): lax.ppermute(d, 'seq', around(-step))]
    unnamed x19 -> x56, local copies, waits for them, and re-layouts: 6.59 us -> 1.44 us
    ppermute x9 -> x20, starting transfers between devices: 30.2 us -> 34.8 us  [the longest x6 9.14 us: per_device(): lax.ppermute(d, 'seq', around(-step))]
    convert_element_type x0 -> x7, other arithmetic: none -> 2.81 us  [the longest x1 1.13 us: per_device(): grad_q = (jnp.concatenate(dqs, axis=1) * factor).astype(jnp.bfloat16)]
    pallas_call x1 -> x2, Pallas kernels: 32.4 us -> 33.9 us  [attend(): pl.pallas_call(attend_kernel, grid=(heads,), out_shape=(pltpu.HBM((tok, h...]
  transfers between devices with their start and end apart: 10 -> 22, of which waited for: 5 -> 10; matrix products, arithmetic and copies ran while one was open for 5% -> 6% of each run, Pallas kernels for 0% -> 26%
where the time goes in v2:
time: 134 us; the launch traced here: 131 us
  starting transfers between devices  45.5 us (34%)
  Pallas kernels  33.9 us (25%)
  waiting for transfers between devices  33.7 us (25%)
  other arithmetic  11.9 us (9%)
  between operations  3.56 us (3%)
  local copies, waits for them, and re-layouts  2.71 us (2%)
    pallas_call x2, Pallas kernels, attend(): pl.pallas_call(attend_kernel, grid=(heads,), out_shape=(pltpu.HBM((tok, h...  33.9 us
    ppermute x6, waiting for transfers between devices, per_device(): lax.ppermute(d, 'seq', around(-step))  11.7 us
    ppermute x6, starting transfers between devices, per_device(): lax.ppermute(d, 'seq', around(-step))  9.14 us
    all_to_all x1, starting transfers between devices, per_device(): lax.all_to_all(terms, 'seq', 0, 0, axis_index_groups=columns, tiled=True)  7.75 us
    ppermute x3, waiting for transfers between devices, per_device(): near_got = [lax.ppermute(near, 'seq', around(step)) for step in ORDER]  7.45 us
    ppermute x3, waiting for transfers between devices, per_device(): lax.ppermute(jnp.where(x + step >= RING, far, own), 'seq', around(step))  7.25 us
    ppermute x3, starting transfers between devices, per_device(): near_got = [lax.ppermute(near, 'seq', around(step)) for step in ORDER]  5.05 us
    ppermute x3, starting transfers between devices, per_device(): lax.ppermute(jnp.where(x + step >= RING, far, own), 'seq', around(step))  4.91 us
  transfers between devices with their start and end apart: 22, of which 10 were waited for; matrix products, arithmetic and copies ran while one was open for 6% of the time, Pallas kernels for 26%

profile of v2, /device:TPU:128, one launch (start us, length us, event | category | flops | bytes accessed | tf_op | source)
XLA Modules:
  0.0 131.4 jit_solution(8171688582484444104)
XLA Ops:
  0.6 0.0 copy-start.17
  0.6 0.0 copy-start.18
  0.7 0.0 copy-start.1
  0.7 1.0 pad_maximum_fusion.refs_0_.refs_9_
  1.7 2.9 %collective-permute-start = (bf16[128,1024]{1,0:T(8,128)(2,1)S(1)}, bf16[128,1024]{1,0:T(8,128)(2,1)S(1)}, u32[]{:S(2)}, u32[]{:S(2)}) collective-permute-start(bf16[128,1024]{1,0:T(8,128)(2,1)S(1)} %pad_maximum_fusion.refs_0_.refs_9_), channel_id=1, source_target_pairs={{0,4},{1,5},{2,6},{3,7},{4,8},{5,9},{6,10},{7,11},{8,12},{9,13},{1... | collective-permute-start | bytes 786440 | tf_op jit(solution)/shard_map/ppermute | solution.py:213
  4.6 0.7 convert_element_type.116
  5.3 1.1 collective-permute-done.1
  6.4 0.7 convert_add_fusion
  7.1 1.6 %collective-permute-start.2 = (f32[1,128]{1,0:T(1,128)S(1)}, f32[1,128]{1,0:T(1,128)S(1)}, u32[]{:S(2)}, u32[]{:S(2)}) collective-permute-start(f32[1,128]{1,0:T(1,128)S(1)} %convert_add_fusion), channel_id=1, source_target_pairs={{0,64},{32,96},{64,0},{96,32},{128,192},{160,224},{192,128},{224,1... | collective-permute-start | bytes 1544 | tf_op jit(solution)/shard_map/ppermute | solution.py:210
  8.7 2.0 %collective-permute-done.2 = f32[1,128]{1,0:T(1,128)S(1)} collective-permute-done((f32[1,128]{1,0:T(1,128)S(1)}, f32[1,128]{1,0:T(1,128)S(1)}, u32[]{:S(2)}, u32[]{:S(2)}) %collective-permute-start.2) | collective-permute-done | bytes 544 | tf_op jit(solution)/shard_map/ppermute | solution.py:210
  10.6 2.2 %collective-permute-done.refs_1_.refs_10_ = bf16[128,1024]{1,0:T(8,128)(2,1)S(1)} collective-permute-done((bf16[128,1024]{1,0:T(8,128)(2,1)S(1)}, bf16[128,1024]{1,0:T(8,128)(2,1)S(1)}, u32[]{:S(2)}, u32[]{:S(2)}) %collective-permute-start) | collective-permute-done | bytes 262176 | tf_op jit(solution)/shard_map/ppermute | solution.py:213
  12.9 3.0 %collective-permute-start.6 = (bf16[128,1024]{1,0:T(8,128)(2,1)S(1)}, bf16[128,1024]{1,0:T(8,128)(2,1)S(1)}, u32[]{:S(2)}, u32[]{:S(2)}) collective-permute-start(bf16[128,1024]{1,0:T(8,128)(2,1)S(1)} %collective-permute-done.refs_1_.refs_10_), channel_id=1, source_target_pairs={{0,2},{1,3},{2,0},{3,1},{4,6},{5,7},{6,4},{7,5},{8,10},{9,11},{10,... | collective-permute-start | bytes 786440 | tf_op jit(solution)/shard_map/ppermute | solution.py:217
  15.9 1.1 collective-permute-start.5
  17.0 0.9 collective-permute-start.4
  17.9 1.9 %collective-permute-start.3 = (bf16[128,1024]{1,0:T(8,128)(2,1)S(1)}, bf16[128,1024]{1,0:T(8,128)(2,1)S(1)}, u32[]{:S(2)}, u32[]{:S(2)}) collective-permute-start(bf16[128,1024]{1,0:T(8,128)(2,1)S(1)} %collective-permute-done.refs_1_.refs_10_), channel_id=1, source_target_pairs={{0,4},{1,5},{2,6},{3,7},{4,8},{5,9},{6,10},{7,11},{8,12},{9,13},{1... | collective-permute-start | bytes 786440 | tf_op jit(solution)/shard_map/ppermute | solution.py:216
  19.8 3.8 %collective-permute-done.6.refs_8_.refs_17_ = bf16[128,1024]{1,0:T(8,128)(2,1)S(1)} collective-permute-done((bf16[128,1024]{1,0:T(8,128)(2,1)S(1)}, bf16[128,1024]{1,0:T(8,128)(2,1)S(1)}, u32[]{:S(2)}, u32[]{:S(2)}) %collective-permute-start.6) | collective-permute-done | bytes 262176 | tf_op jit(solution)/shard_map/ppermute | solution.py:217
  23.6 3.7 %collective-permute-done.5.refs_7_.refs_16_ = bf16[128,1024]{1,0:T(8,128)(2,1)S(1)} collective-permute-done((bf16[128,1024]{1,0:T(8,128)(2,1)S(1)}, bf16[128,1024]{1,0:T(8,128)(2,1)S(1)}, u32[]{:S(2)}, u32[]{:S(2)}) %collective-permute-start.5) | collective-permute-done | bytes 262176 | tf_op jit(solution)/shard_map/ppermute | solution.py:217
  27.3 0.1 collective-permute-done.3.refs_2_.refs_11_
  27.4 1.3 %broadcast_select_fusion = (bf16[128,1024]{1,0:T(8,128)(2,1)S(1)}, bf16[128,1024]{1,0:T(8,128)(2,1)S(1)}, bf16[128,1024]{1,0:T(8,128)(2,1)S(1)}) fusion(bf16[128,1024]{1,0:T(8,128)(2,1)S(1)} %collective-permute-done.3.refs_2_.refs_11_, pred[]{:T(512)S(6)} %ge.19, bf16[128,512]{1,0:T(8,128)(2,1)} %bitcast.37, bf16[128,512]{1,0:T(8,128)(2,1)} %bitcast.39, ...), kind=kLoop, calls=%fused_computation.36 | loop fusion | flops 917504 | bytes 1310723 | tf_op jit(solution)/shard_map/jit(_where)/select_n | solution.py:220
  28.7 2.9 %collective-permute-start.7 = (bf16[128,1024]{1,0:T(8,128)(2,1)S(1)}, bf16[128,1024]{1,0:T(8,128)(2,1)S(1)}, u32[]{:S(2)}, u32[]{:S(2)}) collective-permute-start(bf16[128,1024]{1,0:T(8,128)(2,1)S(1)} %get-tuple-element.83), channel_id=1, source_target_pairs={{0,2},{1,3},{2,0},{3,1},{4,6},{5,7},{6,4},{7,5},{8,10},{9,11},{10,... | collective-permute-start | bytes 786440 | tf_op jit(solution)/shard_map/ppermute | solution.py:220
  31.6 1.2 collective-permute-start.9
  32.8 0.8 collective-permute-start.8
  33.6 0.1 concatenate.64.block_of
  33.7 5.8 %collective-permute-done.7.refs_5_.refs_14_ = bf16[128,1024]{1,0:T(8,128)(2,1)S(1)} collective-permute-done((bf16[128,1024]{1,0:T(8,128)(2,1)S(1)}, bf16[128,1024]{1,0:T(8,128)(2,1)S(1)}, u32[]{:S(2)}, u32[]{:S(2)}) %collective-permute-start.7) | collective-permute-done | bytes 262176 | tf_op jit(solution)/shard_map/ppermute | solution.py:220
  39.5 3.2 %collective-permute-start.10 = (f32[1,128]{1,0:T(1,128)S(1)}, f32[1,128]{1,0:T(1,128)S(1)}, u32[]{:S(2)}, u32[]{:S(2)}) collective-permute-start(f32[1,128]{1,0:T(1,128)S(1)} %add.149.count_ref), channel_id=1, source_target_pairs={{0,128},{32,160},{64,192},{96,224},{128,0},{160,32},{192,64},{224,... | collective-permute-start | bytes 1544 | tf_op jit(solution)/shard_map/ppermute | solution.py:210
  42.7 1.4 %collective-permute-done.9.refs_4_.refs_13_ = bf16[128,1024]{1,0:T(8,128)(2,1)S(1)} collective-permute-done((bf16[128,1024]{1,0:T(8,128)(2,1)S(1)}, bf16[128,1024]{1,0:T(8,128)(2,1)S(1)}, u32[]{:S(2)}, u32[]{:S(2)}) %collective-permute-start.9) | collective-permute-done | bytes 262176 | tf_op jit(solution)/shard_map/ppermute | solution.py:220
  44.2 0.6 copy-done.26
  44.8 0.1 copy-done.27
  44.9 16.9 %shard_map.110 = (bf16[128,2048]{1,0:T(8,128)(2,1)}, f32[128,2048]{1,0:T(8,128)}, f32[1,128]{1,0:T(1,128)S(1)}, bf16[128,512]{1,0:T(8,128)(2,1)}, bf16[128,512]{...) custom-call(s32[9]{0:T(128)S(1)} %concatenate.64.block_of, ...), custom_call_target="tpu_custom_call" | custom-call | flops 7247757312 | bytes 8388608 | tf_op jit(solution)/shard_map/pallas_call | solution.py:155
  61.8 2.7 %collective-permute-start.11 = (bf16[256,512]{1,0:T(8,128)(2,1)}, bf16[256,512]{1,0:T(8,128)(2,1)S(1)}, u32[]{:S(2)}, u32[]{:S(2)}) collective-permute-start(bf16[256,512]{1,0:T(8,128)(2,1)} %get-tuple-element.58), channel_id=1, source_target_pairs={{0,3},{1,0},{2,1},{3,2},{4,7},{5,4},{6,5},{7,6},{8,11},{9,8},{10,9... | collective-permute-start | bytes 786440 | tf_op jit(solution)/shard_map/ppermute | solution.py:242
  64.5 0.0 collective-permute-start.12
  64.5 2.1 %collective-permute-start.13 = (bf16[256,512]{1,0:T(8,128)(2,1)}, bf16[256,512]{1,0:T(8,128)(2,1)S(1)}, u32[]{:S(2)}, u32[]{:S(2)}) collective-permute-start(bf16[256,512]{1,0:T(8,128)(2,1)} %get-tuple-element.60), channel_id=1, source_target_pairs={{0,2},{1,3},{2,0},{3,1},{4,6},{5,7},{6,4},{7,5},{8,10},{9,11},{10,... | collective-permute-start | bytes 786440 | tf_op jit(solution)/shard_map/ppermute | solution.py:242
  66.6 0.0 collective-permute-done.10
  66.6 17.1 %shard_map.111 = (bf16[128,2048]{1,0:T(8,128)(2,1)}, f32[128,2048]{1,0:T(8,128)}, f32[1,128]{1,0:T(1,128)S(1)}, bf16[128,512]{1,0:T(8,128)(2,1)}, bf16[128,512]{...) custom-call(s32[9]{0:T(128)S(1)} %concatenate.64.block_of, ...), custom_call_target="tpu_custom_call" | custom-call | flops 7247757312 | bytes 8388608 | tf_op jit(solution)/shard_map/pallas_call | solution.py:155
  83.7 0.0 collective-permute-done.12
  83.7 0.0 collective-permute-done.13
  83.7 1.4 %collective-permute-start.14 = (bf16[272,512]{1,0:T(8,128)(2,1)}, bf16[272,512]{1,0:T(8,128)(2,1)S(1)}, u32[]{:S(2)}, u32[]{:S(2)}) collective-permute-start(bf16[272,512]{1,0:T(8,128)(2,1)} %get-tuple-element.61), channel_id=1, source_target_pairs={{0,3},{1,0},{2,1},{3,2},{4,7},{5,4},{6,5},{7,6},{8,11},{9,8},{10,9... | collective-permute-start | bytes 835592 | tf_op jit(solution)/shard_map/ppermute | solution.py:242
  85.1 2.1 %maximum_bitcast_fusion = bf16[1,128,4096]{2,1,0:T(8,128)(2,1)} fusion(bf16[128,2048]{1,0:T(8,128)(2,1)} %get-tuple-element.51, bf16[128,2048]{1,0:T(8,128)(2,1)S(1)} %copy-done.6), kind=kLoop, calls=%fused_computation.2 | loop fusion | flops 2097152 | bytes 2097152 | tf_op jit(solution)/shard_map/broadcast_in_dim | solution.py:281
  87.3 0.0 copy-start.10
  87.3 0.2 fusion.9
  87.5 2.1 %collective-permute-start.18 = (bf16[128,512]{1,0:T(8,128)(2,1)S(1)}, bf16[128,512]{1,0:T(8,128)(2,1)S(1)}, u32[]{:S(2)}, u32[]{:S(2)}) collective-permute-start(bf16[128,512]{1,0:T(8,128)(2,1)S(1)} %get-tuple-element.79), channel_id=1, source_target_pairs={{8,0},{9,1},{10,2},{11,3},{12,4},{13,5},{14,6},{15,7},{16,8},{17,9... | collective-permute-start | bytes 393224 | tf_op jit(solution)/shard_map/ppermute | solution.py:270
  89.6 2.1 %collective-permute-start.17 = (bf16[128,512]{1,0:T(8,128)(2,1)S(1)}, bf16[128,512]{1,0:T(8,128)(2,1)S(1)}, u32[]{:S(2)}, u32[]{:S(2)}) collective-permute-start(bf16[128,512]{1,0:T(8,128)(2,1)S(1)} %get-tuple-element.80), channel_id=1, source_target_pairs={{4,0},{5,1},{6,2},{7,3},{8,4},{9,5},{10,6},{11,7},{12,8},{13,9},{1... | collective-permute-start | bytes 393224 | tf_op jit(solution)/shard_map/ppermute | solution.py:270
  91.7 0.8 collective-permute-start.15
  92.4 2.1 %collective-permute-start.16 = (bf16[272,512]{1,0:T(8,128)(2,1)S(1)}, bf16[272,512]{1,0:T(8,128)(2,1)S(1)}, u32[]{:S(2)}, u32[]{:S(2)}) collective-permute-start(bf16[272,512]{1,0:T(8,128)(2,1)S(1)} %copy-done.19), channel_id=1, source_target_pairs={{0,2},{1,3},{2,0},{3,1},{4,6},{5,7},{6,4},{7,5},{8,10},{9,11},{10,... | collective-permute-start | bytes 835592 | tf_op jit(solution)/shard_map/ppermute | solution.py:242
  94.6 0.0 collective-permute-done.14
  94.6 11.7 %collective-permute-done.15 = bf16[272,512]{1,0:T(8,128)(2,1)S(1)} collective-permute-done((bf16[272,512]{1,0:T(8,128)(2,1)S(1)}, bf16[272,512]{1,0:T(8,128)(2,1)S(1)}, u32[]{:S(2)}, u32[]{:S(2)}) %collective-permute-start.15) | collective-permute-done | bytes 278560 | tf_op jit(solution)/shard_map/ppermute | solution.py:242
  106.3 0.0 collective-permute-done.16
  106.3 0.0 copy-start.2
  106.4 0.9 fusion.13
  107.2 0.0 collective-permute-done.18
  107.3 0.6 copy-done.11
  107.9 0.1 copy-done.12
  108.0 0.6 broadcast_in_dim.32
  108.6 7.8 %all-to-all-start = ((f32[8,1,256]{2,1,0:T(1,128)}), f32[8,1,256]{2,1,0:T(1,128)}, u32[]{:S(2)}, u32[]{:S(2)}) async-start(f32[8,1,256]{2,1,0:T(1,128)} %broadcast_in_dim.32), calls=%async_computation | async-start | bytes 16384 | tf_op jit(solution)/shard_map/all_to_all | solution.py:251
  116.3 2.5 %collective-permute-start.19 = (bf16[128,512]{1,0:T(8,128)(2,1)}, bf16[128,512]{1,0:T(8,128)(2,1)}, u32[]{:S(2)}, u32[]{:S(2)}) collective-permute-start(bf16[128,512]{1,0:T(8,128)(2,1)} %get-tuple-element.75), channel_id=1, source_target_pairs={{4,0},{5,1},{6,2},{7,3},{8,4},{9,5},{10,6},{11,7},{12,8},{13,9},{1... | collective-permute-start | bytes 393224 | tf_op jit(solution)/shard_map/ppermute | solution.py:270
  118.8 2.5 %collective-permute-start.20 = (bf16[128,512]{1,0:T(8,128)(2,1)}, bf16[128,512]{1,0:T(8,128)(2,1)}, u32[]{:S(2)}, u32[]{:S(2)}) collective-permute-start(bf16[128,512]{1,0:T(8,128)(2,1)} %get-tuple-element.76), channel_id=1, source_target_pairs={{8,0},{9,1},{10,2},{11,3},{12,4},{13,5},{14,6},{15,7},{16,8},{17,9... | collective-permute-start | bytes 393224 | tf_op jit(solution)/shard_map/ppermute | solution.py:270
  121.3 1.1 fusion.5
  122.4 0.7 reduce_sum.18
  123.1 0.1 bitcast_reduce_fusion
  123.2 0.6 fusion.41
  125.2 1.1 fusion
  126.3 1.9 %collective-permute-done.20 = bf16[128,512]{1,0:T(8,128)(2,1)} collective-permute-done((bf16[128,512]{1,0:T(8,128)(2,1)}, bf16[128,512]{1,0:T(8,128)(2,1)}, u32[]{:S(2)}, u32[]{:S(2)}) %collective-permute-start.20) | collective-permute-done | bytes 131104 | tf_op jit(solution)/shard_map/ppermute | solution.py:270
  128.3 1.2 fusion.18
  129.5 0.7 pad_maximum_fusion.1
  (67 shorter events, 0.2 us)
Async XLA Ops:
  0.6 33.0 %copy-start.17 = (s32[3]{0:T(128)S(1)}, s32[3]{0:T(128)}, u32[]{:S(2)}) copy-start(s32[3]{0:T(128)} %constant.40) | copy-start | bytes 40
  0.6 33.0 %copy-start.18 = (s32[3]{0:T(128)S(1)}, s32[3]{0:T(128)}, u32[]{:S(2)}) copy-start(s32[3]{0:T(128)} %constant.33.clone) | copy-start | bytes 40
  0.7 44.3 %copy-start.1 = (s32[1,128]{1,0:T(1,128)S(1)}, s32[1,128]{1,0:T(1,128)}, u32[]{:S(2)}) copy-start(s32[1,128]{1,0:T(1,128)} %mask_ref.3) | copy-start | bytes 1540
  0.7 44.3 %copy-start = (s32[1,16]{1,0:T(1,128)S(1)}, s32[1,16]{1,0:T(1,128)}, u32[]{:S(2)}) copy-start(s32[1,16]{1,0:T(1,128)} %lengths.3) | copy-start | bytes 196
  1.7 42.5 %copy-start.7 = (bf16[128,1024]{1,0:T(8,128)(2,1)}, bf16[128,1024]{1,0:T(8,128)(2,1)S(1)}, u32[]{:S(2)}) copy-start(bf16[128,1024]{1,0:T(8,128)(2,1)S(1)} %pad_maximum_fusion.refs_0_.refs_9_) | copy-start | bytes 786436
  1.7 11.2 %collective-permute-start = (bf16[128,1024]{1,0:T(8,128)(2,1)S(1)}, bf16[128,1024]{1,0:T(8,128)(2,1)S(1)}, u32[]{:S(2)}, u32[]{:S(2)}) collective-permute-start(bf16[128,1024]{1,0:T(8,128)(2,1)S(1)} %pad_maximum_fusion.refs_0_.refs_9_), channel_id=1, source_target_pairs={{0,4},{1,5},{2,6},{3,7},{4,8},{5,9},{6,10},{7,11},{8,12},{9,13},{1... | collective-permute-start | bytes 786440 | tf_op jit(solution)/shard_map/ppermute | solution.py:213
  5.3 1.1 collective-permute-start.1
  7.1 3.5 %collective-permute-start.2 = (f32[1,128]{1,0:T(1,128)S(1)}, f32[1,128]{1,0:T(1,128)S(1)}, u32[]{:S(2)}, u32[]{:S(2)}) collective-permute-start(f32[1,128]{1,0:T(1,128)S(1)} %convert_add_fusion), channel_id=1, source_target_pairs={{0,64},{32,96},{64,0},{96,32},{128,192},{160,224},{192,128},{224,1... | collective-permute-start | bytes 1544 | tf_op jit(solution)/shard_map/ppermute | solution.py:210
  12.9 31.3 %copy-start.21 = (bf16[128,1024]{1,0:T(8,128)(2,1)}, bf16[128,1024]{1,0:T(8,128)(2,1)S(1)}, u32[]{:S(2)}) copy-start(bf16[128,1024]{1,0:T(8,128)(2,1)S(1)} %collective-permute-done.refs_1_.refs_10_) | copy-start | bytes 786436
  12.9 10.7 %collective-permute-start.6 = (bf16[128,1024]{1,0:T(8,128)(2,1)S(1)}, bf16[128,1024]{1,0:T(8,128)(2,1)S(1)}, u32[]{:S(2)}, u32[]{:S(2)}) collective-permute-start(bf16[128,1024]{1,0:T(8,128)(2,1)S(1)} %collective-permute-done.refs_1_.refs_10_), channel_id=1, source_target_pairs={{0,2},{1,3},{2,0},{3,1},{4,6},{5,7},{6,4},{7,5},{8,10},{9,11},{10,... | collective-permute-start | bytes 786440 | tf_op jit(solution)/shard_map/ppermute | solution.py:217
  15.9 11.4 %collective-permute-start.5 = (bf16[128,1024]{1,0:T(8,128)(2,1)S(1)}, bf16[128,1024]{1,0:T(8,128)(2,1)S(1)}, u32[]{:S(2)}, u32[]{:S(2)}) collective-permute-start(bf16[128,1024]{1,0:T(8,128)(2,1)S(1)} %collective-permute-done.refs_1_.refs_10_), channel_id=1, source_target_pairs={{0,3},{1,0},{2,1},{3,2},{4,7},{5,4},{6,5},{7,6},{8,11},{9,8},{10,9... | collective-permute-start | bytes 786440 | tf_op jit(solution)/shard_map/ppermute | solution.py:217
  17.0 10.3 %collective-permute-start.4 = (bf16[128,1024]{1,0:T(8,128)(2,1)S(1)}, bf16[128,1024]{1,0:T(8,128)(2,1)S(1)}, u32[]{:S(2)}, u32[]{:S(2)}) collective-permute-start(bf16[128,1024]{1,0:T(8,128)(2,1)S(1)} %collective-permute-done.refs_1_.refs_10_), channel_id=1, source_target_pairs={{0,1},{1,2},{2,3},{3,0},{4,5},{5,6},{6,7},{7,4},{8,9},{9,10},{10,1... | collective-permute-start | bytes 786440 | tf_op jit(solution)/shard_map/ppermute | solution.py:217
  17.9 9.5 %collective-permute-start.3 = (bf16[128,1024]{1,0:T(8,128)(2,1)S(1)}, bf16[128,1024]{1,0:T(8,128)(2,1)S(1)}, u32[]{:S(2)}, u32[]{:S(2)}) collective-permute-start(bf16[128,1024]{1,0:T(8,128)(2,1)S(1)} %collective-permute-done.refs_1_.refs_10_), channel_id=1, source_target_pairs={{0,4},{1,5},{2,6},{3,7},{4,8},{5,9},{6,10},{7,11},{8,12},{9,13},{1... | collective-permute-start | bytes 786440 | tf_op jit(solution)/shard_map/ppermute | solution.py:216
  23.6 20.6 %copy-start.22 = (bf16[128,1024]{1,0:T(8,128)(2,1)}, bf16[128,1024]{1,0:T(8,128)(2,1)S(1)}, u32[]{:S(2)}) copy-start(bf16[128,1024]{1,0:T(8,128)(2,1)S(1)} %collective-permute-done.6.refs_8_.refs_17_) | copy-start | bytes 786436
  27.3 16.9 %copy-start.23 = (bf16[128,1024]{1,0:T(8,128)(2,1)}, bf16[128,1024]{1,0:T(8,128)(2,1)S(1)}, u32[]{:S(2)}) copy-start(bf16[128,1024]{1,0:T(8,128)(2,1)S(1)} %collective-permute-done.5.refs_7_.refs_16_) | copy-start | bytes 786436
  27.3 16.9 %copy-start.24 = (bf16[128,1024]{1,0:T(8,128)(2,1)}, bf16[128,1024]{1,0:T(8,128)(2,1)S(1)}, u32[]{:S(2)}) copy-start(bf16[128,1024]{1,0:T(8,128)(2,1)S(1)} %collective-permute-done.4.refs_6_.refs_15_) | copy-start | bytes 786436
  27.4 16.8 %copy-start.8 = (bf16[128,1024]{1,0:T(8,128)(2,1)}, bf16[128,1024]{1,0:T(8,128)(2,1)S(1)}, u32[]{:S(2)}) copy-start(bf16[128,1024]{1,0:T(8,128)(2,1)S(1)} %collective-permute-done.3.refs_2_.refs_11_) | copy-start | bytes 786436
  28.7 10.8 %collective-permute-start.7 = (bf16[128,1024]{1,0:T(8,128)(2,1)S(1)}, bf16[128,1024]{1,0:T(8,128)(2,1)S(1)}, u32[]{:S(2)}, u32[]{:S(2)}) collective-permute-start(bf16[128,1024]{1,0:T(8,128)(2,1)S(1)} %get-tuple-element.83), channel_id=1, source_target_pairs={{0,2},{1,3},{2,0},{3,1},{4,6},{5,7},{6,4},{7,5},{8,10},{9,11},{10,... | collective-permute-start | bytes 786440 | tf_op jit(solution)/shard_map/ppermute | solution.py:220
  31.6 12.6 %collective-permute-start.9 = (bf16[128,1024]{1,0:T(8,128)(2,1)S(1)}, bf16[128,1024]{1,0:T(8,128)(2,1)S(1)}, u32[]{:S(2)}, u32[]{:S(2)}) collective-permute-start(bf16[128,1024]{1,0:T(8,128)(2,1)S(1)} %get-tuple-element.81), channel_id=1, source_target_pairs={{0,3},{1,0},{2,1},{3,2},{4,7},{5,4},{6,5},{7,6},{8,11},{9,8},{10,9... | collective-permute-start | bytes 786440 | tf_op jit(solution)/shard_map/ppermute | solution.py:220
  32.8 11.3 %collective-permute-start.8 = (bf16[128,1024]{1,0:T(8,128)(2,1)S(1)}, bf16[128,1024]{1,0:T(8,128)(2,1)S(1)}, u32[]{:S(2)}, u32[]{:S(2)}) collective-permute-start(bf16[128,1024]{1,0:T(8,128)(2,1)S(1)} %get-tuple-element.82), channel_id=1, source_target_pairs={{0,1},{1,2},{2,3},{3,0},{4,5},{5,6},{6,7},{7,4},{8,9},{9,10},{10,1... | collective-permute-start | bytes 786440 | tf_op jit(solution)/shard_map/ppermute | solution.py:220
  39.5 4.7 %copy-start.25 = (bf16[128,1024]{1,0:T(8,128)(2,1)}, bf16[128,1024]{1,0:T(8,128)(2,1)S(1)}, u32[]{:S(2)}) copy-start(bf16[128,1024]{1,0:T(8,128)(2,1)S(1)} %collective-permute-done.7.refs_5_.refs_14_) | copy-start | bytes 786436
  39.5 27.1 %collective-permute-start.10 = (f32[1,128]{1,0:T(1,128)S(1)}, f32[1,128]{1,0:T(1,128)S(1)}, u32[]{:S(2)}, u32[]{:S(2)}) collective-permute-start(f32[1,128]{1,0:T(1,128)S(1)} %add.149.count_ref), channel_id=1, source_target_pairs={{0,128},{32,160},{64,192},{96,224},{128,0},{160,32},{192,64},{224,... | collective-permute-start | bytes 1544 | tf_op jit(solution)/shard_map/ppermute | solution.py:210
  44.1 0.7 copy-start.26
  44.2 0.8 copy-start.27
  61.8 21.9 %collective-permute-start.11 = (bf16[256,512]{1,0:T(8,128)(2,1)}, bf16[256,512]{1,0:T(8,128)(2,1)S(1)}, u32[]{:S(2)}, u32[]{:S(2)}) collective-permute-start(bf16[256,512]{1,0:T(8,128)(2,1)} %get-tuple-element.58), channel_id=1, source_target_pairs={{0,3},{1,0},{2,1},{3,2},{4,7},{5,4},{6,5},{7,6},{8,11},{9,8},{10,9... | collective-permute-start | bytes 786440 | tf_op jit(solution)/shard_map/ppermute | solution.py:242
  64.5 19.2 %collective-permute-start.12 = (bf16[256,512]{1,0:T(8,128)(2,1)}, bf16[256,512]{1,0:T(8,128)(2,1)S(1)}, u32[]{:S(2)}, u32[]{:S(2)}) collective-permute-start(bf16[256,512]{1,0:T(8,128)(2,1)} %get-tuple-element.59), channel_id=1, source_target_pairs={{0,1},{1,2},{2,3},{3,0},{4,5},{5,6},{6,7},{7,4},{8,9},{9,10},{10,1... | collective-permute-start | bytes 786440 | tf_op jit(solution)/shard_map/ppermute | solution.py:242
  64.5 19.2 %collective-permute-start.13 = (bf16[256,512]{1,0:T(8,128)(2,1)}, bf16[256,512]{1,0:T(8,128)(2,1)S(1)}, u32[]{:S(2)}, u32[]{:S(2)}) collective-permute-start(bf16[256,512]{1,0:T(8,128)(2,1)} %get-tuple-element.60), channel_id=1, source_target_pairs={{0,2},{1,3},{2,0},{3,1},{4,6},{5,7},{6,4},{7,5},{8,10},{9,11},{10,... | collective-permute-start | bytes 786440 | tf_op jit(solution)/shard_map/ppermute | solution.py:242
  66.6 18.5 %copy-start.6 = (bf16[128,2048]{1,0:T(8,128)(2,1)S(1)}, bf16[128,2048]{1,0:T(8,128)(2,1)}, u32[]{:S(2)}) copy-start(bf16[128,2048]{1,0:T(8,128)(2,1)} %get-tuple-element.49) | copy-start | bytes 1572868
  83.7 10.9 %collective-permute-start.14 = (bf16[272,512]{1,0:T(8,128)(2,1)}, bf16[272,512]{1,0:T(8,128)(2,1)S(1)}, u32[]{:S(2)}, u32[]{:S(2)}) collective-permute-start(bf16[272,512]{1,0:T(8,128)(2,1)} %get-tuple-element.61), channel_id=1, source_target_pairs={{0,3},{1,0},{2,1},{3,2},{4,7},{5,4},{6,5},{7,6},{8,11},{9,8},{10,9... | collective-permute-start | bytes 835592 | tf_op jit(solution)/shard_map/ppermute | solution.py:242
  85.1 2.2 %copy-start.15 = (bf16[128,512]{1,0:T(8,128)(2,1)S(1)}, bf16[128,512]{1,0:T(8,128)(2,1)}, u32[]{:S(2)}) copy-start(bf16[128,512]{1,0:T(8,128)(2,1)} %get-tuple-element.70) | copy-start | bytes 393220
  85.1 2.2 %copy-start.16 = (bf16[128,512]{1,0:T(8,128)(2,1)S(1)}, bf16[128,512]{1,0:T(8,128)(2,1)}, u32[]{:S(2)}) copy-start(bf16[128,512]{1,0:T(8,128)(2,1)} %get-tuple-element.71) | copy-start | bytes 393220
  87.3 4.4 %copy-start.20 = (bf16[272,512]{1,0:T(8,128)(2,1)S(1)}, bf16[272,512]{1,0:T(8,128)(2,1)}, u32[]{:S(2)}) copy-start(bf16[272,512]{1,0:T(8,128)(2,1)} %get-tuple-element.62) | copy-start | bytes 835588
  87.3 5.1 %copy-start.19 = (bf16[272,512]{1,0:T(8,128)(2,1)S(1)}, bf16[272,512]{1,0:T(8,128)(2,1)}, u32[]{:S(2)}) copy-start(bf16[272,512]{1,0:T(8,128)(2,1)} %get-tuple-element.63) | copy-start | bytes 835588
  87.3 19.0 %copy-start.13 = (bf16[128,512]{1,0:T(8,128)(2,1)S(1)}, bf16[128,512]{1,0:T(8,128)(2,1)}, u32[]{:S(2)}) copy-start(bf16[128,512]{1,0:T(8,128)(2,1)} %get-tuple-element.68) | copy-start | bytes 393220
  87.3 19.0 %copy-start.14 = (bf16[128,512]{1,0:T(8,128)(2,1)S(1)}, bf16[128,512]{1,0:T(8,128)(2,1)}, u32[]{:S(2)}) copy-start(bf16[128,512]{1,0:T(8,128)(2,1)} %get-tuple-element.69) | copy-start | bytes 393220
  87.3 33.9 %copy-start.10 = (bf16[128,512]{1,0:T(8,128)(2,1)S(1)}, bf16[128,512]{1,0:T(8,128)(2,1)}, u32[]{:S(2)}) copy-start(bf16[128,512]{1,0:T(8,128)(2,1)} %get-tuple-element.64) | copy-start | bytes 393220
  87.5 19.7 %collective-permute-start.18 = (bf16[128,512]{1,0:T(8,128)(2,1)S(1)}, bf16[128,512]{1,0:T(8,128)(2,1)S(1)}, u32[]{:S(2)}, u32[]{:S(2)}) collective-permute-start(bf16[128,512]{1,0:T(8,128)(2,1)S(1)} %get-tuple-element.79), channel_id=1, source_target_pairs={{8,0},{9,1},{10,2},{11,3},{12,4},{13,5},{14,6},{15,7},{16,8},{17,9... | collective-permute-start | bytes 393224 | tf_op jit(solution)/shard_map/ppermute | solution.py:270
  89.6 17.7 %collective-permute-start.17 = (bf16[128,512]{1,0:T(8,128)(2,1)S(1)}, bf16[128,512]{1,0:T(8,128)(2,1)S(1)}, u32[]{:S(2)}, u32[]{:S(2)}) collective-permute-start(bf16[128,512]{1,0:T(8,128)(2,1)S(1)} %get-tuple-element.80), channel_id=1, source_target_pairs={{4,0},{5,1},{6,2},{7,3},{8,4},{9,5},{10,6},{11,7},{12,8},{13,9},{1... | collective-permute-start | bytes 393224 | tf_op jit(solution)/shard_map/ppermute | solution.py:270
  91.7 14.6 %collective-permute-start.15 = (bf16[272,512]{1,0:T(8,128)(2,1)S(1)}, bf16[272,512]{1,0:T(8,128)(2,1)S(1)}, u32[]{:S(2)}, u32[]{:S(2)}) collective-permute-start(bf16[272,512]{1,0:T(8,128)(2,1)S(1)} %copy-done.20), channel_id=1, source_target_pairs={{0,1},{1,2},{2,3},{3,0},{4,5},{5,6},{6,7},{7,4},{8,9},{9,10},{10,1... | collective-permute-start | bytes 835592 | tf_op jit(solution)/shard_map/ppermute | solution.py:242
  92.4 13.9 %collective-permute-start.16 = (bf16[272,512]{1,0:T(8,128)(2,1)S(1)}, bf16[272,512]{1,0:T(8,128)(2,1)S(1)}, u32[]{:S(2)}, u32[]{:S(2)}) collective-permute-start(bf16[272,512]{1,0:T(8,128)(2,1)S(1)} %copy-done.19), channel_id=1, source_target_pairs={{0,2},{1,3},{2,0},{3,1},{4,6},{5,7},{6,4},{7,5},{8,10},{9,11},{10,... | collective-permute-start | bytes 835592 | tf_op jit(solution)/shard_map/ppermute | solution.py:242
  106.3 1.0 copy-start.4
  106.3 1.0 copy-start.5
  106.3 18.8 %copy-start.2 = (f32[128,2048]{1,0:T(8,128)S(1)}, f32[128,2048]{1,0:T(8,128)}, u32[]{:S(2)}) copy-start(f32[128,2048]{1,0:T(8,128)} %get-tuple-element.52) | copy-start | bytes 3145732
  106.4 18.8 %copy-start.3 = (f32[128,2048]{1,0:T(8,128)S(1)}, f32[128,2048]{1,0:T(8,128)}, u32[]{:S(2)}) copy-start(f32[128,2048]{1,0:T(8,128)} %get-tuple-element.53) | copy-start | bytes 3145732
  107.2 0.7 copy-start.11
  107.3 0.7 copy-start.12
  108.6 13.8 %all-to-all-start = ((f32[8,1,256]{2,1,0:T(1,128)}), f32[8,1,256]{2,1,0:T(1,128)}, u32[]{:S(2)}, u32[]{:S(2)}) async-start(f32[8,1,256]{2,1,0:T(1,128)} %broadcast_in_dim.32), calls=%async_computation | async-start | bytes 16384 | tf_op jit(solution)/shard_map/all_to_all | solution.py:251
  116.3 10.0 %collective-permute-start.19 = (bf16[128,512]{1,0:T(8,128)(2,1)}, bf16[128,512]{1,0:T(8,128)(2,1)}, u32[]{:S(2)}, u32[]{:S(2)}) collective-permute-start(bf16[128,512]{1,0:T(8,128)(2,1)} %get-tuple-element.75), channel_id=1, source_target_pairs={{4,0},{5,1},{6,2},{7,3},{8,4},{9,5},{10,6},{11,7},{12,8},{13,9},{1... | collective-permute-start | bytes 393224 | tf_op jit(solution)/shard_map/ppermute | solution.py:270
  118.8 9.5 %collective-permute-start.20 = (bf16[128,512]{1,0:T(8,128)(2,1)}, bf16[128,512]{1,0:T(8,128)(2,1)}, u32[]{:S(2)}, u32[]{:S(2)}) collective-permute-start(bf16[128,512]{1,0:T(8,128)(2,1)} %get-tuple-element.76), channel_id=1, source_target_pairs={{8,0},{9,1},{10,2},{11,3},{12,4},{13,5},{14,6},{15,7},{16,8},{17,9... | collective-permute-start | bytes 393224 | tf_op jit(solution)/shard_map/ppermute | solution.py:270
  125.2 3.1 %copy-start.9 = (bf16[128,512]{1,0:T(8,128)(2,1)S(1)}, bf16[128,512]{1,0:T(8,128)(2,1)}, u32[]{:S(2)}) copy-start(bf16[128,512]{1,0:T(8,128)(2,1)} %get-tuple-element.74) | copy-start | bytes 393220

commit v3 on v2

--- a/solution.py
+++ b/solution.py
@@ -10,6 +10,7 @@
 
 HD = 128
 GROUP = 8
+PAIRS = GROUP // 2
 RING = 4
 ORDER = (1, 3, 2)
 SLOTS = 3 + 2 * len(ORDER)
@@ -34,7 +35,8 @@
     out_ref, dq_ref, loss_ref = refs[2 * SLOTS:2 * SLOTS + 3]
     refs = refs[2 * SLOTS + 3:]
     single_grads, pair_grads = refs[:3], refs[3:3 + n]
-    bias, valid, kg, vg, score, prob, sgrad, dk, dv = refs[3 + n:]
+    bias, valid, kg, vg, prob, sgrad = refs[3 + n:9 + n]
+    scores, pgrads = refs[9 + n:9 + n + PAIRS], refs[9 + n + PAIRS:]
     tok = q_ref.shape[0]
     halves = [slice(0, tok), slice(tok, 2 * tok)]
     grads = [r.at[...] for r in single_grads] + [r.at[h] for h in halves for r in pair_grads]
@@ -59,63 +61,74 @@
     for j in range(SLOTS):
         kg[j * tok:(j + 1) * tok, :] = key_refs[j][...]
         vg[j * tok:(j + 1) * tok, :] = value_refs[j][...]
-    dk[...] = jnp.zeros_like(dk)
-    dv[...] = jnp.zeros_like(dv)
-
-    def head_pair_step(pair, _):
-        h0 = pl.multiple_of(2 * pair * HD, HD)
-        h1 = pl.multiple_of((2 * pair + 1) * HD, HD)
-        q = jnp.concatenate([q_ref[:, pl.ds(h0, HD)], q_ref[:, pl.ds(h1, HD)]], axis=0)
-        up = jnp.concatenate(
-            [c_ref[:, pl.ds(h0, HD)] * valid[...], c_ref[:, pl.ds(h1, HD)] * valid[...]],
-            axis=0,
-        )
-        wide = 2 * tok
-        score[...] = mxu(kg[...], q, NT)
+    wide = 2 * tok
+    heads = [slice(i * HD, (i + 1) * HD) for i in range(GROUP)]
+    spans = [slice(i * wide, (i + 1) * wide) for i in range(PAIRS)]
+    strip = [slice(j * STRIP, (j + 1) * STRIP) for j in range(strips)]
+    q = jnp.concatenate([q_ref[:, h] for h in heads], axis=0)
+    up = jnp.concatenate([c_ref[:, h] * valid[...] for h in heads], axis=0)
+    up_t, inverse, out_t, dq = {}, {}, {}, {}
+
+    def products(i):
+        up_t[i] = up[spans[i]].T
+        scores[i][...] = mxu(kg[...], q[spans[i]], NT)
+        pgrads[i][...] = mxu(vg[...], up_t[i], NN)
+
+    def softmax(i):
+        score = scores[i]
         top = jnp.full((8, wide), MASKED, jnp.float32)
-        for j in range(strips):
-            at = slice(j * STRIP, (j + 1) * STRIP)
+        for at in strip:
             b = bias[at, :]
             s = score[at, :] + jnp.concatenate([b, b], axis=1)
             score[at, :] = s
             top = jnp.maximum(top, jnp.max(s.reshape(STRIP // 8, 8, wide), axis=0))
         top = jnp.max(top, axis=0, keepdims=True)
         total = jnp.zeros((8, wide), jnp.float32)
-        for j in range(strips):
-            at = slice(j * STRIP, (j + 1) * STRIP)
+        for at in strip:
             e = jnp.exp2((score[at, :] - top) * EXP2_SCALE)
             score[at, :] = e
             total = total + jnp.sum(e.reshape(STRIP // 8, 8, wide), axis=0)
-        inverse = 1.0 / jnp.sum(total, axis=0, keepdims=True)
-        for j in range(strips):
-            at = slice(j * STRIP, (j + 1) * STRIP)
-            w = score[at, :] * inverse
-            score[at, :] = w
-            prob[at, :] = w.astype(jnp.bfloat16)
-        out_t = mxu(vg[...], prob[...], TN).astype(jnp.bfloat16)
-        out = out_t.T
-        out_ref[:, pl.ds(h0, HD)] = out[:tok]
-        out_ref[:, pl.ds(h1, HD)] = out[tok:]
-        up_t = up.T
-        terms = up_t.astype(jnp.float32) * out_t.astype(jnp.float32)
+        inverse[i] = 1.0 / jnp.sum(total, axis=0, keepdims=True)
+        for at in strip:
+            prob[at, spans[i]] = (score[at, :] * inverse[i]).astype(jnp.bfloat16)
+
+    def output(i):
+        out_t[i] = mxu(vg[...], prob[:, spans[i]], TN).astype(jnp.bfloat16)
+
+    def score_gradient(i):
+        terms = up_t[i].astype(jnp.float32) * out_t[i].astype(jnp.float32)
         delta = jnp.sum(terms, axis=0, keepdims=True)
         loss_ref[...] += delta[:, :tok] + delta[:, tok:]
-        pgrad = mxu(vg[...], up_t, NN)
-        for j in range(strips):
-            at = slice(j * STRIP, (j + 1) * STRIP)
-            sgrad[at, :] = (score[at, :] * (pgrad[at, :] - delta)).astype(jnp.bfloat16)
-        dq = mxu(kg[...], sgrad[...], TN).T
-        dq_ref[:, pl.ds(h0, HD)] = dq[:tok]
-        dq_ref[:, pl.ds(h1, HD)] = dq[tok:]
-        dk[...] += mxu(sgrad[...], q, NN)
-        dv[...] += mxu(prob[...], up, NN)
-        return 0
-
-    lax.fori_loop(0, GROUP // 2, head_pair_step, 0)
+        for at in strip:
+            w = scores[i][at, :] * inverse[i]
+            sgrad[at, spans[i]] = (w * (pgrads[i][at, :] - delta)).astype(jnp.bfloat16)
+
+    def query_gradient(i):
+        dq[i] = mxu(kg[...], sgrad[:, spans[i]], TN).T
+
+    products(0)
+    for i in range(PAIRS + 2):
+        if 0 <= i - 1 < PAIRS:
+            output(i - 1)
+        if i + 1 < PAIRS:
+            products(i + 1)
+        if i < PAIRS:
+            softmax(i)
+        if 0 <= i - 1 < PAIRS:
+            score_gradient(i - 1)
+        if 0 <= i - 2 < PAIRS:
+            query_gradient(i - 2)
+    for i in range(PAIRS):
+        out = out_t[i].T
+        for part, h in enumerate(heads[2 * i:2 * i + 2]):
+            out_ref[:, h] = out[part * tok:(part + 1) * tok]
+            dq_ref[:, h] = dq[i][part * tok:(part + 1) * tok]
+    dk = mxu(sgrad[...], q, NN).astype(jnp.bfloat16)
+    dv = mxu(prob[...], up, NN).astype(jnp.bfloat16)
     for j in range(SLOTS):
         at = slice(j * tok, (j + 1) * tok)
-        grads[j][:, :HD] = dk[at, :].astype(jnp.bfloat16)
-        grads[j][:, HD:] = dv[at, :].astype(jnp.bfloat16)
+        grads[j][:, :HD] = dk[at, :]
+        grads[j][:, HD:] = dv[at, :]
     if pair_grads[0].shape[0] == 2 * tok:
         return
 
@@ -168,13 +181,11 @@
             pltpu.VMEM((tok, tok), bf16),
             pltpu.VMEM((rows, HD), bf16),
             pltpu.VMEM((rows, HD), bf16),
-            pltpu.VMEM((rows, 2 * tok), f32),
-            pltpu.VMEM((rows, 2 * tok), bf16),
-            pltpu.VMEM((rows, 2 * tok), bf16),
-            pltpu.VMEM((rows, HD), f32),
-            pltpu.VMEM((rows, HD), f32),
+            pltpu.VMEM((rows, GROUP * tok), bf16),
+            pltpu.VMEM((rows, GROUP * tok), bf16),
+            *[pltpu.VMEM((rows, 2 * tok), f32)] * (2 * PAIRS),
         ],
-        compiler_params=pltpu.CompilerParams(vmem_limit_bytes=16 * 2**20),
+        compiler_params=pltpu.CompilerParams(vmem_limit_bytes=32 * 2**20),
         cost_estimate=pl.CostEstimate(
             flops=2 * work, bytes_accessed=8 * 2**20, transcendentals=work // (12 * HD)
         ),

time: 134 us -> 124 us (0.925)
  Pallas kernels: 33.9 us -> 24.3 us
    pallas_call x2, Pallas kernels: 33.9 us -> 24.3 us  [attend(): pl.pallas_call(attend_kernel, grid=(heads,), out_shape=(pltpu.HBM((tok, h...]
  transfers between devices with their start and end apart: 22 -> 22, of which waited for: 10 -> 11; matrix products, arithmetic and copies ran while one was open for 6% -> 7% of each run, Pallas kernels for 26% -> 20%
where the time goes in v3:
time: 124 us; the launch traced here: 122 us
  starting transfers between devices  44.9 us (36%)
  waiting for transfers between devices  34.4 us (28%)
  Pallas kernels  24.3 us (20%)
  other arithmetic  11.9 us (10%)
  between operations  3.55 us (3%)
  local copies, waits for them, and re-layouts  2.71 us (2%)
    pallas_call x2, Pallas kernels, attend(): pl.pallas_call(attend_kernel, grid=(heads,), out_shape=(pltpu.HBM((tok, h...  24.3 us
    ppermute x6, waiting for transfers between devices, per_device(): lax.ppermute(d, 'seq', around(-step))  12.4 us
    ppermute x6, starting transfers between devices, per_device(): lax.ppermute(d, 'seq', around(-step))  8.51 us
    all_to_all x1, starting transfers between devices, per_device(): lax.all_to_all(terms, 'seq', 0, 0, axis_index_groups=columns, tiled=True)  7.75 us
    ppermute x3, waiting for transfers between devices, per_device(): near_got = [lax.ppermute(near, 'seq', around(step)) for step in ORDER]  7.45 us
    ppermute x3, waiting for transfers between devices, per_device(): lax.ppermute(jnp.where(x + step >= RING, far, own), 'seq', around(step))  7.25 us
    ppermute x3, starting transfers between devices, per_device(): near_got = [lax.ppermute(near, 'seq', around(step)) for step in ORDER]  5.05 us
    ppermute x3, starting transfers between devices, per_device(): lax.ppermute(jnp.where(x + step >= RING, far, own), 'seq', around(step))  4.91 us
  transfers between devices with their start and end apart: 22, of which 11 were waited for; matrix products, arithmetic and copies ran while one was open for 7% of the time, Pallas kernels for 20%

profile of v3, /device:TPU:128, one launch (start us, length us, event | category | flops | bytes accessed | tf_op | source)
XLA Modules:
  0.0 121.8 jit_solution(2181675087475367067)
XLA Ops:
  0.6 0.0 copy-start.17
  0.6 0.0 copy-start.18
  0.7 0.0 copy-start.1
  0.7 1.0 pad_maximum_fusion.refs_0_.refs_9_
  1.7 2.9 %collective-permute-start = (bf16[128,1024]{1,0:T(8,128)(2,1)S(1)}, bf16[128,1024]{1,0:T(8,128)(2,1)S(1)}, u32[]{:S(2)}, u32[]{:S(2)}) collective-permute-start(bf16[128,1024]{1,0:T(8,128)(2,1)S(1)} %pad_maximum_fusion.refs_0_.refs_9_), channel_id=1, source_target_pairs={{0,4},{1,5},{2,6},{3,7},{4,8},{5,9},{6,10},{7,11},{8,12},{9,13},{1... | collective-permute-start | bytes 786440 | tf_op jit(solution)/shard_map/ppermute | solution.py:224
  4.6 0.7 convert_element_type.116
  5.3 1.1 collective-permute-done.1
  6.4 0.7 convert_add_fusion
  7.1 1.6 %collective-permute-start.2 = (f32[1,128]{1,0:T(1,128)S(1)}, f32[1,128]{1,0:T(1,128)S(1)}, u32[]{:S(2)}, u32[]{:S(2)}) collective-permute-start(f32[1,128]{1,0:T(1,128)S(1)} %convert_add_fusion), channel_id=1, source_target_pairs={{0,64},{32,96},{64,0},{96,32},{128,192},{160,224},{192,128},{224,1... | collective-permute-start | bytes 1544 | tf_op jit(solution)/shard_map/ppermute | solution.py:221
  8.7 2.0 %collective-permute-done.2 = f32[1,128]{1,0:T(1,128)S(1)} collective-permute-done((f32[1,128]{1,0:T(1,128)S(1)}, f32[1,128]{1,0:T(1,128)S(1)}, u32[]{:S(2)}, u32[]{:S(2)}) %collective-permute-start.2) | collective-permute-done | bytes 544 | tf_op jit(solution)/shard_map/ppermute | solution.py:221
  10.6 2.2 %collective-permute-done.refs_1_.refs_10_ = bf16[128,1024]{1,0:T(8,128)(2,1)S(1)} collective-permute-done((bf16[128,1024]{1,0:T(8,128)(2,1)S(1)}, bf16[128,1024]{1,0:T(8,128)(2,1)S(1)}, u32[]{:S(2)}, u32[]{:S(2)}) %collective-permute-start) | collective-permute-done | bytes 262176 | tf_op jit(solution)/shard_map/ppermute | solution.py:224
  12.9 3.0 %collective-permute-start.6 = (bf16[128,1024]{1,0:T(8,128)(2,1)S(1)}, bf16[128,1024]{1,0:T(8,128)(2,1)S(1)}, u32[]{:S(2)}, u32[]{:S(2)}) collective-permute-start(bf16[128,1024]{1,0:T(8,128)(2,1)S(1)} %collective-permute-done.refs_1_.refs_10_), channel_id=1, source_target_pairs={{0,2},{1,3},{2,0},{3,1},{4,6},{5,7},{6,4},{7,5},{8,10},{9,11},{10,... | collective-permute-start | bytes 786440 | tf_op jit(solution)/shard_map/ppermute | solution.py:228
  15.9 1.1 collective-permute-start.5
  17.0 0.9 collective-permute-start.4
  17.9 1.9 %collective-permute-start.3 = (bf16[128,1024]{1,0:T(8,128)(2,1)S(1)}, bf16[128,1024]{1,0:T(8,128)(2,1)S(1)}, u32[]{:S(2)}, u32[]{:S(2)}) collective-permute-start(bf16[128,1024]{1,0:T(8,128)(2,1)S(1)} %collective-permute-done.refs_1_.refs_10_), channel_id=1, source_target_pairs={{0,4},{1,5},{2,6},{3,7},{4,8},{5,9},{6,10},{7,11},{8,12},{9,13},{1... | collective-permute-start | bytes 786440 | tf_op jit(solution)/shard_map/ppermute | solution.py:227
  19.8 3.8 %collective-permute-done.6.refs_8_.refs_17_ = bf16[128,1024]{1,0:T(8,128)(2,1)S(1)} collective-permute-done((bf16[128,1024]{1,0:T(8,128)(2,1)S(1)}, bf16[128,1024]{1,0:T(8,128)(2,1)S(1)}, u32[]{:S(2)}, u32[]{:S(2)}) %collective-permute-start.6) | collective-permute-done | bytes 262176 | tf_op jit(solution)/shard_map/ppermute | solution.py:228
  23.6 3.7 %collective-permute-done.5.refs_7_.refs_16_ = bf16[128,1024]{1,0:T(8,128)(2,1)S(1)} collective-permute-done((bf16[128,1024]{1,0:T(8,128)(2,1)S(1)}, bf16[128,1024]{1,0:T(8,128)(2,1)S(1)}, u32[]{:S(2)}, u32[]{:S(2)}) %collective-permute-start.5) | collective-permute-done | bytes 262176 | tf_op jit(solution)/shard_map/ppermute | solution.py:228
  27.3 0.1 collective-permute-done.3.refs_2_.refs_11_
  27.4 1.3 %broadcast_select_fusion = (bf16[128,1024]{1,0:T(8,128)(2,1)S(1)}, bf16[128,1024]{1,0:T(8,128)(2,1)S(1)}, bf16[128,1024]{1,0:T(8,128)(2,1)S(1)}) fusion(bf16[128,1024]{1,0:T(8,128)(2,1)S(1)} %collective-permute-done.3.refs_2_.refs_11_, pred[]{:T(512)S(6)} %ge.19, bf16[128,512]{1,0:T(8,128)(2,1)} %bitcast.37, bf16[128,512]{1,0:T(8,128)(2,1)} %bitcast.39, ...), kind=kLoop, calls=%fused_computation.36 | loop fusion | flops 917504 | bytes 1310723 | tf_op jit(solution)/shard_map/jit(_where)/select_n | solution.py:231
  28.7 2.9 %collective-permute-start.7 = (bf16[128,1024]{1,0:T(8,128)(2,1)S(1)}, bf16[128,1024]{1,0:T(8,128)(2,1)S(1)}, u32[]{:S(2)}, u32[]{:S(2)}) collective-permute-start(bf16[128,1024]{1,0:T(8,128)(2,1)S(1)} %get-tuple-element.83), channel_id=1, source_target_pairs={{0,2},{1,3},{2,0},{3,1},{4,6},{5,7},{6,4},{7,5},{8,10},{9,11},{10,... | collective-permute-start | bytes 786440 | tf_op jit(solution)/shard_map/ppermute | solution.py:231
  31.6 1.2 %collective-permute-start.9 = (bf16[128,1024]{1,0:T(8,128)(2,1)S(1)}, bf16[128,1024]{1,0:T(8,128)(2,1)S(1)}, u32[]{:S(2)}, u32[]{:S(2)}) collective-permute-start(bf16[128,1024]{1,0:T(8,128)(2,1)S(1)} %get-tuple-element.81), channel_id=1, source_target_pairs={{0,3},{1,0},{2,1},{3,2},{4,7},{5,4},{6,5},{7,6},{8,11},{9,8},{10,9... | collective-permute-start | bytes 786440 | tf_op jit(solution)/shard_map/ppermute | solution.py:231
  32.8 0.8 collective-permute-start.8
  33.6 0.1 concatenate.64.block_of
  33.7 5.8 %collective-permute-done.7.refs_5_.refs_14_ = bf16[128,1024]{1,0:T(8,128)(2,1)S(1)} collective-permute-done((bf16[128,1024]{1,0:T(8,128)(2,1)S(1)}, bf16[128,1024]{1,0:T(8,128)(2,1)S(1)}, u32[]{:S(2)}, u32[]{:S(2)}) %collective-permute-start.7) | collective-permute-done | bytes 262176 | tf_op jit(solution)/shard_map/ppermute | solution.py:231
  39.5 3.2 %collective-permute-start.10 = (f32[1,128]{1,0:T(1,128)S(1)}, f32[1,128]{1,0:T(1,128)S(1)}, u32[]{:S(2)}, u32[]{:S(2)}) collective-permute-start(f32[1,128]{1,0:T(1,128)S(1)} %add.149.count_ref), channel_id=1, source_target_pairs={{0,128},{32,160},{64,192},{96,224},{128,0},{160,32},{192,64},{224,... | collective-permute-start | bytes 1544 | tf_op jit(solution)/shard_map/ppermute | solution.py:221
  42.7 1.4 %collective-permute-done.9.refs_4_.refs_13_ = bf16[128,1024]{1,0:T(8,128)(2,1)S(1)} collective-permute-done((bf16[128,1024]{1,0:T(8,128)(2,1)S(1)}, bf16[128,1024]{1,0:T(8,128)(2,1)S(1)}, u32[]{:S(2)}, u32[]{:S(2)}) %collective-permute-start.9) | collective-permute-done | bytes 262176 | tf_op jit(solution)/shard_map/ppermute | solution.py:231
  44.2 0.6 copy-done.26
  44.8 0.1 copy-done.27
  44.9 12.1 %shard_map.110 = (bf16[128,2048]{1,0:T(8,128)(2,1)}, f32[128,2048]{1,0:T(8,128)}, f32[1,128]{1,0:T(1,128)S(1)}, bf16[128,512]{1,0:T(8,128)(2,1)}, bf16[128,512]{...) custom-call(s32[9]{0:T(128)S(1)} %concatenate.64.block_of, ...), custom_call_target="tpu_custom_call" | custom-call | flops 7247757312 | bytes 8388608 | tf_op jit(solution)/shard_map/pallas_call | solution.py:168
  57.0 2.7 %collective-permute-start.11 = (bf16[256,512]{1,0:T(8,128)(2,1)}, bf16[256,512]{1,0:T(8,128)(2,1)S(1)}, u32[]{:S(2)}, u32[]{:S(2)}) collective-permute-start(bf16[256,512]{1,0:T(8,128)(2,1)} %get-tuple-element.58), channel_id=1, source_target_pairs={{0,3},{1,0},{2,1},{3,2},{4,7},{5,4},{6,5},{7,6},{8,11},{9,8},{10,9... | collective-permute-start | bytes 786440 | tf_op jit(solution)/shard_map/ppermute | solution.py:253
  59.7 0.0 collective-permute-start.12
  59.7 2.1 %collective-permute-start.13 = (bf16[256,512]{1,0:T(8,128)(2,1)}, bf16[256,512]{1,0:T(8,128)(2,1)S(1)}, u32[]{:S(2)}, u32[]{:S(2)}) collective-permute-start(bf16[256,512]{1,0:T(8,128)(2,1)} %get-tuple-element.60), channel_id=1, source_target_pairs={{0,2},{1,3},{2,0},{3,1},{4,6},{5,7},{6,4},{7,5},{8,10},{9,11},{10,... | collective-permute-start | bytes 786440 | tf_op jit(solution)/shard_map/ppermute | solution.py:253
  61.8 12.2 %shard_map.111 = (bf16[128,2048]{1,0:T(8,128)(2,1)}, f32[128,2048]{1,0:T(8,128)}, f32[1,128]{1,0:T(1,128)S(1)}, bf16[128,512]{1,0:T(8,128)(2,1)}, bf16[128,512]{...) custom-call(s32[9]{0:T(128)S(1)} %concatenate.64.block_of, ...), custom_call_target="tpu_custom_call" | custom-call | flops 7247757312 | bytes 8388608 | tf_op jit(solution)/shard_map/pallas_call | solution.py:168
  74.1 0.6 collective-permute-done.12
  74.7 0.0 collective-permute-done.13
  74.7 0.8 collective-permute-start.14
  75.5 2.1 %maximum_bitcast_fusion = bf16[1,128,4096]{2,1,0:T(8,128)(2,1)} fusion(bf16[128,2048]{1,0:T(8,128)(2,1)} %get-tuple-element.51, bf16[128,2048]{1,0:T(8,128)(2,1)S(1)} %copy-done.6), kind=kLoop, calls=%fused_computation.2 | loop fusion | flops 2097152 | bytes 2097152 | tf_op jit(solution)/shard_map/broadcast_in_dim | solution.py:292
  77.7 0.0 copy-start.10
  77.7 0.2 fusion.9
  77.9 2.1 %collective-permute-start.18 = (bf16[128,512]{1,0:T(8,128)(2,1)S(1)}, bf16[128,512]{1,0:T(8,128)(2,1)S(1)}, u32[]{:S(2)}, u32[]{:S(2)}) collective-permute-start(bf16[128,512]{1,0:T(8,128)(2,1)S(1)} %get-tuple-element.79), channel_id=1, source_target_pairs={{8,0},{9,1},{10,2},{11,3},{12,4},{13,5},{14,6},{15,7},{16,8},{17,9... | collective-permute-start | bytes 393224 | tf_op jit(solution)/shard_map/ppermute | solution.py:281
  79.9 2.1 %collective-permute-start.17 = (bf16[128,512]{1,0:T(8,128)(2,1)S(1)}, bf16[128,512]{1,0:T(8,128)(2,1)S(1)}, u32[]{:S(2)}, u32[]{:S(2)}) collective-permute-start(bf16[128,512]{1,0:T(8,128)(2,1)S(1)} %get-tuple-element.80), channel_id=1, source_target_pairs={{4,0},{5,1},{6,2},{7,3},{8,4},{9,5},{10,6},{11,7},{12,8},{13,9},{1... | collective-permute-start | bytes 393224 | tf_op jit(solution)/shard_map/ppermute | solution.py:281
  82.0 1.3 %collective-permute-start.15 = (bf16[272,512]{1,0:T(8,128)(2,1)S(1)}, bf16[272,512]{1,0:T(8,128)(2,1)S(1)}, u32[]{:S(2)}, u32[]{:S(2)}) collective-permute-start(bf16[272,512]{1,0:T(8,128)(2,1)S(1)} %copy-done.20), channel_id=1, source_target_pairs={{0,1},{1,2},{2,3},{3,0},{4,5},{5,6},{6,7},{7,4},{8,9},{9,10},{10,1... | collective-permute-start | bytes 835592 | tf_op jit(solution)/shard_map/ppermute | solution.py:253
  83.3 1.6 %collective-permute-start.16 = (bf16[272,512]{1,0:T(8,128)(2,1)S(1)}, bf16[272,512]{1,0:T(8,128)(2,1)S(1)}, u32[]{:S(2)}, u32[]{:S(2)}) collective-permute-start(bf16[272,512]{1,0:T(8,128)(2,1)S(1)} %copy-done.19), channel_id=1, source_target_pairs={{0,2},{1,3},{2,0},{3,1},{4,6},{5,7},{6,4},{7,5},{8,10},{9,11},{10,... | collective-permute-start | bytes 835592 | tf_op jit(solution)/shard_map/ppermute | solution.py:253
  85.0 11.7 %collective-permute-done.15 = bf16[272,512]{1,0:T(8,128)(2,1)S(1)} collective-permute-done((bf16[272,512]{1,0:T(8,128)(2,1)S(1)}, bf16[272,512]{1,0:T(8,128)(2,1)S(1)}, u32[]{:S(2)}, u32[]{:S(2)}) %collective-permute-start.15) | collective-permute-done | bytes 278560 | tf_op jit(solution)/shard_map/ppermute | solution.py:253
  96.7 0.0 collective-permute-done.16
  96.7 0.0 copy-start.2
  96.7 0.9 fusion.13
  97.6 0.0 collective-permute-done.18
  97.6 0.0 collective-permute-done.17
  97.7 0.6 copy-done.11
  98.3 0.1 copy-done.12
  98.3 0.6 broadcast_in_dim.32
  98.9 7.8 %all-to-all-start = ((f32[8,1,256]{2,1,0:T(1,128)}), f32[8,1,256]{2,1,0:T(1,128)}, u32[]{:S(2)}, u32[]{:S(2)}) async-start(f32[8,1,256]{2,1,0:T(1,128)} %broadcast_in_dim.32), calls=%async_computation | async-start | bytes 16384 | tf_op jit(solution)/shard_map/all_to_all | solution.py:262
  106.7 2.5 %collective-permute-start.19 = (bf16[128,512]{1,0:T(8,128)(2,1)}, bf16[128,512]{1,0:T(8,128)(2,1)}, u32[]{:S(2)}, u32[]{:S(2)}) collective-permute-start(bf16[128,512]{1,0:T(8,128)(2,1)} %get-tuple-element.75), channel_id=1, source_target_pairs={{4,0},{5,1},{6,2},{7,3},{8,4},{9,5},{10,6},{11,7},{12,8},{13,9},{1... | collective-permute-start | bytes 393224 | tf_op jit(solution)/shard_map/ppermute | solution.py:281
  109.1 2.5 %collective-permute-start.20 = (bf16[128,512]{1,0:T(8,128)(2,1)}, bf16[128,512]{1,0:T(8,128)(2,1)}, u32[]{:S(2)}, u32[]{:S(2)}) collective-permute-start(bf16[128,512]{1,0:T(8,128)(2,1)} %get-tuple-element.76), channel_id=1, source_target_pairs={{8,0},{9,1},{10,2},{11,3},{12,4},{13,5},{14,6},{15,7},{16,8},{17,9... | collective-permute-start | bytes 393224 | tf_op jit(solution)/shard_map/ppermute | solution.py:281
  111.6 1.1 fusion.5
  112.7 0.7 reduce_sum.18
  113.5 0.1 bitcast_reduce_fusion
  113.6 0.6 fusion.41
  115.5 1.1 fusion
  116.7 0.0 collective-permute-done.19
  116.7 1.9 %collective-permute-done.20 = bf16[128,512]{1,0:T(8,128)(2,1)} collective-permute-done((bf16[128,512]{1,0:T(8,128)(2,1)}, bf16[128,512]{1,0:T(8,128)(2,1)}, u32[]{:S(2)}, u32[]{:S(2)}) %collective-permute-start.20) | collective-permute-done | bytes 131104 | tf_op jit(solution)/shard_map/ppermute | solution.py:281
  118.6 1.2 %fusion.18 = f32[128,512]{1,0:T(8,128)S(1)} fusion(bf16[128,512]{1,0:T(8,128)(2,1)} %collective-permute-done.20, bf16[128,512]{1,0:T(8,128)(2,1)} %collective-permute-done.19, bf16[128,512]{1,0:T(8,128)(2,1)S(1)} %copy-done.9, pred[]{:T(512)S(6)} %lt.8, pred[]{:T(512)S(6)} %lt.7, pred[]{:T(512)S(6)} %lt.6, bf16[272,512]{1,0:T(8,128)(2,1)} %copy-done.5, ...), kind=kLoop, calls=%fused_computation.32 | loop fusion | flops 917504 | bytes 1048579 | tf_op jit(solution)/shard_map/add | solution.py:283
  119.9 0.7 pad_maximum_fusion.1
  (67 shorter events, 0.2 us)
Async XLA Ops:
  0.6 33.0 %copy-start.17 = (s32[3]{0:T(128)S(1)}, s32[3]{0:T(128)}, u32[]{:S(2)}) copy-start(s32[3]{0:T(128)} %constant.40) | copy-start | bytes 40
  0.6 33.0 %copy-start.18 = (s32[3]{0:T(128)S(1)}, s32[3]{0:T(128)}, u32[]{:S(2)}) copy-start(s32[3]{0:T(128)} %constant.33.clone) | copy-start | bytes 40
  0.7 44.3 %copy-start.1 = (s32[1,128]{1,0:T(1,128)S(1)}, s32[1,128]{1,0:T(1,128)}, u32[]{:S(2)}) copy-start(s32[1,128]{1,0:T(1,128)} %mask_ref.3) | copy-start | bytes 1540
  0.7 44.3 %copy-start = (s32[1,16]{1,0:T(1,128)S(1)}, s32[1,16]{1,0:T(1,128)}, u32[]{:S(2)}) copy-start(s32[1,16]{1,0:T(1,128)} %lengths.3) | copy-start | bytes 196
  1.7 42.5 %copy-start.7 = (bf16[128,1024]{1,0:T(8,128)(2,1)}, bf16[128,1024]{1,0:T(8,128)(2,1)S(1)}, u32[]{:S(2)}) copy-start(bf16[128,1024]{1,0:T(8,128)(2,1)S(1)} %pad_maximum_fusion.refs_0_.refs_9_) | copy-start | bytes 786436
  1.7 11.2 %collective-permute-start = (bf16[128,1024]{1,0:T(8,128)(2,1)S(1)}, bf16[128,1024]{1,0:T(8,128)(2,1)S(1)}, u32[]{:S(2)}, u32[]{:S(2)}) collective-permute-start(bf16[128,1024]{1,0:T(8,128)(2,1)S(1)} %pad_maximum_fusion.refs_0_.refs_9_), channel_id=1, source_target_pairs={{0,4},{1,5},{2,6},{3,7},{4,8},{5,9},{6,10},{7,11},{8,12},{9,13},{1... | collective-permute-start | bytes 786440 | tf_op jit(solution)/shard_map/ppermute | solution.py:224
  5.3 1.1 collective-permute-start.1
  7.1 3.5 %collective-permute-start.2 = (f32[1,128]{1,0:T(1,128)S(1)}, f32[1,128]{1,0:T(1,128)S(1)}, u32[]{:S(2)}, u32[]{:S(2)}) collective-permute-start(f32[1,128]{1,0:T(1,128)S(1)} %convert_add_fusion), channel_id=1, source_target_pairs={{0,64},{32,96},{64,0},{96,32},{128,192},{160,224},{192,128},{224,1... | collective-permute-start | bytes 1544 | tf_op jit(solution)/shard_map/ppermute | solution.py:221
  12.9 31.3 %copy-start.21 = (bf16[128,1024]{1,0:T(8,128)(2,1)}, bf16[128,1024]{1,0:T(8,128)(2,1)S(1)}, u32[]{:S(2)}) copy-start(bf16[128,1024]{1,0:T(8,128)(2,1)S(1)} %collective-permute-done.refs_1_.refs_10_) | copy-start | bytes 786436
  12.9 10.7 %collective-permute-start.6 = (bf16[128,1024]{1,0:T(8,128)(2,1)S(1)}, bf16[128,1024]{1,0:T(8,128)(2,1)S(1)}, u32[]{:S(2)}, u32[]{:S(2)}) collective-permute-start(bf16[128,1024]{1,0:T(8,128)(2,1)S(1)} %collective-permute-done.refs_1_.refs_10_), channel_id=1, source_target_pairs={{0,2},{1,3},{2,0},{3,1},{4,6},{5,7},{6,4},{7,5},{8,10},{9,11},{10,... | collective-permute-start | bytes 786440 | tf_op jit(solution)/shard_map/ppermute | solution.py:228
  15.9 11.4 %collective-permute-start.5 = (bf16[128,1024]{1,0:T(8,128)(2,1)S(1)}, bf16[128,1024]{1,0:T(8,128)(2,1)S(1)}, u32[]{:S(2)}, u32[]{:S(2)}) collective-permute-start(bf16[128,1024]{1,0:T(8,128)(2,1)S(1)} %collective-permute-done.refs_1_.refs_10_), channel_id=1, source_target_pairs={{0,3},{1,0},{2,1},{3,2},{4,7},{5,4},{6,5},{7,6},{8,11},{9,8},{10,9... | collective-permute-start | bytes 786440 | tf_op jit(solution)/shard_map/ppermute | solution.py:228
  17.0 10.3 %collective-permute-start.4 = (bf16[128,1024]{1,0:T(8,128)(2,1)S(1)}, bf16[128,1024]{1,0:T(8,128)(2,1)S(1)}, u32[]{:S(2)}, u32[]{:S(2)}) collective-permute-start(bf16[128,1024]{1,0:T(8,128)(2,1)S(1)} %collective-permute-done.refs_1_.refs_10_), channel_id=1, source_target_pairs={{0,1},{1,2},{2,3},{3,0},{4,5},{5,6},{6,7},{7,4},{8,9},{9,10},{10,1... | collective-permute-start | bytes 786440 | tf_op jit(solution)/shard_map/ppermute | solution.py:228
  17.9 9.5 %collective-permute-start.3 = (bf16[128,1024]{1,0:T(8,128)(2,1)S(1)}, bf16[128,1024]{1,0:T(8,128)(2,1)S(1)}, u32[]{:S(2)}, u32[]{:S(2)}) collective-permute-start(bf16[128,1024]{1,0:T(8,128)(2,1)S(1)} %collective-permute-done.refs_1_.refs_10_), channel_id=1, source_target_pairs={{0,4},{1,5},{2,6},{3,7},{4,8},{5,9},{6,10},{7,11},{8,12},{9,13},{1... | collective-permute-start | bytes 786440 | tf_op jit(solution)/shard_map/ppermute | solution.py:227
  23.6 20.6 %copy-start.22 = (bf16[128,1024]{1,0:T(8,128)(2,1)}, bf16[128,1024]{1,0:T(8,128)(2,1)S(1)}, u32[]{:S(2)}) copy-start(bf16[128,1024]{1,0:T(8,128)(2,1)S(1)} %collective-permute-done.6.refs_8_.refs_17_) | copy-start | bytes 786436
  27.3 16.9 %copy-start.23 = (bf16[128,1024]{1,0:T(8,128)(2,1)}, bf16[128,1024]{1,0:T(8,128)(2,1)S(1)}, u32[]{:S(2)}) copy-start(bf16[128,1024]{1,0:T(8,128)(2,1)S(1)} %collective-permute-done.5.refs_7_.refs_16_) | copy-start | bytes 786436
  27.3 16.9 %copy-start.24 = (bf16[128,1024]{1,0:T(8,128)(2,1)}, bf16[128,1024]{1,0:T(8,128)(2,1)S(1)}, u32[]{:S(2)}) copy-start(bf16[128,1024]{1,0:T(8,128)(2,1)S(1)} %collective-permute-done.4.refs_6_.refs_15_) | copy-start | bytes 786436
  27.4 16.8 %copy-start.8 = (bf16[128,1024]{1,0:T(8,128)(2,1)}, bf16[128,1024]{1,0:T(8,128)(2,1)S(1)}, u32[]{:S(2)}) copy-start(bf16[128,1024]{1,0:T(8,128)(2,1)S(1)} %collective-permute-done.3.refs_2_.refs_11_) | copy-start | bytes 786436
  28.7 10.8 %collective-permute-start.7 = (bf16[128,1024]{1,0:T(8,128)(2,1)S(1)}, bf16[128,1024]{1,0:T(8,128)(2,1)S(1)}, u32[]{:S(2)}, u32[]{:S(2)}) collective-permute-start(bf16[128,1024]{1,0:T(8,128)(2,1)S(1)} %get-tuple-element.83), channel_id=1, source_target_pairs={{0,2},{1,3},{2,0},{3,1},{4,6},{5,7},{6,4},{7,5},{8,10},{9,11},{10,... | collective-permute-start | bytes 786440 | tf_op jit(solution)/shard_map/ppermute | solution.py:231
  31.6 12.6 %collective-permute-start.9 = (bf16[128,1024]{1,0:T(8,128)(2,1)S(1)}, bf16[128,1024]{1,0:T(8,128)(2,1)S(1)}, u32[]{:S(2)}, u32[]{:S(2)}) collective-permute-start(bf16[128,1024]{1,0:T(8,128)(2,1)S(1)} %get-tuple-element.81), channel_id=1, source_target_pairs={{0,3},{1,0},{2,1},{3,2},{4,7},{5,4},{6,5},{7,6},{8,11},{9,8},{10,9... | collective-permute-start | bytes 786440 | tf_op jit(solution)/shard_map/ppermute | solution.py:231
  32.8 11.3 %collective-permute-start.8 = (bf16[128,1024]{1,0:T(8,128)(2,1)S(1)}, bf16[128,1024]{1,0:T(8,128)(2,1)S(1)}, u32[]{:S(2)}, u32[]{:S(2)}) collective-permute-start(bf16[128,1024]{1,0:T(8,128)(2,1)S(1)} %get-tuple-element.82), channel_id=1, source_target_pairs={{0,1},{1,2},{2,3},{3,0},{4,5},{5,6},{6,7},{7,4},{8,9},{9,10},{10,1... | collective-permute-start | bytes 786440 | tf_op jit(solution)/shard_map/ppermute | solution.py:231
  39.5 4.7 %copy-start.25 = (bf16[128,1024]{1,0:T(8,128)(2,1)}, bf16[128,1024]{1,0:T(8,128)(2,1)S(1)}, u32[]{:S(2)}) copy-start(bf16[128,1024]{1,0:T(8,128)(2,1)S(1)} %collective-permute-done.7.refs_5_.refs_14_) | copy-start | bytes 786436
  39.5 22.3 %collective-permute-start.10 = (f32[1,128]{1,0:T(1,128)S(1)}, f32[1,128]{1,0:T(1,128)S(1)}, u32[]{:S(2)}, u32[]{:S(2)}) collective-permute-start(f32[1,128]{1,0:T(1,128)S(1)} %add.149.count_ref), channel_id=1, source_target_pairs={{0,128},{32,160},{64,192},{96,224},{128,0},{160,32},{192,64},{224,... | collective-permute-start | bytes 1544 | tf_op jit(solution)/shard_map/ppermute | solution.py:221
  44.1 0.7 copy-start.26
  44.2 0.8 copy-start.27
  57.0 17.0 %collective-permute-start.11 = (bf16[256,512]{1,0:T(8,128)(2,1)}, bf16[256,512]{1,0:T(8,128)(2,1)S(1)}, u32[]{:S(2)}, u32[]{:S(2)}) collective-permute-start(bf16[256,512]{1,0:T(8,128)(2,1)} %get-tuple-element.58), channel_id=1, source_target_pairs={{0,3},{1,0},{2,1},{3,2},{4,7},{5,4},{6,5},{7,6},{8,11},{9,8},{10,9... | collective-permute-start | bytes 786440 | tf_op jit(solution)/shard_map/ppermute | solution.py:253
  59.7 15.0 %collective-permute-start.12 = (bf16[256,512]{1,0:T(8,128)(2,1)}, bf16[256,512]{1,0:T(8,128)(2,1)S(1)}, u32[]{:S(2)}, u32[]{:S(2)}) collective-permute-start(bf16[256,512]{1,0:T(8,128)(2,1)} %get-tuple-element.59), channel_id=1, source_target_pairs={{0,1},{1,2},{2,3},{3,0},{4,5},{5,6},{6,7},{7,4},{8,9},{9,10},{10,1... | collective-permute-start | bytes 786440 | tf_op jit(solution)/shard_map/ppermute | solution.py:253
  59.7 15.0 %collective-permute-start.13 = (bf16[256,512]{1,0:T(8,128)(2,1)}, bf16[256,512]{1,0:T(8,128)(2,1)S(1)}, u32[]{:S(2)}, u32[]{:S(2)}) collective-permute-start(bf16[256,512]{1,0:T(8,128)(2,1)} %get-tuple-element.60), channel_id=1, source_target_pairs={{0,2},{1,3},{2,0},{3,1},{4,6},{5,7},{6,4},{7,5},{8,10},{9,11},{10,... | collective-permute-start | bytes 786440 | tf_op jit(solution)/shard_map/ppermute | solution.py:253
  61.8 13.7 %copy-start.6 = (bf16[128,2048]{1,0:T(8,128)(2,1)S(1)}, bf16[128,2048]{1,0:T(8,128)(2,1)}, u32[]{:S(2)}) copy-start(bf16[128,2048]{1,0:T(8,128)(2,1)} %get-tuple-element.49) | copy-start | bytes 1572868
  74.7 10.2 %collective-permute-start.14 = (bf16[272,512]{1,0:T(8,128)(2,1)}, bf16[272,512]{1,0:T(8,128)(2,1)S(1)}, u32[]{:S(2)}, u32[]{:S(2)}) collective-permute-start(bf16[272,512]{1,0:T(8,128)(2,1)} %get-tuple-element.61), channel_id=1, source_target_pairs={{0,3},{1,0},{2,1},{3,2},{4,7},{5,4},{6,5},{7,6},{8,11},{9,8},{10,9... | collective-permute-start | bytes 835592 | tf_op jit(solution)/shard_map/ppermute | solution.py:253
  75.5 2.2 %copy-start.15 = (bf16[128,512]{1,0:T(8,128)(2,1)S(1)}, bf16[128,512]{1,0:T(8,128)(2,1)}, u32[]{:S(2)}) copy-start(bf16[128,512]{1,0:T(8,128)(2,1)} %get-tuple-element.70) | copy-start | bytes 393220
  75.5 2.2 %copy-start.16 = (bf16[128,512]{1,0:T(8,128)(2,1)S(1)}, bf16[128,512]{1,0:T(8,128)(2,1)}, u32[]{:S(2)}) copy-start(bf16[128,512]{1,0:T(8,128)(2,1)} %get-tuple-element.71) | copy-start | bytes 393220
  77.7 4.4 %copy-start.20 = (bf16[272,512]{1,0:T(8,128)(2,1)S(1)}, bf16[272,512]{1,0:T(8,128)(2,1)}, u32[]{:S(2)}) copy-start(bf16[272,512]{1,0:T(8,128)(2,1)} %get-tuple-element.62) | copy-start | bytes 835588
  77.7 5.7 %copy-start.19 = (bf16[272,512]{1,0:T(8,128)(2,1)S(1)}, bf16[272,512]{1,0:T(8,128)(2,1)}, u32[]{:S(2)}) copy-start(bf16[272,512]{1,0:T(8,128)(2,1)} %get-tuple-element.63) | copy-start | bytes 835588
  77.7 19.0 %copy-start.13 = (bf16[128,512]{1,0:T(8,128)(2,1)S(1)}, bf16[128,512]{1,0:T(8,128)(2,1)}, u32[]{:S(2)}) copy-start(bf16[128,512]{1,0:T(8,128)(2,1)} %get-tuple-element.68) | copy-start | bytes 393220
  77.7 19.0 %copy-start.14 = (bf16[128,512]{1,0:T(8,128)(2,1)S(1)}, bf16[128,512]{1,0:T(8,128)(2,1)}, u32[]{:S(2)}) copy-start(bf16[128,512]{1,0:T(8,128)(2,1)} %get-tuple-element.69) | copy-start | bytes 393220
  77.7 33.9 %copy-start.10 = (bf16[128,512]{1,0:T(8,128)(2,1)S(1)}, bf16[128,512]{1,0:T(8,128)(2,1)}, u32[]{:S(2)}) copy-start(bf16[128,512]{1,0:T(8,128)(2,1)} %get-tuple-element.64) | copy-start | bytes 393220
  77.9 19.7 %collective-permute-start.18 = (bf16[128,512]{1,0:T(8,128)(2,1)S(1)}, bf16[128,512]{1,0:T(8,128)(2,1)S(1)}, u32[]{:S(2)}, u32[]{:S(2)}) collective-permute-start(bf16[128,512]{1,0:T(8,128)(2,1)S(1)} %get-tuple-element.79), channel_id=1, source_target_pairs={{8,0},{9,1},{10,2},{11,3},{12,4},{13,5},{14,6},{15,7},{16,8},{17,9... | collective-permute-start | bytes 393224 | tf_op jit(solution)/shard_map/ppermute | solution.py:281
  79.9 17.7 %collective-permute-start.17 = (bf16[128,512]{1,0:T(8,128)(2,1)S(1)}, bf16[128,512]{1,0:T(8,128)(2,1)S(1)}, u32[]{:S(2)}, u32[]{:S(2)}) collective-permute-start(bf16[128,512]{1,0:T(8,128)(2,1)S(1)} %get-tuple-element.80), channel_id=1, source_target_pairs={{4,0},{5,1},{6,2},{7,3},{8,4},{9,5},{10,6},{11,7},{12,8},{13,9},{1... | collective-permute-start | bytes 393224 | tf_op jit(solution)/shard_map/ppermute | solution.py:281
  82.0 14.7 %collective-permute-start.15 = (bf16[272,512]{1,0:T(8,128)(2,1)S(1)}, bf16[272,512]{1,0:T(8,128)(2,1)S(1)}, u32[]{:S(2)}, u32[]{:S(2)}) collective-permute-start(bf16[272,512]{1,0:T(8,128)(2,1)S(1)} %copy-done.20), channel_id=1, source_target_pairs={{0,1},{1,2},{2,3},{3,0},{4,5},{5,6},{6,7},{7,4},{8,9},{9,10},{10,1... | collective-permute-start | bytes 835592 | tf_op jit(solution)/shard_map/ppermute | solution.py:253
  83.3 13.4 %collective-permute-start.16 = (bf16[272,512]{1,0:T(8,128)(2,1)S(1)}, bf16[272,512]{1,0:T(8,128)(2,1)S(1)}, u32[]{:S(2)}, u32[]{:S(2)}) collective-permute-start(bf16[272,512]{1,0:T(8,128)(2,1)S(1)} %copy-done.19), channel_id=1, source_target_pairs={{0,2},{1,3},{2,0},{3,1},{4,6},{5,7},{6,4},{7,5},{8,10},{9,11},{10,... | collective-permute-start | bytes 835592 | tf_op jit(solution)/shard_map/ppermute | solution.py:253
  96.7 1.0 copy-start.4
  96.7 1.0 copy-start.5
  96.7 18.8 %copy-start.2 = (f32[128,2048]{1,0:T(8,128)S(1)}, f32[128,2048]{1,0:T(8,128)}, u32[]{:S(2)}) copy-start(f32[128,2048]{1,0:T(8,128)} %get-tuple-element.52) | copy-start | bytes 3145732
  96.7 18.8 %copy-start.3 = (f32[128,2048]{1,0:T(8,128)S(1)}, f32[128,2048]{1,0:T(8,128)}, u32[]{:S(2)}) copy-start(f32[128,2048]{1,0:T(8,128)} %get-tuple-element.53) | copy-start | bytes 3145732
  97.6 0.7 copy-start.11
  97.6 0.7 copy-start.12
  98.9 13.8 %all-to-all-start = ((f32[8,1,256]{2,1,0:T(1,128)}), f32[8,1,256]{2,1,0:T(1,128)}, u32[]{:S(2)}, u32[]{:S(2)}) async-start(f32[8,1,256]{2,1,0:T(1,128)} %broadcast_in_dim.32), calls=%async_computation | async-start | bytes 16384 | tf_op jit(solution)/shard_map/all_to_all | solution.py:262
  106.7 10.0 %collective-permute-start.19 = (bf16[128,512]{1,0:T(8,128)(2,1)}, bf16[128,512]{1,0:T(8,128)(2,1)}, u32[]{:S(2)}, u32[]{:S(2)}) collective-permute-start(bf16[128,512]{1,0:T(8,128)(2,1)} %get-tuple-element.75), channel_id=1, source_target_pairs={{4,0},{5,1},{6,2},{7,3},{8,4},{9,5},{10,6},{11,7},{12,8},{13,9},{1... | collective-permute-start | bytes 393224 | tf_op jit(solution)/shard_map/ppermute | solution.py:281
  109.1 9.5 %collective-permute-start.20 = (bf16[128,512]{1,0:T(8,128)(2,1)}, bf16[128,512]{1,0:T(8,128)(2,1)}, u32[]{:S(2)}, u32[]{:S(2)}) collective-permute-start(bf16[128,512]{1,0:T(8,128)(2,1)} %get-tuple-element.76), channel_id=1, source_target_pairs={{8,0},{9,1},{10,2},{11,3},{12,4},{13,5},{14,6},{15,7},{16,8},{17,9... | collective-permute-start | bytes 393224 | tf_op jit(solution)/shard_map/ppermute | solution.py:281
  115.5 3.1 %copy-start.9 = (bf16[128,512]{1,0:T(8,128)(2,1)S(1)}, bf16[128,512]{1,0:T(8,128)(2,1)}, u32[]{:S(2)}) copy-start(bf16[128,512]{1,0:T(8,128)(2,1)} %get-tuple-element.74) | copy-start | bytes 393220

commit v4 on v3

--- a/solution.py
+++ b/solution.py
@@ -17,7 +17,6 @@
 PARTS = ((0, 2), (2, 2))
 MASKED = -1e30
 EXP2_SCALE = HD ** -0.5 * math.log2(math.e)
-EXTRA = 16
 STRIP = 64
 
 NT = (((1,), (1,)), ((), ()))
@@ -29,7 +28,7 @@
     return lax.dot_general(a, b, dims, preferred_element_type=jnp.float32)
 
 
-def attend_kernel(block_of, lengths, q_ref, c_ref, mask_ref, count_ref, loss_in, *refs):
+def attend_kernel(block_of, lengths, q_ref, c_ref, mask_ref, loss_in, *refs):
     n = len(ORDER)
     key_refs, value_refs = refs[:SLOTS], refs[SLOTS:2 * SLOTS]
     out_ref, dq_ref, loss_ref = refs[2 * SLOTS:2 * SLOTS + 3]
@@ -129,22 +128,9 @@
         at = slice(j * tok, (j + 1) * tok)
         grads[j][:, :HD] = dk[at, :]
         grads[j][:, HD:] = dv[at, :]
-    if pair_grads[0].shape[0] == 2 * tok:
-        return
-
-    high = loss_ref[...].astype(jnp.bfloat16).astype(jnp.float32)
-    middle = (loss_ref[...] - high).astype(jnp.bfloat16).astype(jnp.float32)
-    low = loss_ref[...] - high - middle
-    row_of = lax.broadcasted_iota(jnp.int32, (EXTRA, tok), 0)
-    extra = jnp.zeros((EXTRA, tok), jnp.float32)
-    for i, row in enumerate([high, middle, low, count_ref[...]]):
-        extra = jnp.where(row_of == i, row, extra)
-    for ref in pair_grads:
-        ref[2 * tok:, :HD] = extra.astype(jnp.bfloat16)
-        ref[2 * tok:, HD:] = extra.astype(jnp.bfloat16)
-
-
-def attend(part, block_of, lengths, queries, cotangent, mask, counts, loss, blocks):
+
+
+def attend(part, block_of, lengths, queries, cotangent, mask, loss, blocks):
     first_head, heads = part
     tok = queries.shape[0]
     kv_heads = blocks[0].shape[1] // (2 * HD)
@@ -159,7 +145,7 @@
     key = pl.BlockSpec((tok, HD), lambda g: (0, first_head + g))
     value = pl.BlockSpec((tok, HD), lambda g: (0, kv_heads + first_head + g))
     single = pl.BlockSpec((tok, 2 * HD), lambda g: (0, g))
-    pair_rows = 2 * tok + (EXTRA if part is PARTS[-1] else 0)
+    pair_rows = 2 * tok
     pair = pl.BlockSpec((pair_rows, 2 * HD), lambda g: (0, g))
     halo = [key] * SLOTS + [value] * SLOTS
     grads = [pltpu.HBM((tok, heads * 2 * HD), bf16)] * 3
@@ -174,7 +160,7 @@
             jax.ShapeDtypeStruct((1, tok), f32),
             *grads,
         ),
-        in_specs=[smem, smem, wide_in, wide_in, row, row, row, *halo],
+        in_specs=[smem, smem, wide_in, wide_in, row, row, *halo],
         out_specs=(wide_out, wide_out, row, *[single] * 3, *[pair] * n),
         scratch_shapes=[
             pltpu.VMEM((rows, tok), f32),
@@ -189,7 +175,7 @@
         cost_estimate=pl.CostEstimate(
             flops=2 * work, bytes_accessed=8 * 2**20, transcendentals=work // (12 * HD)
         ),
-    )(block_of, lengths, queries, cotangent, mask, counts, loss, *blocks, *blocks)
+    )(block_of, lengths, queries, cotangent, mask, loss, *blocks, *blocks)
     return result[0], result[1], result[2], result[3:6], result[6:]
 
 
@@ -232,7 +218,7 @@
         for step in ORDER
     ]
     counts, mixed_got[-1] = lax.optimization_barrier((counts, mixed_got[-1]))
-    all_counts = swap(counts, "dp", 4)
+    counts = swap(counts, "dp", 4)
 
     in_hbm = functools.partial(pltpu.with_memory_space_constraint, memory_space=pltpu.HBM)
     blocks = [in_hbm(a) for a in (own, near, far, *mixed_got, *near_got)]
@@ -240,9 +226,8 @@
     outs, dqs, sums, backs = [], [], [], []
     loss = jnp.zeros((1, tok), jnp.float32)
     for part in PARTS:
-        counts = all_counts if part is PARTS[-1] else counts
         out, dq, loss, dsingle, dpair = attend(
-            part, block_of, lengths, queries_in, cotangent_in, loss_mask, counts, loss, blocks
+            part, block_of, lengths, queries_in, cotangent_in, loss_mask, loss, blocks
         )
         if backs:
             *dpair, backs[-1] = lax.optimization_barrier((*dpair, backs[-1]))
@@ -252,20 +237,16 @@
         backs.append([
             lax.ppermute(d, "seq", around(-step)) for step, d in zip(ORDER, dpair)
         ])
-    last = 2 * HD * (PARTS[-1][1] - 1)
-    terms = jnp.concatenate([counts, loss], axis=0)
-    for b in backs[-1]:
-        extra = b[2 * tok:2 * tok + 4, last:last + HD].astype(jnp.float32)
-        terms = terms + jnp.stack([extra[3], extra[0] + extra[1] + extra[2]])
-    columns = [[RING * z + i for z in range(seq_count // RING)] for i in range(RING)]
-    terms = jnp.broadcast_to(terms.reshape(1, 2 * tok), (seq_count // RING, 2 * tok))
-    terms = lax.all_to_all(terms, "seq", 0, 0, axis_index_groups=columns, tiled=True)
-    terms = jnp.sum(terms, axis=0).reshape(2, tok)
-    terms = jnp.sum(terms, axis=1)
-    grad_scale = jnp.float32(dp_count * seq_count * tok) / terms[0]
-    factor = grad_scale * HD ** -0.5
-    row_loss = (grad_scale * terms[1] / (seq_count * tok)).reshape(1)
-
+    def total_of(terms, groups):
+        copies = jnp.broadcast_to(terms[None], (len(groups[0]), terms.size))
+        parts = lax.all_to_all(copies, "seq", 0, 0, axis_index_groups=groups, tiled=True)
+        return jnp.sum(parts, axis=0)
+
+    rows = [[RING * z + i for i in range(RING)] for z in range(seq_count // RING)]
+    columns = [list(c) for c in zip(*rows)]
+    terms = jnp.concatenate([counts[0], loss[0]])
+    terms, backs[-1][0] = lax.optimization_barrier((terms, backs[-1][0]))
+    terms = total_of(terms, columns)
     grad_k, grad_v, totals, before = [], [], [], []
     for part, single, back in zip(PARTS, sums, backs):
         own_sum, near_sum, far_sum = [s.astype(jnp.float32) for s in single]
@@ -280,6 +261,11 @@
             totals[-1] = totals[-1] + before[0].astype(jnp.float32) + before[1].astype(jnp.float32)
         before = [lax.ppermute(near_sum, "seq", up(RING)), lax.ppermute(far_sum, "seq", up(2 * RING))]
         totals.append(own_sum)
+    terms, before[0] = lax.optimization_barrier((terms, before[0]))
+    terms = total_of(terms, rows)
+    grad_scale = jnp.float32(dp_count * seq_count * tok) / jnp.sum(terms[:tok])
+    factor = grad_scale * HD ** -0.5
+    row_loss = (grad_scale * jnp.sum(terms[tok:]) / (seq_count * tok)).reshape(1)
     totals[-1] = totals[-1] + before[0].astype(jnp.float32) + before[1].astype(jnp.float32)
     for part, total in zip(PARTS, totals):
         for h in range(part[1]):

time: 124 us -> 122 us (0.984)
  waiting for transfers between devices: 34.4 us -> 28.3 us
  starting transfers between devices: 44.9 us -> 50.6 us
    ppermute x6, waiting for transfers between devices: 12.4 us -> 0.87 us  [per_device(): lax.ppermute(d, 'seq', around(-step))]
    all_to_all x1 -> x2, starting transfers between devices: 7.75 us -> 13.1 us  [total_of(): lax.all_to_all(copies, 'seq', 0, 0, axis_index_groups=groups, tiled=True)]
    all_to_all x1 -> x2, waiting for transfers between devices: 0.01 us -> 4.19 us  [total_of(): lax.all_to_all(copies, 'seq', 0, 0, axis_index_groups=groups, tiled=True)]
    ppermute x2, waiting for transfers between devices: 0.01 us -> 3.17 us  [per_device(): lax.ppermute(near_sum, 'seq', up(RING))]
    ppermute x2, waiting for transfers between devices: 1.92 us -> 0.01 us  [per_device(): lax.ppermute(far_sum, 'seq', up(2 * RING))]
  transfers between devices with their start and end apart: 22 -> 23, of which waited for: 11 -> 11; matrix products, arithmetic and copies ran while one was open for 7% -> 6% of each run, Pallas kernels for 20% -> 20%
where the time goes in v4:
time: 122 us; the launch traced here: 119 us
  starting transfers between devices  50.6 us (41%)
  waiting for transfers between devices  28.3 us (23%)
  Pallas kernels  24.2 us (20%)
  other arithmetic  10.7 us (9%)
  between operations  3.55 us (3%)
  local copies, waits for them, and re-layouts  2.1 us (2%)
    pallas_call x2, Pallas kernels, attend(): pl.pallas_call(attend_kernel, grid=(heads,), out_shape=(pltpu.HBM((tok, h...  24.2 us
    all_to_all x2, starting transfers between devices, total_of(): lax.all_to_all(copies, 'seq', 0, 0, axis_index_groups=groups, tiled=True)  13.1 us
    ppermute x6, starting transfers between devices, per_device(): lax.ppermute(d, 'seq', around(-step))  9.04 us
    ppermute x3, waiting for transfers between devices, per_device(): near_got = [lax.ppermute(near, 'seq', around(step)) for step in ORDER]  7.45 us
    ppermute x3, waiting for transfers between devices, per_device(): lax.ppermute(jnp.where(x + step >= RING, far, own), 'seq', around(step))  7.25 us
    ppermute x3, starting transfers between devices, per_device(): near_got = [lax.ppermute(near, 'seq', around(step)) for step in ORDER]  5.05 us
    ppermute x3, starting transfers between devices, per_device(): lax.ppermute(jnp.where(x + step >= RING, far, own), 'seq', around(step))  4.91 us
    ppermute x3, starting transfers between devices, swap(): lax.ppermute(a, axis, [(i, i ^ bit) for i in range(lax.axis_size(axis))])  4.77 us
  transfers between devices with their start and end apart: 23, of which 11 were waited for; matrix products, arithmetic and copies ran while one was open for 6% of the time, Pallas kernels for 20%

profile of v4, /device:TPU:128, one launch (start us, length us, event | category | flops | bytes accessed | tf_op | source)
XLA Modules:
  0.0 119.5 jit_solution(4881713389432178751)
XLA Ops:
  0.6 0.0 copy-start.13
  0.6 0.0 copy-start.14
  0.7 0.0 copy-start.1
  0.7 1.0 pad_maximum_fusion.refs_0_.refs_9_
  1.7 2.9 %collective-permute-start = (bf16[128,1024]{1,0:T(8,128)(2,1)S(1)}, bf16[128,1024]{1,0:T(8,128)(2,1)S(1)}, u32[]{:S(2)}, u32[]{:S(2)}) collective-permute-start(bf16[128,1024]{1,0:T(8,128)(2,1)S(1)} %pad_maximum_fusion.refs_0_.refs_9_), channel_id=1, source_target_pairs={{0,4},{1,5},{2,6},{3,7},{4,8},{5,9},{6,10},{7,11},{8,12},{9,13},{1... | collective-permute-start | bytes 786440 | tf_op jit(solution)/shard_map/ppermute | solution.py:210
  4.6 0.7 convert_element_type.107
  5.3 0.0 collective-permute-start.1
  5.3 1.1 collective-permute-done.1
  6.4 0.7 convert_add_fusion
  7.1 1.6 %collective-permute-start.2 = (f32[1,128]{1,0:T(1,128)S(1)}, f32[1,128]{1,0:T(1,128)S(1)}, u32[]{:S(2)}, u32[]{:S(2)}) collective-permute-start(f32[1,128]{1,0:T(1,128)S(1)} %convert_add_fusion), channel_id=1, source_target_pairs={{0,64},{32,96},{64,0},{96,32},{128,192},{160,224},{192,128},{224,1... | collective-permute-start | bytes 1544 | tf_op jit(solution)/shard_map/ppermute | solution.py:207
  8.7 2.0 %collective-permute-done.2 = f32[1,128]{1,0:T(1,128)S(1)} collective-permute-done((f32[1,128]{1,0:T(1,128)S(1)}, f32[1,128]{1,0:T(1,128)S(1)}, u32[]{:S(2)}, u32[]{:S(2)}) %collective-permute-start.2) | collective-permute-done | bytes 544 | tf_op jit(solution)/shard_map/ppermute | solution.py:207
  10.6 2.2 %collective-permute-done.refs_1_.refs_10_ = bf16[128,1024]{1,0:T(8,128)(2,1)S(1)} collective-permute-done((bf16[128,1024]{1,0:T(8,128)(2,1)S(1)}, bf16[128,1024]{1,0:T(8,128)(2,1)S(1)}, u32[]{:S(2)}, u32[]{:S(2)}) %collective-permute-start) | collective-permute-done | bytes 262176 | tf_op jit(solution)/shard_map/ppermute | solution.py:210
  12.9 3.0 %collective-permute-start.6 = (bf16[128,1024]{1,0:T(8,128)(2,1)S(1)}, bf16[128,1024]{1,0:T(8,128)(2,1)S(1)}, u32[]{:S(2)}, u32[]{:S(2)}) collective-permute-start(bf16[128,1024]{1,0:T(8,128)(2,1)S(1)} %collective-permute-done.refs_1_.refs_10_), channel_id=1, source_target_pairs={{0,2},{1,3},{2,0},{3,1},{4,6},{5,7},{6,4},{7,5},{8,10},{9,11},{10,... | collective-permute-start | bytes 786440 | tf_op jit(solution)/shard_map/ppermute | solution.py:214
  15.9 1.1 collective-permute-start.5
  17.0 0.9 collective-permute-start.4
  17.9 1.9 %collective-permute-start.3 = (bf16[128,1024]{1,0:T(8,128)(2,1)S(1)}, bf16[128,1024]{1,0:T(8,128)(2,1)S(1)}, u32[]{:S(2)}, u32[]{:S(2)}) collective-permute-start(bf16[128,1024]{1,0:T(8,128)(2,1)S(1)} %collective-permute-done.refs_1_.refs_10_), channel_id=1, source_target_pairs={{0,4},{1,5},{2,6},{3,7},{4,8},{5,9},{6,10},{7,11},{8,12},{9,13},{1... | collective-permute-start | bytes 786440 | tf_op jit(solution)/shard_map/ppermute | solution.py:213
  19.8 3.8 %collective-permute-done.6.refs_8_.refs_17_ = bf16[128,1024]{1,0:T(8,128)(2,1)S(1)} collective-permute-done((bf16[128,1024]{1,0:T(8,128)(2,1)S(1)}, bf16[128,1024]{1,0:T(8,128)(2,1)S(1)}, u32[]{:S(2)}, u32[]{:S(2)}) %collective-permute-start.6) | collective-permute-done | bytes 262176 | tf_op jit(solution)/shard_map/ppermute | solution.py:214
  23.6 3.7 %collective-permute-done.5.refs_7_.refs_16_ = bf16[128,1024]{1,0:T(8,128)(2,1)S(1)} collective-permute-done((bf16[128,1024]{1,0:T(8,128)(2,1)S(1)}, bf16[128,1024]{1,0:T(8,128)(2,1)S(1)}, u32[]{:S(2)}, u32[]{:S(2)}) %collective-permute-start.5) | collective-permute-done | bytes 262176 | tf_op jit(solution)/shard_map/ppermute | solution.py:214
  27.3 0.0 collective-permute-done.4.refs_6_.refs_15_
  27.3 0.1 collective-permute-done.3.refs_2_.refs_11_
  27.4 1.3 %broadcast_select_fusion = (bf16[128,1024]{1,0:T(8,128)(2,1)S(1)}, bf16[128,1024]{1,0:T(8,128)(2,1)S(1)}, bf16[128,1024]{1,0:T(8,128)(2,1)S(1)}) fusion(bf16[128,1024]{1,0:T(8,128)(2,1)S(1)} %collective-permute-done.3.refs_2_.refs_11_, pred[]{:T(512)S(6)} %ge.19, bf16[128,512]{1,0:T(8,128)(2,1)} %bitcast.35, bf16[128,512]{1,0:T(8,128)(2,1)} %bitcast.37, ...), kind=kLoop, calls=%fused_computation.36 | loop fusion | flops 917504 | bytes 1310723 | tf_op jit(solution)/shard_map/jit(_where)/select_n | solution.py:217
  28.7 2.9 %collective-permute-start.9 = (bf16[128,1024]{1,0:T(8,128)(2,1)S(1)}, bf16[128,1024]{1,0:T(8,128)(2,1)S(1)}, u32[]{:S(2)}, u32[]{:S(2)}) collective-permute-start(bf16[128,1024]{1,0:T(8,128)(2,1)S(1)} %get-tuple-element.91), channel_id=1, source_target_pairs={{0,2},{1,3},{2,0},{3,1},{4,6},{5,7},{6,4},{7,5},{8,10},{9,11},{10,... | collective-permute-start | bytes 786440 | tf_op jit(solution)/shard_map/ppermute | solution.py:217
  31.6 1.2 %collective-permute-start.8 = (bf16[128,1024]{1,0:T(8,128)(2,1)S(1)}, bf16[128,1024]{1,0:T(8,128)(2,1)S(1)}, u32[]{:S(2)}, u32[]{:S(2)}) collective-permute-start(bf16[128,1024]{1,0:T(8,128)(2,1)S(1)} %get-tuple-element.92), channel_id=1, source_target_pairs={{0,3},{1,0},{2,1},{3,2},{4,7},{5,4},{6,5},{7,6},{8,11},{9,8},{10,9... | collective-permute-start | bytes 786440 | tf_op jit(solution)/shard_map/ppermute | solution.py:217
  32.8 0.8 collective-permute-start.7
  33.6 0.1 concatenate.64.block_of
  33.7 5.8 %collective-permute-done.9.refs_5_.refs_14_ = bf16[128,1024]{1,0:T(8,128)(2,1)S(1)} collective-permute-done((bf16[128,1024]{1,0:T(8,128)(2,1)S(1)}, bf16[128,1024]{1,0:T(8,128)(2,1)S(1)}, u32[]{:S(2)}, u32[]{:S(2)}) %collective-permute-start.9) | collective-permute-done | bytes 262176 | tf_op jit(solution)/shard_map/ppermute | solution.py:217
  39.5 3.2 %collective-permute-start.10 = (f32[1,128]{1,0:T(1,128)S(1)}, f32[1,128]{1,0:T(1,128)S(1)}, u32[]{:S(2)}, u32[]{:S(2)}) collective-permute-start(f32[1,128]{1,0:T(1,128)S(1)} %add.99), channel_id=1, source_target_pairs={{0,128},{32,160},{64,192},{96,224},{128,0},{160,32},{192,64},{224,... | collective-permute-start | bytes 1544 | tf_op jit(solution)/shard_map/ppermute | solution.py:207
  42.7 1.4 %collective-permute-done.8.refs_4_.refs_13_ = bf16[128,1024]{1,0:T(8,128)(2,1)S(1)} collective-permute-done((bf16[128,1024]{1,0:T(8,128)(2,1)S(1)}, bf16[128,1024]{1,0:T(8,128)(2,1)S(1)}, u32[]{:S(2)}, u32[]{:S(2)}) %collective-permute-start.8) | collective-permute-done | bytes 262176 | tf_op jit(solution)/shard_map/ppermute | solution.py:217
  44.2 0.6 copy-done.20
  44.8 0.1 copy-done.21
  45.0 12.1 %shard_map.110 = (bf16[128,2048]{1,0:T(8,128)(2,1)}, f32[128,2048]{1,0:T(8,128)}, f32[1,128]{1,0:T(1,128)S(1)}, bf16[128,512]{1,0:T(8,128)(2,1)}, bf16[128,512]{...) custom-call(s32[9]{0:T(128)S(1)} %concatenate.64.block_of, ...), custom_call_target="tpu_custom_call" | custom-call | flops 7247757312 | bytes 8388608 | tf_op jit(solution)/shard_map/pallas_call | solution.py:154
  57.0 2.7 %collective-permute-start.11 = (bf16[256,512]{1,0:T(8,128)(2,1)}, bf16[256,512]{1,0:T(8,128)(2,1)S(1)}, u32[]{:S(2)}, u32[]{:S(2)}) collective-permute-start(bf16[256,512]{1,0:T(8,128)(2,1)} %get-tuple-element.62), channel_id=1, source_target_pairs={{0,3},{1,0},{2,1},{3,2},{4,7},{5,4},{6,5},{7,6},{8,11},{9,8},{10,9... | collective-permute-start | bytes 786440 | tf_op jit(solution)/shard_map/ppermute | solution.py:238
  59.7 0.0 collective-permute-start.12
  59.7 2.1 %collective-permute-start.13 = (bf16[256,512]{1,0:T(8,128)(2,1)}, bf16[256,512]{1,0:T(8,128)(2,1)S(1)}, u32[]{:S(2)}, u32[]{:S(2)}) collective-permute-start(bf16[256,512]{1,0:T(8,128)(2,1)} %get-tuple-element.64), channel_id=1, source_target_pairs={{0,2},{1,3},{2,0},{3,1},{4,6},{5,7},{6,4},{7,5},{8,10},{9,11},{10,... | collective-permute-start | bytes 786440 | tf_op jit(solution)/shard_map/ppermute | solution.py:238
  61.8 12.2 %shard_map.111 = (bf16[128,2048]{1,0:T(8,128)(2,1)}, f32[128,2048]{1,0:T(8,128)}, f32[1,128]{1,0:T(1,128)S(1)}, bf16[128,512]{1,0:T(8,128)(2,1)}, bf16[128,512]{...) custom-call(s32[9]{0:T(128)S(1)} %concatenate.64.block_of, ...), custom_call_target="tpu_custom_call" | custom-call | flops 7247757312 | bytes 8388608 | tf_op jit(solution)/shard_map/pallas_call | solution.py:154
  74.0 0.0 copy-start.11
  74.1 2.2 %maximum_bitcast_fusion = bf16[1,128,4096]{2,1,0:T(8,128)(2,1)} fusion(bf16[128,2048]{1,0:T(8,128)(2,1)} %get-tuple-element.54, bf16[128,2048]{1,0:T(8,128)(2,1)S(1)} %copy-done.4), kind=kLoop, calls=%fused_computation.2 | loop fusion | flops 2097152 | bytes 2097152 | tf_op jit(solution)/shard_map/broadcast_in_dim | solution.py:278
  76.2 0.0 collective-permute-done.10
  76.3 0.0 collective-permute-done.13
  76.3 1.4 %collective-permute-start.14 = (bf16[256,512]{1,0:T(8,128)(2,1)S(1)}, bf16[256,512]{1,0:T(8,128)(2,1)S(1)}, u32[]{:S(2)}, u32[]{:S(2)}) collective-permute-start(bf16[256,512]{1,0:T(8,128)(2,1)S(1)} %copy-done.24), channel_id=1, source_target_pairs={{0,3},{1,0},{2,1},{3,2},{4,7},{5,4},{6,5},{7,6},{8,11},{9,8},{10,9... | collective-permute-start | bytes 786440 | tf_op jit(solution)/shard_map/ppermute | solution.py:238
  77.7 0.8 collective-permute-start.15
  78.5 2.1 %collective-permute-start.16 = (bf16[256,512]{1,0:T(8,128)(2,1)S(1)}, bf16[256,512]{1,0:T(8,128)(2,1)S(1)}, u32[]{:S(2)}, u32[]{:S(2)}) collective-permute-start(bf16[256,512]{1,0:T(8,128)(2,1)S(1)} %copy-done.22), channel_id=1, source_target_pairs={{0,2},{1,3},{2,0},{3,1},{4,6},{5,7},{6,4},{7,5},{8,10},{9,11},{10,... | collective-permute-start | bytes 786440 | tf_op jit(solution)/shard_map/ppermute | solution.py:238
  80.6 0.0 copy-start.8
  80.6 0.2 fusion.13
  80.7 1.9 %collective-permute-start.18 = (bf16[128,512]{1,0:T(8,128)(2,1)S(1)}, bf16[128,512]{1,0:T(8,128)(2,1)S(1)}, u32[]{:S(2)}, u32[]{:S(2)}) collective-permute-start(bf16[128,512]{1,0:T(8,128)(2,1)S(1)} %get-tuple-element.87), channel_id=1, source_target_pairs={{8,0},{9,1},{10,2},{11,3},{12,4},{13,5},{14,6},{15,7},{16,8},{17,9... | collective-permute-start | bytes 393224 | tf_op jit(solution)/shard_map/ppermute | solution.py:262
  82.7 2.1 %collective-permute-start.17 = (bf16[128,512]{1,0:T(8,128)(2,1)S(1)}, bf16[128,512]{1,0:T(8,128)(2,1)S(1)}, u32[]{:S(2)}, u32[]{:S(2)}) collective-permute-start(bf16[128,512]{1,0:T(8,128)(2,1)S(1)} %get-tuple-element.88), channel_id=1, source_target_pairs={{4,0},{5,1},{6,2},{7,3},{8,4},{9,5},{10,6},{11,7},{12,8},{13,9},{1... | collective-permute-start | bytes 393224 | tf_op jit(solution)/shard_map/ppermute | solution.py:262
  84.8 0.9 collective-permute-done.14
  85.6 0.6 broadcast_in_dim.39
  86.2 7.3 %all-to-all-start = ((f32[8,1,256]{2,1,0:T(1,128)}), f32[8,1,256]{2,1,0:T(1,128)S(1)}, u32[]{:S(2)}, u32[]{:S(2)}) async-start(f32[8,1,256]{2,1,0:T(1,128)} %broadcast_in_dim.39), calls=%async_computation | async-start | bytes 16384 | tf_op jit(solution)/shard_map/all_to_all | solution.py:242
  93.6 0.9 fusion.4
  94.4 2.5 %collective-permute-start.19 = (bf16[128,512]{1,0:T(8,128)(2,1)}, bf16[128,512]{1,0:T(8,128)(2,1)}, u32[]{:S(2)}, u32[]{:S(2)}) collective-permute-start(bf16[128,512]{1,0:T(8,128)(2,1)} %get-tuple-element.77), channel_id=1, source_target_pairs={{4,0},{5,1},{6,2},{7,3},{8,4},{9,5},{10,6},{11,7},{12,8},{13,9},{1... | collective-permute-start | bytes 393224 | tf_op jit(solution)/shard_map/ppermute | solution.py:262
  96.9 2.5 %collective-permute-start.20 = (bf16[128,512]{1,0:T(8,128)(2,1)}, bf16[128,512]{1,0:T(8,128)(2,1)}, u32[]{:S(2)}, u32[]{:S(2)}) collective-permute-start(bf16[128,512]{1,0:T(8,128)(2,1)} %get-tuple-element.84), channel_id=1, source_target_pairs={{8,0},{9,1},{10,2},{11,3},{12,4},{13,5},{14,6},{15,7},{16,8},{17,9... | collective-permute-start | bytes 393224 | tf_op jit(solution)/shard_map/ppermute | solution.py:262
  99.4 0.1 fusion.18
  99.5 0.0 copy-start.2
  99.6 0.0 all-to-all-done
  99.6 3.2 %collective-permute-done.19 = bf16[128,512]{1,0:T(8,128)(2,1)} collective-permute-done((bf16[128,512]{1,0:T(8,128)(2,1)}, bf16[128,512]{1,0:T(8,128)(2,1)}, u32[]{:S(2)}, u32[]{:S(2)}) %collective-permute-start.19) | collective-permute-done | bytes 131104 | tf_op jit(solution)/shard_map/ppermute | solution.py:262
  102.8 0.6 broadcast_in_dim.41
  103.4 5.8 %all-to-all-start.1 = ((f32[4,1,256]{2,1,0:T(1,128)}), f32[4,1,256]{2,1,0:T(1,128)S(1)}, u32[]{:S(2)}, u32[]{:S(2)}) async-start(f32[4,1,256]{2,1,0:T(1,128)} %broadcast_in_dim.41), calls=%async_computation.1 | async-start | bytes 8192 | tf_op jit(solution)/shard_map/all_to_all | solution.py:242
  109.1 0.0 collective-permute-done.20
  109.1 1.1 fusion.9
  110.2 4.2 %all-to-all-done.1 = f32[4,1,256]{2,1,0:T(1,128)S(1)} async-done(((f32[4,1,256]{2,1,0:T(1,128)}), f32[4,1,256]{2,1,0:T(1,128)S(1)}, u32[]{:S(2)}, u32[]{:S(2)}) %all-to-all-start.1) | async-done | bytes 4128 | tf_op jit(solution)/shard_map/all_to_all | solution.py:242
  114.4 0.6 slice_reduce_fusion
  116.5 1.1 fusion
  117.6 0.7 pad_maximum_fusion.1
  (58 shorter events, 0.2 us)
Async XLA Ops:
  0.6 33.0 %copy-start.13 = (s32[3]{0:T(128)S(1)}, s32[3]{0:T(128)}, u32[]{:S(2)}) copy-start(s32[3]{0:T(128)} %constant.39) | copy-start | bytes 40
  0.6 33.0 %copy-start.14 = (s32[3]{0:T(128)S(1)}, s32[3]{0:T(128)}, u32[]{:S(2)}) copy-start(s32[3]{0:T(128)} %constant.32.clone) | copy-start | bytes 40
  0.7 44.3 %copy-start.1 = (s32[1,128]{1,0:T(1,128)S(1)}, s32[1,128]{1,0:T(1,128)}, u32[]{:S(2)}) copy-start(s32[1,128]{1,0:T(1,128)} %mask_ref.3) | copy-start | bytes 1540
  0.7 44.3 %copy-start = (s32[1,16]{1,0:T(1,128)S(1)}, s32[1,16]{1,0:T(1,128)}, u32[]{:S(2)}) copy-start(s32[1,16]{1,0:T(1,128)} %lengths.3) | copy-start | bytes 196
  1.7 42.5 %copy-start.5 = (bf16[128,1024]{1,0:T(8,128)(2,1)}, bf16[128,1024]{1,0:T(8,128)(2,1)S(1)}, u32[]{:S(2)}) copy-start(bf16[128,1024]{1,0:T(8,128)(2,1)S(1)} %pad_maximum_fusion.refs_0_.refs_9_) | copy-start | bytes 786436
  1.7 11.2 %collective-permute-start = (bf16[128,1024]{1,0:T(8,128)(2,1)S(1)}, bf16[128,1024]{1,0:T(8,128)(2,1)S(1)}, u32[]{:S(2)}, u32[]{:S(2)}) collective-permute-start(bf16[128,1024]{1,0:T(8,128)(2,1)S(1)} %pad_maximum_fusion.refs_0_.refs_9_), channel_id=1, source_target_pairs={{0,4},{1,5},{2,6},{3,7},{4,8},{5,9},{6,10},{7,11},{8,12},{9,13},{1... | collective-permute-start | bytes 786440 | tf_op jit(solution)/shard_map/ppermute | solution.py:210
  5.3 1.1 collective-permute-start.1
  7.1 3.5 %collective-permute-start.2 = (f32[1,128]{1,0:T(1,128)S(1)}, f32[1,128]{1,0:T(1,128)S(1)}, u32[]{:S(2)}, u32[]{:S(2)}) collective-permute-start(f32[1,128]{1,0:T(1,128)S(1)} %convert_add_fusion), channel_id=1, source_target_pairs={{0,64},{32,96},{64,0},{96,32},{128,192},{160,224},{192,128},{224,1... | collective-permute-start | bytes 1544 | tf_op jit(solution)/shard_map/ppermute | solution.py:207
  12.9 31.3 %copy-start.15 = (bf16[128,1024]{1,0:T(8,128)(2,1)}, bf16[128,1024]{1,0:T(8,128)(2,1)S(1)}, u32[]{:S(2)}) copy-start(bf16[128,1024]{1,0:T(8,128)(2,1)S(1)} %collective-permute-done.refs_1_.refs_10_) | copy-start | bytes 786436
  12.9 10.7 %collective-permute-start.6 = (bf16[128,1024]{1,0:T(8,128)(2,1)S(1)}, bf16[128,1024]{1,0:T(8,128)(2,1)S(1)}, u32[]{:S(2)}, u32[]{:S(2)}) collective-permute-start(bf16[128,1024]{1,0:T(8,128)(2,1)S(1)} %collective-permute-done.refs_1_.refs_10_), channel_id=1, source_target_pairs={{0,2},{1,3},{2,0},{3,1},{4,6},{5,7},{6,4},{7,5},{8,10},{9,11},{10,... | collective-permute-start | bytes 786440 | tf_op jit(solution)/shard_map/ppermute | solution.py:214
  15.9 11.4 %collective-permute-start.5 = (bf16[128,1024]{1,0:T(8,128)(2,1)S(1)}, bf16[128,1024]{1,0:T(8,128)(2,1)S(1)}, u32[]{:S(2)}, u32[]{:S(2)}) collective-permute-start(bf16[128,1024]{1,0:T(8,128)(2,1)S(1)} %collective-permute-done.refs_1_.refs_10_), channel_id=1, source_target_pairs={{0,3},{1,0},{2,1},{3,2},{4,7},{5,4},{6,5},{7,6},{8,11},{9,8},{10,9... | collective-permute-start | bytes 786440 | tf_op jit(solution)/shard_map/ppermute | solution.py:214
  17.0 10.3 %collective-permute-start.4 = (bf16[128,1024]{1,0:T(8,128)(2,1)S(1)}, bf16[128,1024]{1,0:T(8,128)(2,1)S(1)}, u32[]{:S(2)}, u32[]{:S(2)}) collective-permute-start(bf16[128,1024]{1,0:T(8,128)(2,1)S(1)} %collective-permute-done.refs_1_.refs_10_), channel_id=1, source_target_pairs={{0,1},{1,2},{2,3},{3,0},{4,5},{5,6},{6,7},{7,4},{8,9},{9,10},{10,1... | collective-permute-start | bytes 786440 | tf_op jit(solution)/shard_map/ppermute | solution.py:214
  17.9 9.5 %collective-permute-start.3 = (bf16[128,1024]{1,0:T(8,128)(2,1)S(1)}, bf16[128,1024]{1,0:T(8,128)(2,1)S(1)}, u32[]{:S(2)}, u32[]{:S(2)}) collective-permute-start(bf16[128,1024]{1,0:T(8,128)(2,1)S(1)} %collective-permute-done.refs_1_.refs_10_), channel_id=1, source_target_pairs={{0,4},{1,5},{2,6},{3,7},{4,8},{5,9},{6,10},{7,11},{8,12},{9,13},{1... | collective-permute-start | bytes 786440 | tf_op jit(solution)/shard_map/ppermute | solution.py:213
  23.6 20.6 %copy-start.16 = (bf16[128,1024]{1,0:T(8,128)(2,1)}, bf16[128,1024]{1,0:T(8,128)(2,1)S(1)}, u32[]{:S(2)}) copy-start(bf16[128,1024]{1,0:T(8,128)(2,1)S(1)} %collective-permute-done.6.refs_8_.refs_17_) | copy-start | bytes 786436
  27.3 16.9 %copy-start.17 = (bf16[128,1024]{1,0:T(8,128)(2,1)}, bf16[128,1024]{1,0:T(8,128)(2,1)S(1)}, u32[]{:S(2)}) copy-start(bf16[128,1024]{1,0:T(8,128)(2,1)S(1)} %collective-permute-done.5.refs_7_.refs_16_) | copy-start | bytes 786436
  27.3 16.9 %copy-start.18 = (bf16[128,1024]{1,0:T(8,128)(2,1)}, bf16[128,1024]{1,0:T(8,128)(2,1)S(1)}, u32[]{:S(2)}) copy-start(bf16[128,1024]{1,0:T(8,128)(2,1)S(1)} %collective-permute-done.4.refs_6_.refs_15_) | copy-start | bytes 786436
  27.4 16.8 %copy-start.6 = (bf16[128,1024]{1,0:T(8,128)(2,1)}, bf16[128,1024]{1,0:T(8,128)(2,1)S(1)}, u32[]{:S(2)}) copy-start(bf16[128,1024]{1,0:T(8,128)(2,1)S(1)} %collective-permute-done.3.refs_2_.refs_11_) | copy-start | bytes 786436
  28.7 10.8 %collective-permute-start.9 = (bf16[128,1024]{1,0:T(8,128)(2,1)S(1)}, bf16[128,1024]{1,0:T(8,128)(2,1)S(1)}, u32[]{:S(2)}, u32[]{:S(2)}) collective-permute-start(bf16[128,1024]{1,0:T(8,128)(2,1)S(1)} %get-tuple-element.91), channel_id=1, source_target_pairs={{0,2},{1,3},{2,0},{3,1},{4,6},{5,7},{6,4},{7,5},{8,10},{9,11},{10,... | collective-permute-start | bytes 786440 | tf_op jit(solution)/shard_map/ppermute | solution.py:217
  31.6 12.6 %collective-permute-start.8 = (bf16[128,1024]{1,0:T(8,128)(2,1)S(1)}, bf16[128,1024]{1,0:T(8,128)(2,1)S(1)}, u32[]{:S(2)}, u32[]{:S(2)}) collective-permute-start(bf16[128,1024]{1,0:T(8,128)(2,1)S(1)} %get-tuple-element.92), channel_id=1, source_target_pairs={{0,3},{1,0},{2,1},{3,2},{4,7},{5,4},{6,5},{7,6},{8,11},{9,8},{10,9... | collective-permute-start | bytes 786440 | tf_op jit(solution)/shard_map/ppermute | solution.py:217
  32.8 11.3 %collective-permute-start.7 = (bf16[128,1024]{1,0:T(8,128)(2,1)S(1)}, bf16[128,1024]{1,0:T(8,128)(2,1)S(1)}, u32[]{:S(2)}, u32[]{:S(2)}) collective-permute-start(bf16[128,1024]{1,0:T(8,128)(2,1)S(1)} %get-tuple-element.93), channel_id=1, source_target_pairs={{0,1},{1,2},{2,3},{3,0},{4,5},{5,6},{6,7},{7,4},{8,9},{9,10},{10,1... | collective-permute-start | bytes 786440 | tf_op jit(solution)/shard_map/ppermute | solution.py:217
  39.5 4.7 %copy-start.19 = (bf16[128,1024]{1,0:T(8,128)(2,1)}, bf16[128,1024]{1,0:T(8,128)(2,1)S(1)}, u32[]{:S(2)}) copy-start(bf16[128,1024]{1,0:T(8,128)(2,1)S(1)} %collective-permute-done.9.refs_5_.refs_14_) | copy-start | bytes 786436
  39.5 36.7 %collective-permute-start.10 = (f32[1,128]{1,0:T(1,128)S(1)}, f32[1,128]{1,0:T(1,128)S(1)}, u32[]{:S(2)}, u32[]{:S(2)}) collective-permute-start(f32[1,128]{1,0:T(1,128)S(1)} %add.99), channel_id=1, source_target_pairs={{0,128},{32,160},{64,192},{96,224},{128,0},{160,32},{192,64},{224,... | collective-permute-start | bytes 1544 | tf_op jit(solution)/shard_map/ppermute | solution.py:207
  44.1 0.7 copy-start.20
  44.2 0.8 copy-start.21
  57.0 19.2 %collective-permute-start.11 = (bf16[256,512]{1,0:T(8,128)(2,1)}, bf16[256,512]{1,0:T(8,128)(2,1)S(1)}, u32[]{:S(2)}, u32[]{:S(2)}) collective-permute-start(bf16[256,512]{1,0:T(8,128)(2,1)} %get-tuple-element.62), channel_id=1, source_target_pairs={{0,3},{1,0},{2,1},{3,2},{4,7},{5,4},{6,5},{7,6},{8,11},{9,8},{10,9... | collective-permute-start | bytes 786440 | tf_op jit(solution)/shard_map/ppermute | solution.py:238
  59.7 16.5 %collective-permute-start.12 = (bf16[256,512]{1,0:T(8,128)(2,1)}, bf16[256,512]{1,0:T(8,128)(2,1)S(1)}, u32[]{:S(2)}, u32[]{:S(2)}) collective-permute-start(bf16[256,512]{1,0:T(8,128)(2,1)} %get-tuple-element.63), channel_id=1, source_target_pairs={{0,1},{1,2},{2,3},{3,0},{4,5},{5,6},{6,7},{7,4},{8,9},{9,10},{10,1... | collective-permute-start | bytes 786440 | tf_op jit(solution)/shard_map/ppermute | solution.py:238
  59.7 16.5 %collective-permute-start.13 = (bf16[256,512]{1,0:T(8,128)(2,1)}, bf16[256,512]{1,0:T(8,128)(2,1)S(1)}, u32[]{:S(2)}, u32[]{:S(2)}) collective-permute-start(bf16[256,512]{1,0:T(8,128)(2,1)} %get-tuple-element.64), channel_id=1, source_target_pairs={{0,2},{1,3},{2,0},{3,1},{4,6},{5,7},{6,4},{7,5},{8,10},{9,11},{10,... | collective-permute-start | bytes 786440 | tf_op jit(solution)/shard_map/ppermute | solution.py:238
  61.8 12.2 %copy-start.4 = (bf16[128,2048]{1,0:T(8,128)(2,1)S(1)}, bf16[128,2048]{1,0:T(8,128)(2,1)}, u32[]{:S(2)}) copy-start(bf16[128,2048]{1,0:T(8,128)(2,1)} %get-tuple-element.52) | copy-start | bytes 1572868
  74.0 2.3 %copy-start.24 = (bf16[256,512]{1,0:T(8,128)(2,1)S(1)}, bf16[256,512]{1,0:T(8,128)(2,1)}, u32[]{:S(2)}) copy-start(bf16[256,512]{1,0:T(8,128)(2,1)} %get-tuple-element.65) | copy-start | bytes 786436
  74.0 3.7 %copy-start.23 = (bf16[256,512]{1,0:T(8,128)(2,1)S(1)}, bf16[256,512]{1,0:T(8,128)(2,1)}, u32[]{:S(2)}) copy-start(bf16[256,512]{1,0:T(8,128)(2,1)} %get-tuple-element.69) | copy-start | bytes 786436
  74.0 4.4 %copy-start.22 = (bf16[256,512]{1,0:T(8,128)(2,1)S(1)}, bf16[256,512]{1,0:T(8,128)(2,1)}, u32[]{:S(2)}) copy-start(bf16[256,512]{1,0:T(8,128)(2,1)} %get-tuple-element.70) | copy-start | bytes 786436
  74.0 6.5 %copy-start.11 = (bf16[128,512]{1,0:T(8,128)(2,1)S(1)}, bf16[128,512]{1,0:T(8,128)(2,1)}, u32[]{:S(2)}) copy-start(bf16[128,512]{1,0:T(8,128)(2,1)} %get-tuple-element.72) | copy-start | bytes 393220
  74.1 6.5 %copy-start.12 = (bf16[128,512]{1,0:T(8,128)(2,1)S(1)}, bf16[128,512]{1,0:T(8,128)(2,1)}, u32[]{:S(2)}) copy-start(bf16[128,512]{1,0:T(8,128)(2,1)} %get-tuple-element.76) | copy-start | bytes 393220
  76.2 17.3 %copy-start.9 = (bf16[128,512]{1,0:T(8,128)(2,1)S(1)}, bf16[128,512]{1,0:T(8,128)(2,1)}, u32[]{:S(2)}) copy-start(bf16[128,512]{1,0:T(8,128)(2,1)} %get-tuple-element.67) | copy-start | bytes 393220
  76.2 17.3 %copy-start.10 = (bf16[128,512]{1,0:T(8,128)(2,1)S(1)}, bf16[128,512]{1,0:T(8,128)(2,1)}, u32[]{:S(2)}) copy-start(bf16[128,512]{1,0:T(8,128)(2,1)} %get-tuple-element.71) | copy-start | bytes 393220
  76.3 9.3 %collective-permute-start.14 = (bf16[256,512]{1,0:T(8,128)(2,1)S(1)}, bf16[256,512]{1,0:T(8,128)(2,1)S(1)}, u32[]{:S(2)}, u32[]{:S(2)}) collective-permute-start(bf16[256,512]{1,0:T(8,128)(2,1)S(1)} %copy-done.24), channel_id=1, source_target_pairs={{0,3},{1,0},{2,1},{3,2},{4,7},{5,4},{6,5},{7,6},{8,11},{9,8},{10,9... | collective-permute-start | bytes 786440 | tf_op jit(solution)/shard_map/ppermute | solution.py:238
  77.7 15.8 %collective-permute-start.15 = (bf16[256,512]{1,0:T(8,128)(2,1)S(1)}, bf16[256,512]{1,0:T(8,128)(2,1)S(1)}, u32[]{:S(2)}, u32[]{:S(2)}) collective-permute-start(bf16[256,512]{1,0:T(8,128)(2,1)S(1)} %copy-done.23), channel_id=1, source_target_pairs={{0,1},{1,2},{2,3},{3,0},{4,5},{5,6},{6,7},{7,4},{8,9},{9,10},{10,1... | collective-permute-start | bytes 786440 | tf_op jit(solution)/shard_map/ppermute | solution.py:238
  78.5 15.0 %collective-permute-start.16 = (bf16[256,512]{1,0:T(8,128)(2,1)S(1)}, bf16[256,512]{1,0:T(8,128)(2,1)S(1)}, u32[]{:S(2)}, u32[]{:S(2)}) collective-permute-start(bf16[256,512]{1,0:T(8,128)(2,1)S(1)} %copy-done.22), channel_id=1, source_target_pairs={{0,2},{1,3},{2,0},{3,1},{4,6},{5,7},{6,4},{7,5},{8,10},{9,11},{10,... | collective-permute-start | bytes 786440 | tf_op jit(solution)/shard_map/ppermute | solution.py:238
  80.6 18.8 %copy-start.8 = (bf16[128,512]{1,0:T(8,128)(2,1)S(1)}, bf16[128,512]{1,0:T(8,128)(2,1)}, u32[]{:S(2)}) copy-start(bf16[128,512]{1,0:T(8,128)(2,1)} %get-tuple-element.79) | copy-start | bytes 393220
  80.7 13.7 %collective-permute-start.18 = (bf16[128,512]{1,0:T(8,128)(2,1)S(1)}, bf16[128,512]{1,0:T(8,128)(2,1)S(1)}, u32[]{:S(2)}, u32[]{:S(2)}) collective-permute-start(bf16[128,512]{1,0:T(8,128)(2,1)S(1)} %get-tuple-element.87), channel_id=1, source_target_pairs={{8,0},{9,1},{10,2},{11,3},{12,4},{13,5},{14,6},{15,7},{16,8},{17,9... | collective-permute-start | bytes 393224 | tf_op jit(solution)/shard_map/ppermute | solution.py:262
  82.7 11.8 %collective-permute-start.17 = (bf16[128,512]{1,0:T(8,128)(2,1)S(1)}, bf16[128,512]{1,0:T(8,128)(2,1)S(1)}, u32[]{:S(2)}, u32[]{:S(2)}) collective-permute-start(bf16[128,512]{1,0:T(8,128)(2,1)S(1)} %get-tuple-element.88), channel_id=1, source_target_pairs={{4,0},{5,1},{6,2},{7,3},{8,4},{9,5},{10,6},{11,7},{12,8},{13,9},{1... | collective-permute-start | bytes 393224 | tf_op jit(solution)/shard_map/ppermute | solution.py:262
  86.2 13.3 %all-to-all-start = ((f32[8,1,256]{2,1,0:T(1,128)}), f32[8,1,256]{2,1,0:T(1,128)S(1)}, u32[]{:S(2)}, u32[]{:S(2)}) async-start(f32[8,1,256]{2,1,0:T(1,128)} %broadcast_in_dim.39), calls=%async_computation | async-start | bytes 16384 | tf_op jit(solution)/shard_map/all_to_all | solution.py:242
  93.5 15.6 %copy-start.7 = (bf16[128,512]{1,0:T(8,128)(2,1)S(1)}, bf16[128,512]{1,0:T(8,128)(2,1)}, u32[]{:S(2)}) copy-start(bf16[128,512]{1,0:T(8,128)(2,1)} %get-tuple-element.82) | copy-start | bytes 393220
  94.4 8.3 %collective-permute-start.19 = (bf16[128,512]{1,0:T(8,128)(2,1)}, bf16[128,512]{1,0:T(8,128)(2,1)}, u32[]{:S(2)}, u32[]{:S(2)}) collective-permute-start(bf16[128,512]{1,0:T(8,128)(2,1)} %get-tuple-element.77), channel_id=1, source_target_pairs={{4,0},{5,1},{6,2},{7,3},{8,4},{9,5},{10,6},{11,7},{12,8},{13,9},{1... | collective-permute-start | bytes 393224 | tf_op jit(solution)/shard_map/ppermute | solution.py:262
  96.9 12.2 %collective-permute-start.20 = (bf16[128,512]{1,0:T(8,128)(2,1)}, bf16[128,512]{1,0:T(8,128)(2,1)}, u32[]{:S(2)}, u32[]{:S(2)}) collective-permute-start(bf16[128,512]{1,0:T(8,128)(2,1)} %get-tuple-element.84), channel_id=1, source_target_pairs={{8,0},{9,1},{10,2},{11,3},{12,4},{13,5},{14,6},{15,7},{16,8},{17,9... | collective-permute-start | bytes 393224 | tf_op jit(solution)/shard_map/ppermute | solution.py:262
  99.4 17.1 %copy-start.3 = (f32[128,2048]{1,0:T(8,128)S(1)}, f32[128,2048]{1,0:T(8,128)}, u32[]{:S(2)}) copy-start(f32[128,2048]{1,0:T(8,128)} %get-tuple-element.56) | copy-start | bytes 3145732
  99.5 16.9 %copy-start.2 = (f32[128,2048]{1,0:T(8,128)S(1)}, f32[128,2048]{1,0:T(8,128)}, u32[]{:S(2)}) copy-start(f32[128,2048]{1,0:T(8,128)} %get-tuple-element.55) | copy-start | bytes 3145732
  103.4 11.1 %all-to-all-start.1 = ((f32[4,1,256]{2,1,0:T(1,128)}), f32[4,1,256]{2,1,0:T(1,128)S(1)}, u32[]{:S(2)}, u32[]{:S(2)}) async-start(f32[4,1,256]{2,1,0:T(1,128)} %broadcast_in_dim.41), calls=%async_computation.1 | async-start | bytes 8192 | tf_op jit(solution)/shard_map/all_to_all | solution.py:242

commit v5 on v4

--- a/solution.py
+++ b/solution.py
@@ -12,7 +12,7 @@
 GROUP = 8
 PAIRS = GROUP // 2
 RING = 4
-ORDER = (1, 3, 2)
+ORDER = (3, 1, 2)
 SLOTS = 3 + 2 * len(ORDER)
 PARTS = ((0, 2), (2, 2))
 MASKED = -1e30

time: 122 us -> 119 us (0.975)
    ppermute x3, waiting for transfers between devices: 7.45 us -> 6.19 us  [per_device(): near_got = [lax.ppermute(near, 'seq', around(step)) for step in ORDER]]
    ppermute x1, waiting for transfers between devices: 0.08 us -> 1.34 us  [per_device(): far = lax.ppermute(near, 'seq', down(RING))]
  transfers between devices with their start and end apart: 23 -> 23, of which waited for: 11 -> 11; matrix products, arithmetic and copies ran while one was open for 6% -> 6% of each run, Pallas kernels for 20% -> 21%
where the time goes in v5:
time: 119 us; the launch traced here: 118 us
  starting transfers between devices  49.8 us (42%)
  waiting for transfers between devices  27.3 us (23%)
  Pallas kernels  24.2 us (20%)
  other arithmetic  10.5 us (9%)
  between operations  3.56 us (3%)
  local copies, waits for them, and re-layouts  2.08 us (2%)
    pallas_call x2, Pallas kernels, attend(): pl.pallas_call(attend_kernel, grid=(heads,), out_shape=(pltpu.HBM((tok, h...  24.2 us
    all_to_all x2, starting transfers between devices, total_of(): lax.all_to_all(copies, 'seq', 0, 0, axis_index_groups=groups, tiled=True)  12 us
    ppermute x6, starting transfers between devices, per_device(): lax.ppermute(d, 'seq', around(-step))  8.95 us
    ppermute x3, waiting for transfers between devices, per_device(): lax.ppermute(jnp.where(x + step >= RING, far, own), 'seq', around(step))  6.5 us
    ppermute x3, starting transfers between devices, per_device(): near_got = [lax.ppermute(near, 'seq', around(step)) for step in ORDER]  6.26 us
    ppermute x3, waiting for transfers between devices, per_device(): near_got = [lax.ppermute(near, 'seq', around(step)) for step in ORDER]  6.19 us
    ppermute x3, starting transfers between devices, swap(): lax.ppermute(a, axis, [(i, i ^ bit) for i in range(lax.axis_size(axis))])  4.77 us
    ppermute x2, starting transfers between devices, per_device(): lax.ppermute(far_sum, 'seq', up(2 * RING))  4.39 us
  transfers between devices with their start and end apart: 23, of which 11 were waited for; matrix products, arithmetic and copies ran while one was open for 6% of the time, Pallas kernels for 21%

profile of v5, /device:TPU:128, one launch (start us, length us, event | category | flops | bytes accessed | tf_op | source)
XLA Modules:
  0.0 117.6 jit_solution(11150710022193437100)
XLA Ops:
  0.6 0.0 copy-start.13
  0.6 0.0 copy-start.14
  0.7 0.0 copy-start.1
  0.7 1.0 pad_maximum_fusion.refs_0_.refs_9_
  1.7 2.9 %collective-permute-start = (bf16[128,1024]{1,0:T(8,128)(2,1)S(1)}, bf16[128,1024]{1,0:T(8,128)(2,1)S(1)}, u32[]{:S(2)}, u32[]{:S(2)}) collective-permute-start(bf16[128,1024]{1,0:T(8,128)(2,1)S(1)} %pad_maximum_fusion.refs_0_.refs_9_), channel_id=1, source_target_pairs={{0,4},{1,5},{2,6},{3,7},{4,8},{5,9},{6,10},{7,11},{8,12},{9,13},{1... | collective-permute-start | bytes 786440 | tf_op jit(solution)/shard_map/ppermute | solution.py:210
  4.6 0.7 convert_element_type.107
  5.3 1.1 collective-permute-done.1
  6.4 0.7 convert_add_fusion
  7.1 1.6 %collective-permute-start.2 = (f32[1,128]{1,0:T(1,128)S(1)}, f32[1,128]{1,0:T(1,128)S(1)}, u32[]{:S(2)}, u32[]{:S(2)}) collective-permute-start(f32[1,128]{1,0:T(1,128)S(1)} %convert_add_fusion), channel_id=1, source_target_pairs={{0,64},{32,96},{64,0},{96,32},{128,192},{160,224},{192,128},{224,1... | collective-permute-start | bytes 1544 | tf_op jit(solution)/shard_map/ppermute | solution.py:207
  8.7 2.0 %collective-permute-done.2 = f32[1,128]{1,0:T(1,128)S(1)} collective-permute-done((f32[1,128]{1,0:T(1,128)S(1)}, f32[1,128]{1,0:T(1,128)S(1)}, u32[]{:S(2)}, u32[]{:S(2)}) %collective-permute-start.2) | collective-permute-done | bytes 544 | tf_op jit(solution)/shard_map/ppermute | solution.py:207
  10.6 2.2 %collective-permute-done.refs_1_.refs_10_ = bf16[128,1024]{1,0:T(8,128)(2,1)S(1)} collective-permute-done((bf16[128,1024]{1,0:T(8,128)(2,1)S(1)}, bf16[128,1024]{1,0:T(8,128)(2,1)S(1)}, u32[]{:S(2)}, u32[]{:S(2)}) %collective-permute-start) | collective-permute-done | bytes 262176 | tf_op jit(solution)/shard_map/ppermute | solution.py:210
  12.9 3.0 %collective-permute-start.6 = (bf16[128,1024]{1,0:T(8,128)(2,1)S(1)}, bf16[128,1024]{1,0:T(8,128)(2,1)S(1)}, u32[]{:S(2)}, u32[]{:S(2)}) collective-permute-start(bf16[128,1024]{1,0:T(8,128)(2,1)S(1)} %collective-permute-done.refs_1_.refs_10_), channel_id=1, source_target_pairs={{0,2},{1,3},{2,0},{3,1},{4,6},{5,7},{6,4},{7,5},{8,10},{9,11},{10,... | collective-permute-start | bytes 786440 | tf_op jit(solution)/shard_map/ppermute | solution.py:214
  15.9 0.6 collective-permute-start.5
  16.5 2.6 %collective-permute-start.4 = (bf16[128,1024]{1,0:T(8,128)(2,1)S(1)}, bf16[128,1024]{1,0:T(8,128)(2,1)S(1)}, u32[]{:S(2)}, u32[]{:S(2)}) collective-permute-start(bf16[128,1024]{1,0:T(8,128)(2,1)S(1)} %collective-permute-done.refs_1_.refs_10_), channel_id=1, source_target_pairs={{0,3},{1,0},{2,1},{3,2},{4,7},{5,4},{6,5},{7,6},{8,11},{9,8},{10,9... | collective-permute-start | bytes 786440 | tf_op jit(solution)/shard_map/ppermute | solution.py:214
  19.1 1.9 %collective-permute-start.3 = (bf16[128,1024]{1,0:T(8,128)(2,1)S(1)}, bf16[128,1024]{1,0:T(8,128)(2,1)S(1)}, u32[]{:S(2)}, u32[]{:S(2)}) collective-permute-start(bf16[128,1024]{1,0:T(8,128)(2,1)S(1)} %collective-permute-done.refs_1_.refs_10_), channel_id=1, source_target_pairs={{0,4},{1,5},{2,6},{3,7},{4,8},{5,9},{6,10},{7,11},{8,12},{9,13},{1... | collective-permute-start | bytes 786440 | tf_op jit(solution)/shard_map/ppermute | solution.py:213
  21.0 2.6 %collective-permute-done.6.refs_8_.refs_17_ = bf16[128,1024]{1,0:T(8,128)(2,1)S(1)} collective-permute-done((bf16[128,1024]{1,0:T(8,128)(2,1)S(1)}, bf16[128,1024]{1,0:T(8,128)(2,1)S(1)}, u32[]{:S(2)}, u32[]{:S(2)}) %collective-permute-start.6) | collective-permute-done | bytes 262176 | tf_op jit(solution)/shard_map/ppermute | solution.py:214
  23.6 3.5 %collective-permute-done.5.refs_7_.refs_16_ = bf16[128,1024]{1,0:T(8,128)(2,1)S(1)} collective-permute-done((bf16[128,1024]{1,0:T(8,128)(2,1)S(1)}, bf16[128,1024]{1,0:T(8,128)(2,1)S(1)}, u32[]{:S(2)}, u32[]{:S(2)}) %collective-permute-start.5) | collective-permute-done | bytes 262176 | tf_op jit(solution)/shard_map/ppermute | solution.py:214
  27.2 0.1 collective-permute-done.4.refs_6_.refs_15_
  27.2 1.3 %collective-permute-done.3.refs_2_.refs_11_ = bf16[128,1024]{1,0:T(8,128)(2,1)S(1)} collective-permute-done((bf16[128,1024]{1,0:T(8,128)(2,1)S(1)}, bf16[128,1024]{1,0:T(8,128)(2,1)S(1)}, u32[]{:S(2)}, u32[]{:S(2)}) %collective-permute-start.3) | collective-permute-done | bytes 262176 | tf_op jit(solution)/shard_map/ppermute | solution.py:213
  28.6 1.2 %broadcast_select_fusion = (bf16[128,1024]{1,0:T(8,128)(2,1)S(1)}, bf16[128,1024]{1,0:T(8,128)(2,1)S(1)}, bf16[128,1024]{1,0:T(8,128)(2,1)S(1)}) fusion(bf16[128,1024]{1,0:T(8,128)(2,1)S(1)} %collective-permute-done.3.refs_2_.refs_11_, pred[]{:T(512)S(6)} %ge.19, bf16[128,512]{1,0:T(8,128)(2,1)} %bitcast.35, bf16[128,512]{1,0:T(8,128)(2,1)} %bitcast.37, ...), kind=kLoop, calls=%fused_computation.36 | loop fusion | flops 917504 | bytes 1310723 | tf_op jit(solution)/shard_map/jit(_where)/select_n | solution.py:217
  29.8 1.0 collective-permute-start.9
  30.8 1.4 %collective-permute-start.8 = (bf16[128,1024]{1,0:T(8,128)(2,1)S(1)}, bf16[128,1024]{1,0:T(8,128)(2,1)S(1)}, u32[]{:S(2)}, u32[]{:S(2)}) collective-permute-start(bf16[128,1024]{1,0:T(8,128)(2,1)S(1)} %get-tuple-element.92), channel_id=1, source_target_pairs={{0,1},{1,2},{2,3},{3,0},{4,5},{5,6},{6,7},{7,4},{8,9},{9,10},{10,1... | collective-permute-start | bytes 786440 | tf_op jit(solution)/shard_map/ppermute | solution.py:217
  32.2 1.9 %collective-permute-start.7 = (bf16[128,1024]{1,0:T(8,128)(2,1)S(1)}, bf16[128,1024]{1,0:T(8,128)(2,1)S(1)}, u32[]{:S(2)}, u32[]{:S(2)}) collective-permute-start(bf16[128,1024]{1,0:T(8,128)(2,1)S(1)} %get-tuple-element.93), channel_id=1, source_target_pairs={{0,3},{1,0},{2,1},{3,2},{4,7},{5,4},{6,5},{7,6},{8,11},{9,8},{10,9... | collective-permute-start | bytes 786440 | tf_op jit(solution)/shard_map/ppermute | solution.py:217
  34.1 0.1 concatenate.64.block_of
  34.2 6.5 %collective-permute-done.9.refs_5_.refs_14_ = bf16[128,1024]{1,0:T(8,128)(2,1)S(1)} collective-permute-done((bf16[128,1024]{1,0:T(8,128)(2,1)S(1)}, bf16[128,1024]{1,0:T(8,128)(2,1)S(1)}, u32[]{:S(2)}, u32[]{:S(2)}) %collective-permute-start.9) | collective-permute-done | bytes 262176 | tf_op jit(solution)/shard_map/ppermute | solution.py:217
  40.6 3.2 %collective-permute-start.10 = (f32[1,128]{1,0:T(1,128)S(1)}, f32[1,128]{1,0:T(1,128)S(1)}, u32[]{:S(2)}, u32[]{:S(2)}) collective-permute-start(f32[1,128]{1,0:T(1,128)S(1)} %add.99), channel_id=1, source_target_pairs={{0,128},{32,160},{64,192},{96,224},{128,0},{160,32},{192,64},{224,... | collective-permute-start | bytes 1544 | tf_op jit(solution)/shard_map/ppermute | solution.py:207
  43.8 0.0 collective-permute-done.8.refs_4_.refs_13_
  43.8 0.0 collective-permute-done.7.refs_3_.refs_12_
  43.9 0.6 copy-done.20
  44.5 0.1 copy-done.21
  44.7 12.1 %shard_map.110 = (bf16[128,2048]{1,0:T(8,128)(2,1)}, f32[128,2048]{1,0:T(8,128)}, f32[1,128]{1,0:T(1,128)S(1)}, bf16[128,512]{1,0:T(8,128)(2,1)}, bf16[128,512]{...) custom-call(s32[9]{0:T(128)S(1)} %concatenate.64.block_of, ...), custom_call_target="tpu_custom_call" | custom-call | flops 7247757312 | bytes 8388608 | tf_op jit(solution)/shard_map/pallas_call | solution.py:154
  56.7 1.5 %collective-permute-start.11 = (bf16[256,512]{1,0:T(8,128)(2,1)}, bf16[256,512]{1,0:T(8,128)(2,1)S(1)}, u32[]{:S(2)}, u32[]{:S(2)}) collective-permute-start(bf16[256,512]{1,0:T(8,128)(2,1)} %get-tuple-element.62), channel_id=1, source_target_pairs={{0,1},{1,2},{2,3},{3,0},{4,5},{5,6},{6,7},{7,4},{8,9},{9,10},{10,1... | collective-permute-start | bytes 786440 | tf_op jit(solution)/shard_map/ppermute | solution.py:238
  58.3 1.8 %collective-permute-start.12 = (bf16[256,512]{1,0:T(8,128)(2,1)}, bf16[256,512]{1,0:T(8,128)(2,1)S(1)}, u32[]{:S(2)}, u32[]{:S(2)}) collective-permute-start(bf16[256,512]{1,0:T(8,128)(2,1)} %get-tuple-element.63), channel_id=1, source_target_pairs={{0,3},{1,0},{2,1},{3,2},{4,7},{5,4},{6,5},{7,6},{8,11},{9,8},{10,9... | collective-permute-start | bytes 786440 | tf_op jit(solution)/shard_map/ppermute | solution.py:238
  60.0 0.9 collective-permute-start.13
  60.9 12.2 %shard_map.111 = (bf16[128,2048]{1,0:T(8,128)(2,1)}, f32[128,2048]{1,0:T(8,128)}, f32[1,128]{1,0:T(1,128)S(1)}, bf16[128,512]{1,0:T(8,128)(2,1)}, bf16[128,512]{...) custom-call(s32[9]{0:T(128)S(1)} %concatenate.64.block_of, ...), custom_call_target="tpu_custom_call" | custom-call | flops 7247757312 | bytes 8388608 | tf_op jit(solution)/shard_map/pallas_call | solution.py:154
  73.2 0.0 copy-start.11
  73.2 2.2 %maximum_bitcast_fusion = bf16[1,128,4096]{2,1,0:T(8,128)(2,1)} fusion(bf16[128,2048]{1,0:T(8,128)(2,1)} %get-tuple-element.54, bf16[128,2048]{1,0:T(8,128)(2,1)S(1)} %copy-done.4), kind=kLoop, calls=%fused_computation.2 | loop fusion | flops 2097152 | bytes 2097152 | tf_op jit(solution)/shard_map/broadcast_in_dim | solution.py:278
  75.4 0.0 collective-permute-done.10
  75.4 0.0 collective-permute-done.13
  75.4 0.8 collective-permute-start.14
  76.2 2.6 %collective-permute-start.15 = (bf16[256,512]{1,0:T(8,128)(2,1)S(1)}, bf16[256,512]{1,0:T(8,128)(2,1)S(1)}, u32[]{:S(2)}, u32[]{:S(2)}) collective-permute-start(bf16[256,512]{1,0:T(8,128)(2,1)S(1)} %copy-done.23), channel_id=1, source_target_pairs={{0,3},{1,0},{2,1},{3,2},{4,7},{5,4},{6,5},{7,6},{8,11},{9,8},{10,9... | collective-permute-start | bytes 786440 | tf_op jit(solution)/shard_map/ppermute | solution.py:238
  78.7 1.4 %collective-permute-start.16 = (bf16[256,512]{1,0:T(8,128)(2,1)S(1)}, bf16[256,512]{1,0:T(8,128)(2,1)S(1)}, u32[]{:S(2)}, u32[]{:S(2)}) collective-permute-start(bf16[256,512]{1,0:T(8,128)(2,1)S(1)} %copy-done.22), channel_id=1, source_target_pairs={{0,2},{1,3},{2,0},{3,1},{4,6},{5,7},{6,4},{7,5},{8,10},{9,11},{10,... | collective-permute-start | bytes 786440 | tf_op jit(solution)/shard_map/ppermute | solution.py:238
  80.2 0.0 copy-start.8
  80.2 0.2 fusion.13
  80.4 1.9 %collective-permute-start.18 = (bf16[128,512]{1,0:T(8,128)(2,1)S(1)}, bf16[128,512]{1,0:T(8,128)(2,1)S(1)}, u32[]{:S(2)}, u32[]{:S(2)}) collective-permute-start(bf16[128,512]{1,0:T(8,128)(2,1)S(1)} %get-tuple-element.87), channel_id=1, source_target_pairs={{8,0},{9,1},{10,2},{11,3},{12,4},{13,5},{14,6},{15,7},{16,8},{17,9... | collective-permute-start | bytes 393224 | tf_op jit(solution)/shard_map/ppermute | solution.py:262
  82.3 1.9 %collective-permute-start.17 = (bf16[128,512]{1,0:T(8,128)(2,1)S(1)}, bf16[128,512]{1,0:T(8,128)(2,1)S(1)}, u32[]{:S(2)}, u32[]{:S(2)}) collective-permute-start(bf16[128,512]{1,0:T(8,128)(2,1)S(1)} %get-tuple-element.88), channel_id=1, source_target_pairs={{4,0},{5,1},{6,2},{7,3},{8,4},{9,5},{10,6},{11,7},{12,8},{13,9},{1... | collective-permute-start | bytes 393224 | tf_op jit(solution)/shard_map/ppermute | solution.py:262
  84.2 1.4 %collective-permute-done.14 = bf16[256,512]{1,0:T(8,128)(2,1)S(1)} collective-permute-done((bf16[256,512]{1,0:T(8,128)(2,1)S(1)}, bf16[256,512]{1,0:T(8,128)(2,1)S(1)}, u32[]{:S(2)}, u32[]{:S(2)}) %collective-permute-start.14) | collective-permute-done | bytes 262176 | tf_op jit(solution)/shard_map/ppermute | solution.py:238
  85.6 0.6 broadcast_in_dim.39
  86.2 7.2 %all-to-all-start = ((f32[8,1,256]{2,1,0:T(1,128)}), f32[8,1,256]{2,1,0:T(1,128)S(1)}, u32[]{:S(2)}, u32[]{:S(2)}) async-start(f32[8,1,256]{2,1,0:T(1,128)} %broadcast_in_dim.39), calls=%async_computation | async-start | bytes 16384 | tf_op jit(solution)/shard_map/all_to_all | solution.py:242
  93.4 0.0 collective-permute-done.15
  93.4 0.0 collective-permute-done.16
  93.4 0.9 fusion.4
  94.3 2.5 %collective-permute-start.19 = (bf16[128,512]{1,0:T(8,128)(2,1)}, bf16[128,512]{1,0:T(8,128)(2,1)}, u32[]{:S(2)}, u32[]{:S(2)}) collective-permute-start(bf16[128,512]{1,0:T(8,128)(2,1)} %get-tuple-element.77), channel_id=1, source_target_pairs={{4,0},{5,1},{6,2},{7,3},{8,4},{9,5},{10,6},{11,7},{12,8},{13,9},{1... | collective-permute-start | bytes 393224 | tf_op jit(solution)/shard_map/ppermute | solution.py:262
  96.8 2.5 %collective-permute-start.20 = (bf16[128,512]{1,0:T(8,128)(2,1)}, bf16[128,512]{1,0:T(8,128)(2,1)}, u32[]{:S(2)}, u32[]{:S(2)}) collective-permute-start(bf16[128,512]{1,0:T(8,128)(2,1)} %get-tuple-element.84), channel_id=1, source_target_pairs={{8,0},{9,1},{10,2},{11,3},{12,4},{13,5},{14,6},{15,7},{16,8},{17,9... | collective-permute-start | bytes 393224 | tf_op jit(solution)/shard_map/ppermute | solution.py:262
  99.3 0.1 fusion.18
  99.4 0.0 copy-start.2
  99.5 2.4 %collective-permute-done.19 = bf16[128,512]{1,0:T(8,128)(2,1)} collective-permute-done((bf16[128,512]{1,0:T(8,128)(2,1)}, bf16[128,512]{1,0:T(8,128)(2,1)}, u32[]{:S(2)}, u32[]{:S(2)}) %collective-permute-start.19) | collective-permute-done | bytes 131104 | tf_op jit(solution)/shard_map/ppermute | solution.py:262
  101.9 0.6 broadcast_in_dim.41
  102.5 4.8 %all-to-all-start.1 = ((f32[4,1,256]{2,1,0:T(1,128)}), f32[4,1,256]{2,1,0:T(1,128)S(1)}, u32[]{:S(2)}, u32[]{:S(2)}) async-start(f32[4,1,256]{2,1,0:T(1,128)} %broadcast_in_dim.41), calls=%async_computation.1 | async-start | bytes 8192 | tf_op jit(solution)/shard_map/all_to_all | solution.py:242
  107.2 1.1 fusion.9
  108.3 4.2 %all-to-all-done.1 = f32[4,1,256]{2,1,0:T(1,128)S(1)} async-done(((f32[4,1,256]{2,1,0:T(1,128)}), f32[4,1,256]{2,1,0:T(1,128)S(1)}, u32[]{:S(2)}, u32[]{:S(2)}) %all-to-all-start.1) | async-done | bytes 4128 | tf_op jit(solution)/shard_map/all_to_all | solution.py:242
  112.5 0.6 slice_reduce_fusion
  114.6 1.1 fusion
  115.7 0.7 pad_maximum_fusion.1
  (58 shorter events, 0.2 us)
Async XLA Ops:
  0.6 33.4 %copy-start.13 = (s32[3]{0:T(128)S(1)}, s32[3]{0:T(128)}, u32[]{:S(2)}) copy-start(s32[3]{0:T(128)} %constant.39) | copy-start | bytes 40
  0.6 33.4 %copy-start.14 = (s32[3]{0:T(128)S(1)}, s32[3]{0:T(128)}, u32[]{:S(2)}) copy-start(s32[3]{0:T(128)} %constant.32.clone) | copy-start | bytes 40
  0.7 44.0 %copy-start.1 = (s32[1,128]{1,0:T(1,128)S(1)}, s32[1,128]{1,0:T(1,128)}, u32[]{:S(2)}) copy-start(s32[1,128]{1,0:T(1,128)} %mask_ref.3) | copy-start | bytes 1540
  0.7 44.0 %copy-start = (s32[1,16]{1,0:T(1,128)S(1)}, s32[1,16]{1,0:T(1,128)}, u32[]{:S(2)}) copy-start(s32[1,16]{1,0:T(1,128)} %lengths.3) | copy-start | bytes 196
  1.7 42.2 %copy-start.5 = (bf16[128,1024]{1,0:T(8,128)(2,1)}, bf16[128,1024]{1,0:T(8,128)(2,1)S(1)}, u32[]{:S(2)}) copy-start(bf16[128,1024]{1,0:T(8,128)(2,1)S(1)} %pad_maximum_fusion.refs_0_.refs_9_) | copy-start | bytes 786436
  1.7 11.2 %collective-permute-start = (bf16[128,1024]{1,0:T(8,128)(2,1)S(1)}, bf16[128,1024]{1,0:T(8,128)(2,1)S(1)}, u32[]{:S(2)}, u32[]{:S(2)}) collective-permute-start(bf16[128,1024]{1,0:T(8,128)(2,1)S(1)} %pad_maximum_fusion.refs_0_.refs_9_), channel_id=1, source_target_pairs={{0,4},{1,5},{2,6},{3,7},{4,8},{5,9},{6,10},{7,11},{8,12},{9,13},{1... | collective-permute-start | bytes 786440 | tf_op jit(solution)/shard_map/ppermute | solution.py:210
  5.3 1.1 collective-permute-start.1
  7.1 3.5 %collective-permute-start.2 = (f32[1,128]{1,0:T(1,128)S(1)}, f32[1,128]{1,0:T(1,128)S(1)}, u32[]{:S(2)}, u32[]{:S(2)}) collective-permute-start(f32[1,128]{1,0:T(1,128)S(1)} %convert_add_fusion), channel_id=1, source_target_pairs={{0,64},{32,96},{64,0},{96,32},{128,192},{160,224},{192,128},{224,1... | collective-permute-start | bytes 1544 | tf_op jit(solution)/shard_map/ppermute | solution.py:207
  12.9 31.0 %copy-start.15 = (bf16[128,1024]{1,0:T(8,128)(2,1)}, bf16[128,1024]{1,0:T(8,128)(2,1)S(1)}, u32[]{:S(2)}) copy-start(bf16[128,1024]{1,0:T(8,128)(2,1)S(1)} %collective-permute-done.refs_1_.refs_10_) | copy-start | bytes 786436
  12.9 10.7 %collective-permute-start.6 = (bf16[128,1024]{1,0:T(8,128)(2,1)S(1)}, bf16[128,1024]{1,0:T(8,128)(2,1)S(1)}, u32[]{:S(2)}, u32[]{:S(2)}) collective-permute-start(bf16[128,1024]{1,0:T(8,128)(2,1)S(1)} %collective-permute-done.refs_1_.refs_10_), channel_id=1, source_target_pairs={{0,2},{1,3},{2,0},{3,1},{4,6},{5,7},{6,4},{7,5},{8,10},{9,11},{10,... | collective-permute-start | bytes 786440 | tf_op jit(solution)/shard_map/ppermute | solution.py:214
  15.9 11.3 %collective-permute-start.5 = (bf16[128,1024]{1,0:T(8,128)(2,1)S(1)}, bf16[128,1024]{1,0:T(8,128)(2,1)S(1)}, u32[]{:S(2)}, u32[]{:S(2)}) collective-permute-start(bf16[128,1024]{1,0:T(8,128)(2,1)S(1)} %collective-permute-done.refs_1_.refs_10_), channel_id=1, source_target_pairs={{0,1},{1,2},{2,3},{3,0},{4,5},{5,6},{6,7},{7,4},{8,9},{9,10},{10,1... | collective-permute-start | bytes 786440 | tf_op jit(solution)/shard_map/ppermute | solution.py:214
  16.5 10.8 %collective-permute-start.4 = (bf16[128,1024]{1,0:T(8,128)(2,1)S(1)}, bf16[128,1024]{1,0:T(8,128)(2,1)S(1)}, u32[]{:S(2)}, u32[]{:S(2)}) collective-permute-start(bf16[128,1024]{1,0:T(8,128)(2,1)S(1)} %collective-permute-done.refs_1_.refs_10_), channel_id=1, source_target_pairs={{0,3},{1,0},{2,1},{3,2},{4,7},{5,4},{6,5},{7,6},{8,11},{9,8},{10,9... | collective-permute-start | bytes 786440 | tf_op jit(solution)/shard_map/ppermute | solution.py:214
  19.1 9.5 %collective-permute-start.3 = (bf16[128,1024]{1,0:T(8,128)(2,1)S(1)}, bf16[128,1024]{1,0:T(8,128)(2,1)S(1)}, u32[]{:S(2)}, u32[]{:S(2)}) collective-permute-start(bf16[128,1024]{1,0:T(8,128)(2,1)S(1)} %collective-permute-done.refs_1_.refs_10_), channel_id=1, source_target_pairs={{0,4},{1,5},{2,6},{3,7},{4,8},{5,9},{6,10},{7,11},{8,12},{9,13},{1... | collective-permute-start | bytes 786440 | tf_op jit(solution)/shard_map/ppermute | solution.py:213
  23.6 20.3 %copy-start.16 = (bf16[128,1024]{1,0:T(8,128)(2,1)}, bf16[128,1024]{1,0:T(8,128)(2,1)S(1)}, u32[]{:S(2)}) copy-start(bf16[128,1024]{1,0:T(8,128)(2,1)S(1)} %collective-permute-done.6.refs_8_.refs_17_) | copy-start | bytes 786436
  27.1 16.8 %copy-start.17 = (bf16[128,1024]{1,0:T(8,128)(2,1)}, bf16[128,1024]{1,0:T(8,128)(2,1)S(1)}, u32[]{:S(2)}) copy-start(bf16[128,1024]{1,0:T(8,128)(2,1)S(1)} %collective-permute-done.5.refs_7_.refs_16_) | copy-start | bytes 786436
  27.2 16.7 %copy-start.18 = (bf16[128,1024]{1,0:T(8,128)(2,1)}, bf16[128,1024]{1,0:T(8,128)(2,1)S(1)}, u32[]{:S(2)}) copy-start(bf16[128,1024]{1,0:T(8,128)(2,1)S(1)} %collective-permute-done.4.refs_6_.refs_15_) | copy-start | bytes 786436
  28.6 15.3 %copy-start.6 = (bf16[128,1024]{1,0:T(8,128)(2,1)}, bf16[128,1024]{1,0:T(8,128)(2,1)S(1)}, u32[]{:S(2)}) copy-start(bf16[128,1024]{1,0:T(8,128)(2,1)S(1)} %collective-permute-done.3.refs_2_.refs_11_) | copy-start | bytes 786436
  29.8 10.8 %collective-permute-start.9 = (bf16[128,1024]{1,0:T(8,128)(2,1)S(1)}, bf16[128,1024]{1,0:T(8,128)(2,1)S(1)}, u32[]{:S(2)}, u32[]{:S(2)}) collective-permute-start(bf16[128,1024]{1,0:T(8,128)(2,1)S(1)} %get-tuple-element.91), channel_id=1, source_target_pairs={{0,2},{1,3},{2,0},{3,1},{4,6},{5,7},{6,4},{7,5},{8,10},{9,11},{10,... | collective-permute-start | bytes 786440 | tf_op jit(solution)/shard_map/ppermute | solution.py:217
  30.8 13.0 %collective-permute-start.8 = (bf16[128,1024]{1,0:T(8,128)(2,1)S(1)}, bf16[128,1024]{1,0:T(8,128)(2,1)S(1)}, u32[]{:S(2)}, u32[]{:S(2)}) collective-permute-start(bf16[128,1024]{1,0:T(8,128)(2,1)S(1)} %get-tuple-element.92), channel_id=1, source_target_pairs={{0,1},{1,2},{2,3},{3,0},{4,5},{5,6},{6,7},{7,4},{8,9},{9,10},{10,1... | collective-permute-start | bytes 786440 | tf_op jit(solution)/shard_map/ppermute | solution.py:217
  32.2 11.7 %collective-permute-start.7 = (bf16[128,1024]{1,0:T(8,128)(2,1)S(1)}, bf16[128,1024]{1,0:T(8,128)(2,1)S(1)}, u32[]{:S(2)}, u32[]{:S(2)}) collective-permute-start(bf16[128,1024]{1,0:T(8,128)(2,1)S(1)} %get-tuple-element.93), channel_id=1, source_target_pairs={{0,3},{1,0},{2,1},{3,2},{4,7},{5,4},{6,5},{7,6},{8,11},{9,8},{10,9... | collective-permute-start | bytes 786440 | tf_op jit(solution)/shard_map/ppermute | solution.py:217
  40.6 3.3 %copy-start.19 = (bf16[128,1024]{1,0:T(8,128)(2,1)}, bf16[128,1024]{1,0:T(8,128)(2,1)S(1)}, u32[]{:S(2)}) copy-start(bf16[128,1024]{1,0:T(8,128)(2,1)S(1)} %collective-permute-done.9.refs_5_.refs_14_) | copy-start | bytes 786436
  40.6 34.7 %collective-permute-start.10 = (f32[1,128]{1,0:T(1,128)S(1)}, f32[1,128]{1,0:T(1,128)S(1)}, u32[]{:S(2)}, u32[]{:S(2)}) collective-permute-start(f32[1,128]{1,0:T(1,128)S(1)} %add.99), channel_id=1, source_target_pairs={{0,128},{32,160},{64,192},{96,224},{128,0},{160,32},{192,64},{224,... | collective-permute-start | bytes 1544 | tf_op jit(solution)/shard_map/ppermute | solution.py:207
  43.8 0.7 copy-start.20
  43.9 0.8 copy-start.21
  56.7 18.6 %collective-permute-start.11 = (bf16[256,512]{1,0:T(8,128)(2,1)}, bf16[256,512]{1,0:T(8,128)(2,1)S(1)}, u32[]{:S(2)}, u32[]{:S(2)}) collective-permute-start(bf16[256,512]{1,0:T(8,128)(2,1)} %get-tuple-element.62), channel_id=1, source_target_pairs={{0,1},{1,2},{2,3},{3,0},{4,5},{5,6},{6,7},{7,4},{8,9},{9,10},{10,1... | collective-permute-start | bytes 786440 | tf_op jit(solution)/shard_map/ppermute | solution.py:238
  58.3 17.1 %collective-permute-start.12 = (bf16[256,512]{1,0:T(8,128)(2,1)}, bf16[256,512]{1,0:T(8,128)(2,1)S(1)}, u32[]{:S(2)}, u32[]{:S(2)}) collective-permute-start(bf16[256,512]{1,0:T(8,128)(2,1)} %get-tuple-element.63), channel_id=1, source_target_pairs={{0,3},{1,0},{2,1},{3,2},{4,7},{5,4},{6,5},{7,6},{8,11},{9,8},{10,9... | collective-permute-start | bytes 786440 | tf_op jit(solution)/shard_map/ppermute | solution.py:238
  60.0 15.3 %collective-permute-start.13 = (bf16[256,512]{1,0:T(8,128)(2,1)}, bf16[256,512]{1,0:T(8,128)(2,1)S(1)}, u32[]{:S(2)}, u32[]{:S(2)}) collective-permute-start(bf16[256,512]{1,0:T(8,128)(2,1)} %get-tuple-element.64), channel_id=1, source_target_pairs={{0,2},{1,3},{2,0},{3,1},{4,6},{5,7},{6,4},{7,5},{8,10},{9,11},{10,... | collective-permute-start | bytes 786440 | tf_op jit(solution)/shard_map/ppermute | solution.py:238
  60.9 12.2 %copy-start.4 = (bf16[128,2048]{1,0:T(8,128)(2,1)S(1)}, bf16[128,2048]{1,0:T(8,128)(2,1)}, u32[]{:S(2)}) copy-start(bf16[128,2048]{1,0:T(8,128)(2,1)} %get-tuple-element.52) | copy-start | bytes 1572868
  73.1 2.3 %copy-start.24 = (bf16[256,512]{1,0:T(8,128)(2,1)S(1)}, bf16[256,512]{1,0:T(8,128)(2,1)}, u32[]{:S(2)}) copy-start(bf16[256,512]{1,0:T(8,128)(2,1)} %get-tuple-element.65) | copy-start | bytes 786436
  73.1 3.0 %copy-start.23 = (bf16[256,512]{1,0:T(8,128)(2,1)S(1)}, bf16[256,512]{1,0:T(8,128)(2,1)}, u32[]{:S(2)}) copy-start(bf16[256,512]{1,0:T(8,128)(2,1)} %get-tuple-element.69) | copy-start | bytes 786436
  73.1 5.6 %copy-start.22 = (bf16[256,512]{1,0:T(8,128)(2,1)S(1)}, bf16[256,512]{1,0:T(8,128)(2,1)}, u32[]{:S(2)}) copy-start(bf16[256,512]{1,0:T(8,128)(2,1)} %get-tuple-element.70) | copy-start | bytes 786436
  73.2 7.0 %copy-start.11 = (bf16[128,512]{1,0:T(8,128)(2,1)S(1)}, bf16[128,512]{1,0:T(8,128)(2,1)}, u32[]{:S(2)}) copy-start(bf16[128,512]{1,0:T(8,128)(2,1)} %get-tuple-element.72) | copy-start | bytes 393220
  73.2 7.0 %copy-start.12 = (bf16[128,512]{1,0:T(8,128)(2,1)S(1)}, bf16[128,512]{1,0:T(8,128)(2,1)}, u32[]{:S(2)}) copy-start(bf16[128,512]{1,0:T(8,128)(2,1)} %get-tuple-element.76) | copy-start | bytes 393220
  75.4 18.0 %copy-start.9 = (bf16[128,512]{1,0:T(8,128)(2,1)S(1)}, bf16[128,512]{1,0:T(8,128)(2,1)}, u32[]{:S(2)}) copy-start(bf16[128,512]{1,0:T(8,128)(2,1)} %get-tuple-element.67) | copy-start | bytes 393220
  75.4 18.0 %copy-start.10 = (bf16[128,512]{1,0:T(8,128)(2,1)S(1)}, bf16[128,512]{1,0:T(8,128)(2,1)}, u32[]{:S(2)}) copy-start(bf16[128,512]{1,0:T(8,128)(2,1)} %get-tuple-element.71) | copy-start | bytes 393220
  75.4 10.2 %collective-permute-start.14 = (bf16[256,512]{1,0:T(8,128)(2,1)S(1)}, bf16[256,512]{1,0:T(8,128)(2,1)S(1)}, u32[]{:S(2)}, u32[]{:S(2)}) collective-permute-start(bf16[256,512]{1,0:T(8,128)(2,1)S(1)} %copy-done.24), channel_id=1, source_target_pairs={{0,1},{1,2},{2,3},{3,0},{4,5},{5,6},{6,7},{7,4},{8,9},{9,10},{10,1... | collective-permute-start | bytes 786440 | tf_op jit(solution)/shard_map/ppermute | solution.py:238
  76.2 17.2 %collective-permute-start.15 = (bf16[256,512]{1,0:T(8,128)(2,1)S(1)}, bf16[256,512]{1,0:T(8,128)(2,1)S(1)}, u32[]{:S(2)}, u32[]{:S(2)}) collective-permute-start(bf16[256,512]{1,0:T(8,128)(2,1)S(1)} %copy-done.23), channel_id=1, source_target_pairs={{0,3},{1,0},{2,1},{3,2},{4,7},{5,4},{6,5},{7,6},{8,11},{9,8},{10,9... | collective-permute-start | bytes 786440 | tf_op jit(solution)/shard_map/ppermute | solution.py:238
  78.7 14.7 %collective-permute-start.16 = (bf16[256,512]{1,0:T(8,128)(2,1)S(1)}, bf16[256,512]{1,0:T(8,128)(2,1)S(1)}, u32[]{:S(2)}, u32[]{:S(2)}) collective-permute-start(bf16[256,512]{1,0:T(8,128)(2,1)S(1)} %copy-done.22), channel_id=1, source_target_pairs={{0,2},{1,3},{2,0},{3,1},{4,6},{5,7},{6,4},{7,5},{8,10},{9,11},{10,... | collective-permute-start | bytes 786440 | tf_op jit(solution)/shard_map/ppermute | solution.py:238
  80.2 19.1 %copy-start.8 = (bf16[128,512]{1,0:T(8,128)(2,1)S(1)}, bf16[128,512]{1,0:T(8,128)(2,1)}, u32[]{:S(2)}) copy-start(bf16[128,512]{1,0:T(8,128)(2,1)} %get-tuple-element.79) | copy-start | bytes 393220
  80.4 13.9 %collective-permute-start.18 = (bf16[128,512]{1,0:T(8,128)(2,1)S(1)}, bf16[128,512]{1,0:T(8,128)(2,1)S(1)}, u32[]{:S(2)}, u32[]{:S(2)}) collective-permute-start(bf16[128,512]{1,0:T(8,128)(2,1)S(1)} %get-tuple-element.87), channel_id=1, source_target_pairs={{8,0},{9,1},{10,2},{11,3},{12,4},{13,5},{14,6},{15,7},{16,8},{17,9... | collective-permute-start | bytes 393224 | tf_op jit(solution)/shard_map/ppermute | solution.py:262
  82.3 12.0 %collective-permute-start.17 = (bf16[128,512]{1,0:T(8,128)(2,1)S(1)}, bf16[128,512]{1,0:T(8,128)(2,1)S(1)}, u32[]{:S(2)}, u32[]{:S(2)}) collective-permute-start(bf16[128,512]{1,0:T(8,128)(2,1)S(1)} %get-tuple-element.88), channel_id=1, source_target_pairs={{4,0},{5,1},{6,2},{7,3},{8,4},{9,5},{10,6},{11,7},{12,8},{13,9},{1... | collective-permute-start | bytes 393224 | tf_op jit(solution)/shard_map/ppermute | solution.py:262
  86.2 13.2 %all-to-all-start = ((f32[8,1,256]{2,1,0:T(1,128)}), f32[8,1,256]{2,1,0:T(1,128)S(1)}, u32[]{:S(2)}, u32[]{:S(2)}) async-start(f32[8,1,256]{2,1,0:T(1,128)} %broadcast_in_dim.39), calls=%async_computation | async-start | bytes 16384 | tf_op jit(solution)/shard_map/all_to_all | solution.py:242
  93.4 13.8 %copy-start.7 = (bf16[128,512]{1,0:T(8,128)(2,1)S(1)}, bf16[128,512]{1,0:T(8,128)(2,1)}, u32[]{:S(2)}) copy-start(bf16[128,512]{1,0:T(8,128)(2,1)} %get-tuple-element.82) | copy-start | bytes 393220
  94.3 7.6 %collective-permute-start.19 = (bf16[128,512]{1,0:T(8,128)(2,1)}, bf16[128,512]{1,0:T(8,128)(2,1)}, u32[]{:S(2)}, u32[]{:S(2)}) collective-permute-start(bf16[128,512]{1,0:T(8,128)(2,1)} %get-tuple-element.77), channel_id=1, source_target_pairs={{4,0},{5,1},{6,2},{7,3},{8,4},{9,5},{10,6},{11,7},{12,8},{13,9},{1... | collective-permute-start | bytes 393224 | tf_op jit(solution)/shard_map/ppermute | solution.py:262
  96.8 10.5 %collective-permute-start.20 = (bf16[128,512]{1,0:T(8,128)(2,1)}, bf16[128,512]{1,0:T(8,128)(2,1)}, u32[]{:S(2)}, u32[]{:S(2)}) collective-permute-start(bf16[128,512]{1,0:T(8,128)(2,1)} %get-tuple-element.84), channel_id=1, source_target_pairs={{8,0},{9,1},{10,2},{11,3},{12,4},{13,5},{14,6},{15,7},{16,8},{17,9... | collective-permute-start | bytes 393224 | tf_op jit(solution)/shard_map/ppermute | solution.py:262
  99.3 15.3 %copy-start.3 = (f32[128,2048]{1,0:T(8,128)S(1)}, f32[128,2048]{1,0:T(8,128)}, u32[]{:S(2)}) copy-start(f32[128,2048]{1,0:T(8,128)} %get-tuple-element.56) | copy-start | bytes 3145732
  99.4 15.2 %copy-start.2 = (f32[128,2048]{1,0:T(8,128)S(1)}, f32[128,2048]{1,0:T(8,128)}, u32[]{:S(2)}) copy-start(f32[128,2048]{1,0:T(8,128)} %get-tuple-element.55) | copy-start | bytes 3145732
  102.5 10.0 %all-to-all-start.1 = ((f32[4,1,256]{2,1,0:T(1,128)}), f32[4,1,256]{2,1,0:T(1,128)S(1)}, u32[]{:S(2)}, u32[]{:S(2)}) async-start(f32[4,1,256]{2,1,0:T(1,128)} %broadcast_in_dim.41), calls=%async_computation.1 | async-start | bytes 8192 | tf_op jit(solution)/shard_map/all_to_all | solution.py:242
